TPU v7x, 256 devices: a whole 4x4x8 slice. The times are simulated.
256 devices in a mesh: dp: 2 (over core), expert: 8 (over z_hi, x), tensor: 16 (over y, z_lo).
Axes of the slice: x: 4, y: 4, z: 8 (z_hi: 2, z_lo: 4; z = z_hi * 4 + z_lo), core: 2. Of those that a mesh axis runs over, the one named last changes fastest.
Arguments:
- cotangent: bfloat16 [2, 8192, 3072], P('dp', ('expert', 'tensor')), may hold values from -6 to 6
- scales: float32 [2, 8192], P('dp', ('expert', 'tensor')), may hold values from 0.1 to 1
- routes: int32 [2, 8192, 1], P('dp', ('expert', 'tensor')), may hold values from 0 to 7; in each aligned block of 64 rows (0 to 63, 64 to 127, ..., all dimensions but the last counted through in order) at most 16 rows name the same one
- gate: bfloat16 [2, 8, 2048, 8192], P('dp', 'expert', None, 'tensor'), may hold values from -6 to 6
- up: bfloat16 [2, 8, 2048, 8192], P('dp', 'expert', None, 'tensor'), may hold values from -6 to 6
- weight: bfloat16 [8, 8192, 3072], P('expert', 'tensor'), may hold values from -0.0625 to 0.0625
Outputs:
- grad_gate: bfloat16 [2, 8, 2048, 8192], P('dp', 'expert', None, 'tensor')
- grad_up: bfloat16 [2, 8, 2048, 8192], P('dp', 'expert', None, 'tensor')
- weight_grad: bfloat16 [8, 8192, 3072], P('expert', 'tensor', 'dp')
Inputs may be any that keep to these rules, and one draw needn't show every extreme that they name: `routes`: in each source device's block of 64 rows at most 16 rows name one expert, and in every draw some block has exactly 16 rows for one expert.
All inputs are finite; a program needn't handle non-finite values.
Results may differ from a plain program's by a relative error of at most 0.0057.
Values may be sent and summed in bfloat16 or wider, within the bound.
No kernel may reach another device: no remote copies, remote signals or barrier semaphores. Data moves between devices by JAX's collectives and lax.ppermute only.
A program may use at most 128 MiB of HBM per device.

v0:
```python
import jax
import jax.numpy as jnp
from jax import lax
from jax.sharding import PartitionSpec as P


def local_grads(rows, pre_gate, up_value, weight_local):
    grad_hidden = lax.dot_general(
        rows, weight_local, (((1,), (1,)), ((), ())), preferred_element_type=jnp.float32
    )
    gate_f = pre_gate.astype(jnp.float32)
    up_f = up_value.astype(jnp.float32)
    sig = jax.nn.sigmoid(gate_f)
    silu = gate_f * sig
    grad_g = (grad_hidden * up_f * sig * (1.0 + gate_f * (1.0 - sig))).astype(jnp.bfloat16)
    grad_u = (grad_hidden * silu).astype(jnp.bfloat16)
    hidden = (silu * up_f).astype(jnp.bfloat16)
    partial_w = lax.dot_general(
        hidden, rows, (((0,), (0,)), ((), ())), preferred_element_type=jnp.float32
    )
    return (grad_g, grad_u, partial_w)


def per_device(cotangent, scales, routes, gate, up, weight):
    n_dp = lax.axis_size("dp")
    n_exp = lax.axis_size("expert")
    n_tensor = lax.axis_size("tensor")
    tok = cotangent.shape[1]
    width = cotangent.shape[2]
    capacity = gate.shape[2]
    slot_count = capacity // (n_tensor * n_exp)
    expert_ids = routes[0, :, 0]
    onehot = (expert_ids[:, None] == jnp.arange(n_exp, dtype=jnp.int32)[None, :]).astype(jnp.int32)
    before = jnp.cumsum(onehot, axis=0) - onehot
    slot_in = jnp.sum(before * onehot, axis=1)
    target = expert_ids * slot_count + slot_in
    scaled = (cotangent[0].astype(jnp.float32) * scales[0][:, None]).astype(jnp.bfloat16)
    send_buf = jnp.zeros((n_exp * slot_count, width), jnp.bfloat16).at[target].set(scaled)
    send_buf = send_buf.reshape(n_exp, slot_count, width)
    received = lax.all_to_all(send_buf, "expert", split_axis=0, concat_axis=0, tiled=True)
    received = received.reshape(n_exp * slot_count, width)
    gate_local = gate[0, 0]
    up_local = up[0, 0]
    weight_local = weight[0]
    rows = lax.all_gather(received, "tensor", axis=0, tiled=True)
    grad_g, grad_u, partial_w = local_grads(rows, gate_local, up_local, weight_local)
    factor = 1.0 / jnp.sqrt(jnp.float32(n_dp * tok * n_exp * n_tensor))
    share = width // n_dp
    summed = lax.psum(partial_w, "dp")
    mine = lax.dynamic_slice_in_dim(summed, lax.axis_index("dp") * share, share, 1)
    weight_grad = (mine * factor).astype(jnp.bfloat16)
    return (grad_g[None, None], grad_u[None, None], weight_grad[None])


def solution(mesh):
    in_specs = (
        P("dp", ("expert", "tensor"), None),
        P("dp", ("expert", "tensor")),
        P("dp", ("expert", "tensor"), None),
        P("dp", "expert", None, "tensor"),
        P("dp", "expert", None, "tensor"),
        P("expert", "tensor", None),
    )
    out_specs = (
        P("dp", "expert", None, "tensor"),
        P("dp", "expert", None, "tensor"),
        P("expert", "tensor", "dp"),
    )
    return jax.shard_map(
        per_device, mesh=mesh, in_specs=in_specs, out_specs=out_specs, check_vma=False
    )
```

profile of v0, /device:TPU:1, one launch (start us, length us, event | category | flops | bytes accessed | tf_op | source)
XLA Modules:
  0.0 381.7 jit_solution(5113404071279116516)
XLA Ops:
  7.2 0.0 copy-start
  7.2 0.0 all-gather.2.cloned.1.call-start
  7.2 0.9 fusion.22
  8.1 0.1 reduce_window_sum.11
  8.2 0.8 select_reduce_fusion
  9.0 0.7 fusion.23
  9.7 2.6 scatter_custom_fusion
  12.3 28.1 %all_to_all.5 = bf16[8,16,3072]{2,1,0:T(8,128)(2,1)} all-to-all(bf16[8,16,3072]{2,1,0:T(8,128)(2,1)} %bitcast.52), channel_id=1, replica_groups=mesh['dp'=2,'expert'=8,'tensor'=16] {'expert'}, dimensions={0} | all-to-all | bytes 1572864 | tf_op jit(solution)/shard_map/all_to_all | solution.py:40
  40.4 0.0 all-gather.2.cloned.1.call-update
  40.4 0.0 all-reduce.2.cloned.1.call-start
  40.5 275.7 %all-gather.2.cloned.1.call-done = bf16[2048,3072]{1,0:T(8,128)(2,1)} async-done(((bf16[128,3072]{1,0:T(8,128)(2,1)}), bf16[2048,3072]{1,0:T(8,128)(2,1)}) %all-gather.2.cloned.1.call-update) | async-done | bytes 12582928 | tf_op jit(solution)/shard_map/all_gather | solution.py:45
  316.2 12.8 %fusion.11 = f32[512,3072]{1,0:T(8,128)} fusion(bf16[2048,3072]{1,0:T(8,128)(2,1)} %all-gather.2.cloned.1.call-done, bf16[1,1,2048,512]{3,2,1,0:T(8,128)(2,1)} %param.10, bf16[1,1,2048,512]{3,2,1,0:T(8,128)(2,1)} %param.9), kind=kOutput, calls=%fused_computation.19 | convolution fusion | flops 6450839552 | bytes 23068672 | tf_op jit(solution)/shard_map/dot_general | solution.py:18
  329.0 0.0 all-reduce.2.cloned.1.call-update
  329.0 0.0 copy-done
  329.0 15.3 %fusion.10 = (bf16[1,1,2048,512]{3,2,1,0:T(8,128)(2,1)}, bf16[1,1,2048,512]{3,2,1,0:T(8,128)(2,1)}) fusion(bf16[1,1,2048,512]{3,2,1,0:T(8,128)(2,1)} %param.9, bf16[1,1,2048,512]{3,2,1,0:T(8,128)(2,1)} %param.10, bf16[2048,3072]{1,0:T(8,128)(2,1)} %all-gather.2.cloned.1.call-done, bf16[1,512,3072]{2,1,0:T(8,128)(2,1)S(1)} %copy-done), kind=kOutput, calls=%fused_computation.18 | convolution fusion | flops 6458179584 | bytes 24117248 | tf_op jit(solution)/shard_map/dot_general | solution.py:8
  344.3 27.2 %all-reduce.2.cloned.1.call-done = f32[512,3072]{1,0:T(8,128)} async-done(((f32[512,3072]{1,0:T(8,128)}), f32[512,3072]{1,0:T(8,128)}) %all-reduce.2.cloned.1.call-update) | async-done | bytes 6291472 | tf_op jit(solution)/shard_map/psum | solution.py:49
  371.5 3.4 fusion.15
Async XLA Ops:
  7.2 321.9 %copy-start = (bf16[1,512,3072]{2,1,0:T(8,128)(2,1)S(1)}, bf16[1,512,3072]{2,1,0:T(8,128)(2,1)}, u32[]{:S(2)}) copy-start(bf16[1,512,3072]{2,1,0:T(8,128)(2,1)} %param.11) | copy-start | bytes 9437188
  7.2 309.0 %all-gather.2.cloned.1.call-start = ((), (), s32[]{:S(2)}) async-start(), calls=%async_computation.1 | async-start | bytes 13369344 | tf_op jit(solution)/shard_map/all_gather | solution.py:45
  40.4 331.1 %all-reduce.2.cloned.1.call-start = ((), (), s32[]{:S(2)}) async-start(), calls=%async_computation.2 | async-start | bytes 12582912 | tf_op jit(solution)/shard_map/psum | solution.py:49
Sparse Core Ops, SparseCore 0:
  40.5 275.6 all-gather.1
  329.2 42.3 all-reduce.1
where the time goes:
time: 382 us
  waiting for transfers between devices  303 us (79%)
  blocking collectives  28.1 us (7%)
  matrix products  28.1 us (7%)
  between operations  14.1 us (4%)
  other arithmetic  8.47 us (2%)
    all_gather x1, waiting for transfers between devices, per_device(): rows = lax.all_gather(received, 'tensor', axis=0, tiled=True)  276 us
    all_to_all x1, blocking collectives, per_device(): lax.all_to_all(send_buf, 'expert', split_axis=0, concat_axis=0, tiled=True)  28.1 us
    psum x1, waiting for transfers between devices, per_device(): summed = lax.psum(partial_w, 'dp')  27.2 us
    dot_general x1, matrix products, local_grads(): lax.dot_general(rows, weight_local, (((1,), (1,)), ((), ())), preferred_e...  15.3 us
    dot_general x1, matrix products, local_grads(): lax.dot_general(hidden, rows, (((0,), (0,)), ((), ())), preferred_element...  12.8 us
  transfers between devices with their start and end apart: 2, of which 2 were waited for; matrix products, arithmetic and copies ran while one was open for 4% of the time, Pallas kernels for 0%

commit v1 on v0

v1 whole, which is shorter than its diff:
```python
import functools

import jax
import jax.numpy as jnp
from jax import lax
from jax.experimental import pallas as pl
from jax.experimental.pallas import tpu as pltpu
from jax.sharding import PartitionSpec as P

AX = ("dp", "expert", "tensor")
NX, NY, NZ = 4, 4, 4
SLOT = 16
HALF = NX * SLOT
ANY = pl.ANY
VMEM_LIMIT = 48 * 1024 * 1024


def chip_perm(fn):
    pairs = []
    for c in range(2):
        for z in range(2 * NZ):
            for x in range(NX):
                for y in range(NY):
                    to = fn(c, x, y, z)
                    if to is not None:
                        pairs.append((flat(c, x, y, z), flat(*to)))
    return pairs


def flat(c, x, y, z):
    x, y, z = x % NX, y % NY, z % (2 * NZ)
    return (c * 2 * NX + (z // NZ) * NX + x) * NY * NZ + y * NZ + z % NZ


X_STEP = [chip_perm(lambda c, x, y, z, k=k: (c, x + k, y, z)) for k in range(NX)]
Y_STEP = chip_perm(lambda c, x, y, z: (c, x, y + 1 - 2 * c, z))
Z_MIRROR = chip_perm(lambda c, x, y, z: (c, x, y, 2 * NZ - 1 - z))
Z_PAIR = chip_perm(lambda c, x, y, z: (c, x, y, z ^ 1))
Z_MIDDLE = chip_perm(lambda c, x, y, z: (c, x, y, z ^ 3) if z % NZ in (1, 2) else None)
Z_OUT = chip_perm(lambda c, x, y, z: (c, x, y, z ^ 1) if z % NZ in (1, 2) else None)
DP_SWAP = chip_perm(lambda c, x, y, z: (1 - c, x, y, z))


def send(a, pairs):
    return lax.ppermute(a, AX, pairs)


def dispatch_kernel(place, cot, scales, ids_col, ids_row, u0, u1, u2, u3, v):
    tok = cot.shape[0]
    x, zhi = place[0], place[1]
    col, row = ids_col[...], ids_row[...]
    shape = (tok, tok)
    earlier = lax.broadcasted_iota(jnp.int32, shape, 0) < lax.broadcasted_iota(jnp.int32, shape, 1)
    same = jnp.where((col == row) & earlier, 1.0, 0.0)
    slot = jnp.sum(same, axis=0, keepdims=True).astype(jnp.int32)
    other = jnp.where((row >> 2) == zhi, 0, HALF)
    target = other + ((row - x) & (NX - 1)) * SLOT + slot
    pick = lax.broadcasted_iota(jnp.int32, (2 * HALF, tok), 0) == target
    pick = jnp.where(pick, 1.0, 0.0).astype(jnp.bfloat16)
    scaled = (cot[...].astype(jnp.float32) * scales[...]).astype(jnp.bfloat16)
    out = jnp.dot(pick, scaled, preferred_element_type=jnp.float32).astype(jnp.bfloat16)
    for k, ref in enumerate((u0, u1, u2, u3)):
        ref[...] = out[k * SLOT:(k + 1) * SLOT]
    v[...] = out[HALF:]


def dispatch(place, cot, scales, ids):
    tok, width = cot.shape
    block = jax.ShapeDtypeStruct((SLOT, width), jnp.bfloat16)
    vmem = pl.BlockSpec(memory_space=pltpu.VMEM)
    return pl.pallas_call(
        dispatch_kernel,
        out_shape=(block,) * NX + (jax.ShapeDtypeStruct((HALF, width), jnp.bfloat16),),
        in_specs=[pl.BlockSpec(memory_space=pltpu.SMEM)] + [vmem] * 4,
        out_specs=(vmem,) * (NX + 1),
        name="dispatch",
    )(place, cot, scales.reshape(tok, 1), ids.reshape(tok, 1), ids.reshape(1, tok))


def assemble_kernel(place, b0, b1, b2, b3, out):
    x = place[0]
    for k, ref in enumerate((b0, b1, b2, b3)):
        at = pl.multiple_of(((x - k) & (NX - 1)) * SLOT, SLOT)
        out[pl.ds(at, SLOT), :] = ref[...]


def assemble(place, blocks):
    vmem = pl.BlockSpec(memory_space=pltpu.VMEM)
    return pl.pallas_call(
        assemble_kernel,
        out_shape=jax.ShapeDtypeStruct((HALF, blocks[0].shape[1]), jnp.bfloat16),
        in_specs=[pl.BlockSpec(memory_space=pltpu.SMEM)] + [vmem] * NX,
        out_specs=vmem,
        name="assemble",
    )(place, *blocks)


def hidden_grad_kernel(counts, fresh, *refs):
    n = len(counts)
    offs, rows, (wt, gate, up) = refs[0], refs[1:1 + n], refs[1 + n:4 + n]
    rest = refs[4 + n:] if fresh else refs[6 + n:]
    gg, gu, rows_s, wt_s, gate_s, up_s, gg_s, gu_s, sems, row_sems, blk_sems, out_sems = rest
    total = sum(counts)
    blocks = total // HALF
    w_copy = pltpu.make_async_copy(wt, wt_s, sems.at[0])
    w_copy.start()
    row_copies, at = [], 0
    for i, m in enumerate(counts):
        row_copies.append(pltpu.make_async_copy(rows[i], rows_s.at[pl.ds(at, m)], row_sems.at[i]))
        row_copies[-1].start()
        at += m
    blk_copies, out_copies = [], []
    for b in range(blocks):
        here = pl.ds(b * HALF, HALF)
        there = pl.ds(pl.multiple_of(offs[b], HALF), HALF)
        for k, (src, dst) in enumerate(((gate, gate_s), (up, up_s))):
            blk_copies.append(pltpu.make_async_copy(src.at[there], dst.at[here], blk_sems.at[k, b]))
            blk_copies[-1].start()
        for k, (src, dst) in enumerate(((gg_s, gg), (gu_s, gu))):
            out_copies.append(pltpu.make_async_copy(src.at[here], dst.at[there], out_sems.at[k, b]))
    w_copy.wait()
    for c in row_copies + blk_copies:
        c.wait()
    step = 256 if total % 256 == 0 else 128
    for t in range(total // step):
        here = pl.ds(t * step, step)
        grad = jnp.dot(rows_s[here, :], wt_s[...], preferred_element_type=jnp.float32)
        g = gate_s[here, :].astype(jnp.float32)
        u = up_s[here, :].astype(jnp.float32)
        sig = jax.nn.sigmoid(g)
        gg_s[here, :] = (grad * u * sig * (1.0 + g * (1.0 - sig))).astype(jnp.bfloat16)
        gu_s[here, :] = (grad * (g * sig)).astype(jnp.bfloat16)
        per = step // HALF
        for c in out_copies[2 * per * t:2 * per * (t + 1)]:
            c.start()
    for c in out_copies:
        c.wait()


def hidden_grads(rows, offs, wt, gate, up, outs):
    counts = tuple(r.shape[0] for r in rows)
    total, blocks = sum(counts), sum(counts) // HALF
    width, units = wt.shape
    fresh = outs is None
    n = len(rows)
    out = jax.ShapeDtypeStruct(gate.shape, jnp.bfloat16)
    args = (offs, *rows, wt, gate, up) + (() if fresh else tuple(outs))
    tile = pltpu.VMEM((total, units), jnp.bfloat16)
    return pl.pallas_call(
        functools.partial(hidden_grad_kernel, counts, fresh),
        out_shape=(out, out),
        in_specs=[pl.BlockSpec(memory_space=pltpu.SMEM)] + [pl.BlockSpec(memory_space=ANY)] * (len(args) - 1),
        out_specs=(pl.BlockSpec(memory_space=ANY),) * 2,
        scratch_shapes=[
            pltpu.VMEM((total, width), jnp.bfloat16),
            pltpu.VMEM((width, units), jnp.bfloat16),
            tile, tile, tile, tile,
            pltpu.SemaphoreType.DMA((1,)),
            pltpu.SemaphoreType.DMA((n,)),
            pltpu.SemaphoreType.DMA((2, blocks)),
            pltpu.SemaphoreType.DMA((2, blocks)),
        ],
        input_output_aliases={} if fresh else {n + 4: 0, n + 5: 1},
        compiler_params=pltpu.CompilerParams(vmem_limit_bytes=VMEM_LIMIT),
        cost_estimate=pl.CostEstimate(
            flops=2 * total * width * units,
            bytes_accessed=2 * (total * width + width * units + 4 * total * units),
            transcendentals=total * units,
        ),
        name="hidden_grads",
    )(*args)


def weight_grad_kernel(counts, fresh, *refs):
    n = len(counts)
    half, offs, rows, hid = refs[0], refs[1], refs[2:2 + n], refs[2 + n]
    rest = refs[3 + n:]
    acc = None if fresh else rest[0]
    out, hid_s, hid_t, rows_s, sems = rest[0 if fresh else 1:]
    blocks = sum(counts) // HALF

    @pl.when(pl.program_id(0) == 0)
    def _():
        copies = []
        for b in range(blocks):
            there = pl.ds(pl.multiple_of(offs[b], HALF), HALF)
            copies.append(pltpu.make_async_copy(hid.at[there], hid_s.at[pl.ds(b * HALF, HALF)], sems.at[b]))
            copies[-1].start()
        for c in copies:
            c.wait()
        hid_t[...] = hid_s[...].T

    at = 0
    for i, m in enumerate(counts):
        rows_s[pl.ds(at, m), :] = rows[i][...]
        at += m
    part = jnp.dot(hid_t[...], rows_s[...], preferred_element_type=jnp.float32)
    out[...] = part if fresh else acc[...] + part


def weight_grad_part(rows, half, offs, hid, acc):
    counts = tuple(r.shape[0] for r in rows)
    total, width, units = sum(counts), rows[0].shape[1], hid.shape[1]
    cols = 512
    steps = width // 2 // cols
    fresh = acc is None
    n = len(rows)
    acc_spec = pl.BlockSpec((units, cols), lambda j, h, o: (0, j))
    grid_spec = pltpu.PrefetchScalarGridSpec(
        num_scalar_prefetch=2,
        grid=(steps,),
        in_specs=[pl.BlockSpec((m, cols), lambda j, h, o: (0, h[0] * steps + j)) for m in counts]
        + [pl.BlockSpec(memory_space=ANY)] + ([] if fresh else [acc_spec]),
        out_specs=acc_spec,
        scratch_shapes=[
            pltpu.VMEM((total, units), jnp.bfloat16),
            pltpu.VMEM((units, total), jnp.bfloat16),
            pltpu.VMEM((total, cols), jnp.bfloat16),
            pltpu.SemaphoreType.DMA((total // HALF,)),
        ],
    )
    args = (half, offs, *rows, hid) + (() if fresh else (acc,))
    return pl.pallas_call(
        functools.partial(weight_grad_kernel, counts, fresh),
        out_shape=jax.ShapeDtypeStruct((units, width // 2), jnp.float32),
        grid_spec=grid_spec,
        input_output_aliases={} if fresh else {n + 3: 0},
        compiler_params=pltpu.CompilerParams(vmem_limit_bytes=VMEM_LIMIT),
        cost_estimate=pl.CostEstimate(
            flops=total * width * units,
            bytes_accessed=total * width + 2 * total * units + 4 * units * width,
            transcendentals=0,
        ),
        name="weight_grad_part",
    )(*args)


def gather_z(own, inner):
    near = send(own, Z_PAIR)
    mid1 = send(own, Z_MIDDLE)
    mid2 = send(near, Z_MIDDLE)
    out1 = send(mid1, Z_OUT)
    out2 = send(mid2, Z_OUT)
    far = jnp.concatenate([jnp.where(inner, mid1, out1), jnp.where(inner, mid2, out2)], axis=0)
    return near, far


def ring_y(own):
    parts = [own]
    for _ in range(NY - 1):
        parts.append(send(parts[-1], Y_STEP))
    return parts


def per_device(cotangent, scales, routes, gate, up, weight):
    dp = lax.axis_index("dp")
    expert = lax.axis_index("expert")
    tensor = lax.axis_index("tensor")
    x, zhi = expert % NX, expert // NX
    y, z = tensor // NZ, tensor % NZ
    gate, up, weight = gate[0, 0], up[0, 0], weight[0]
    inner = (z == 1) | (z == 2)

    place = jnp.stack([x, zhi]).astype(jnp.int32)
    *u_blocks, v_send = dispatch(place, cotangent[0], scales[0], routes[0, :, 0])
    v_here = send(v_send, Z_MIRROR)
    u_own = assemble(place, [u_blocks[0]] + [send(u_blocks[k], X_STEP[k]) for k in range(1, NX)])
    v_blocks = [v_here[k * SLOT:(k + 1) * SLOT] for k in range(NX)]
    v_own = assemble(place, [v_blocks[0]] + [send(v_blocks[k], X_STEP[k]) for k in range(1, NX)])

    u_near, u_far = gather_z(u_own, inner)
    v_near, v_far = gather_z(v_own, inner)

    far1 = jnp.where(z < 2, 2, 1)
    far2 = jnp.where(z < 2, 3, 0)
    items = [
        (u_own, 0, [z]),
        (u_near, 0, [z ^ 1]),
        (u_far, 0, [far1, far2]),
        (jnp.concatenate([v_own, v_near], axis=0), 1, [z, z ^ 1]),
        (v_far, 1, [far1, far2]),
    ]

    def offsets(kind, zs):
        at = []
        for k in range(NY):
            yy = (y - k * (1 - 2 * dp)) % NY
            for zz in zs:
                src, hi = (zz, zhi) if kind == 0 else (NZ - 1 - zz, 1 - zhi)
                at.append((yy * NZ + src) * (2 * HALF) + hi * HALF)
        return jnp.stack(at).astype(jnp.int32)

    wt = weight.T
    gate_f = gate.astype(jnp.float32)
    hid = (gate_f * jax.nn.sigmoid(gate_f) * up.astype(jnp.float32)).astype(jnp.bfloat16)
    theirs = (1 - dp).astype(jnp.int32).reshape(1)
    mine = dp.astype(jnp.int32).reshape(1)

    gathered = [(ring_y(own), offsets(kind, zs)) for own, kind, zs in items]
    outs = None
    for rows, offs in gathered:
        outs = hidden_grads(rows, offs, wt, gate, up, outs)
    groups = [gathered[0:3], gathered[3:4], gathered[4:5]]
    sums = [None, None]
    for group in groups:
        rows = [r for part in group for r in part[0]]
        offs = jnp.concatenate([part[1] for part in group])
        sums = [weight_grad_part(rows, h, offs, hid, s) for h, s in zip((theirs, mine), sums)]
    got = send(sums[0], DP_SWAP)
    n_tok = 2 * 64 * 8 * 16
    factor = 1.0 / jnp.sqrt(jnp.float32(n_tok))
    weight_grad = ((sums[1] + got) * factor).astype(jnp.bfloat16)
    return (outs[0][None, None], outs[1][None, None], weight_grad[None])


def solution(mesh):
    in_specs = (
        P("dp", ("expert", "tensor"), None),
        P("dp", ("expert", "tensor")),
        P("dp", ("expert", "tensor"), None),
        P("dp", "expert", None, "tensor"),
        P("dp", "expert", None, "tensor"),
        P("expert", "tensor", None),
    )
    out_specs = (
        P("dp", "expert", None, "tensor"),
        P("dp", "expert", None, "tensor"),
        P("expert", "tensor", "dp"),
    )
    return jax.shard_map(
        per_device, mesh=mesh, in_specs=in_specs, out_specs=out_specs, check_vma=False
    )
```

time: 382 us -> 252 us (0.66)
  waiting for transfers between devices: 303 us -> 86 us
  Pallas kernels: 0 us -> 77 us
  starting transfers between devices: 0.08 us -> 61.6 us
  matrix products: 28.1 us -> 0 us
  blocking collectives: 28.1 us -> 0 us
  local copies, waits for them, and re-layouts: 0.01 us -> 14.4 us
  between operations: 14.1 us -> 1.26 us
    all_gather x1 -> x0, waiting for transfers between devices: 276 us -> none  [per_device(): rows = lax.all_gather(received, 'tensor', axis=0, tiled=True)]
    ppermute x0 -> x33, waiting for transfers between devices: none -> 86 us  [send(): return lax.ppermute(a, AX, pairs)]
    pallas_call x0 -> x14, Pallas kernels: none -> 77 us  [the longest x6 42.7 us: weight_grad_part(): pl.pallas_call(functools.partial(weight_grad_kernel, counts, fresh), out_...]
    ppermute x0 -> x33, starting transfers between devices: none -> 61.6 us  [send(): return lax.ppermute(a, AX, pairs)]
    dot_general x2 -> x0, matrix products: 28.1 us -> none  [the longest x1 15.3 us: local_grads(): lax.dot_general(rows, weight_local, (((1,), (1,)), ((), ())), preferred_e...]
    all_to_all x1 -> x0, blocking collectives: 28.1 us -> none  [per_device(): lax.all_to_all(send_buf, 'expert', split_axis=0, concat_axis=0, tiled=True)]
    psum x1 -> x0, waiting for transfers between devices: 27.2 us -> none  [per_device(): summed = lax.psum(partial_w, 'dp')]
    unnamed x2 -> x71, local copies, waits for them, and re-layouts: 0.01 us -> 10.7 us
  transfers between devices with their start and end apart: 2 -> 33, of which waited for: 2 -> 17; matrix products, arithmetic and copies ran while one was open for 4% -> 5% of each run, Pallas kernels for 0% -> 27%
where the time goes in v1:
time: 252 us; the launch traced here: 250 us
  waiting for transfers between devices  86 us (34%)
  Pallas kernels  77 us (31%)
  starting transfers between devices  61.6 us (24%)
  local copies, waits for them, and re-layouts  14.4 us (6%)
  other arithmetic  10.1 us (4%)
    ppermute x33, waiting for transfers between devices, send(): return lax.ppermute(a, AX, pairs)  86 us
    ppermute x33, starting transfers between devices, send(): return lax.ppermute(a, AX, pairs)  61.6 us
    pallas_call x6, Pallas kernels, weight_grad_part(): pl.pallas_call(functools.partial(weight_grad_kernel, counts, fresh), out_...  42.7 us
    pallas_call x5, Pallas kernels, hidden_grads(): pl.pallas_call(functools.partial(hidden_grad_kernel, counts, fresh), out_...  28.3 us
    unnamed x71, local copies, waits for them, and re-layouts  10.7 us
  transfers between devices with their start and end apart: 33, of which 17 were waited for; matrix products, arithmetic and copies ran while one was open for 5% of the time, Pallas kernels for 27%

profile of v1, /device:TPU:1, one launch (start us, length us, event | category | flops | bytes accessed | tf_op | source)
XLA Modules:
  0.0 250.3 jit_solution(12947687293298939333)
XLA Ops:
  0.6 1.4 copy.21.scales
  2.0 1.4 copy.22.ids_col
  4.0 2.3 dispatch.1
  6.3 6.4 %collective-permute-start = (bf16[64,3072]{1,0:T(8,128)(2,1)}, bf16[64,3072]{1,0:T(8,128)(2,1)S(1)}, u32[]{:S(2)}, u32[]{:S(2)}) collective-permute-start(bf16[64,3072]{1,0:T(8,128)(2,1)} %get-tuple-element.18), channel_id=1, source_target_pairs={{0,67},{4,71},{8,75},{12,79},{16,83},{20,87},{24,91},{28,95},{32,9... | collective-permute-start | bytes 1179656 | tf_op jit(solution)/shard_map/ppermute | solution.py:45
  13.9 2.5 collective-permute-start.16
  17.5 13.0 %collective-permute-done = bf16[64,3072]{1,0:T(8,128)(2,1)S(1)} collective-permute-done((bf16[64,3072]{1,0:T(8,128)(2,1)}, bf16[64,3072]{1,0:T(8,128)(2,1)S(1)}, u32[]{:S(2)}, u32[]{:S(2)}) %collective-permute-start) | collective-permute-done | bytes 393248 | tf_op jit(solution)/shard_map/ppermute | solution.py:45
  32.4 2.5 collective-permute-start.2
  36.7 1.8 assemble.3.refs_1_.refs_2_
  40.1 1.8 assemble.2
  41.9 3.2 %collective-permute-start.6 = (bf16[64,3072]{1,0:T(8,128)(2,1)}, bf16[64,3072]{1,0:T(8,128)(2,1)}, u32[]{:S(2)}, u32[]{:S(2)}) collective-permute-start(bf16[64,3072]{1,0:T(8,128)(2,1)} %assemble.2), channel_id=1, source_target_pairs={{0,1},{4,5},{8,9},{12,13},{16,17},{20,21},{24,25},{28,29},{32,33},... | collective-permute-start | bytes 1179656 | tf_op jit(solution)/shard_map/ppermute | solution.py:45
  45.1 2.5 collective-permute-done.20.refs_1_.refs_6_
  48.2 1.4 collective-permute-start.4
  51.0 5.1 %collective-permute-done.6 = bf16[64,3072]{1,0:T(8,128)(2,1)} collective-permute-done((bf16[64,3072]{1,0:T(8,128)(2,1)}, bf16[64,3072]{1,0:T(8,128)(2,1)}, u32[]{:S(2)}, u32[]{:S(2)}) %collective-permute-start.6) | collective-permute-done | bytes 393248 | tf_op jit(solution)/shard_map/ppermute | solution.py:45
  57.3 2.8 %collective-permute-start.12 = (bf16[128,3072]{1,0:T(8,128)(2,1)S(1)}, bf16[128,3072]{1,0:T(8,128)(2,1)}, u32[]{:S(2)}, u32[]{:S(2)}) collective-permute-start(bf16[128,3072]{1,0:T(8,128)(2,1)S(1)} %pad_maximum_fusion.1.refs_1_.refs_2_), channel_id=1, source_target_pairs={{0,4},{4,8},{8,12},{12,0},{16,20},{20,24},{24,28},{28,16},{32,36},... | collective-permute-start | bytes 2359304 | tf_op jit(solution)/shard_map/ppermute | solution.py:45
  60.8 1.3 collective-permute-start.22
  64.4 7.8 %collective-permute-done.22 = bf16[64,3072]{1,0:T(8,128)(2,1)S(1)} collective-permute-done((bf16[64,3072]{1,0:T(8,128)(2,1)S(1)}, bf16[64,3072]{1,0:T(8,128)(2,1)S(1)}, u32[]{:S(2)}, u32[]{:S(2)}) %collective-permute-start.22) | collective-permute-done | bytes 393248 | tf_op jit(solution)/shard_map/ppermute | solution.py:45
  72.4 3.4 %collective-permute-start.23 = (bf16[128,3072]{1,0:T(8,128)(2,1)S(1)}, bf16[128,3072]{1,0:T(8,128)(2,1)S(1)}, u32[]{:S(2)}, u32[]{:S(2)}) collective-permute-start(bf16[128,3072]{1,0:T(8,128)(2,1)S(1)} %pad_maximum_fusion.2.refs_1_.refs_10_), channel_id=1, source_target_pairs={{0,4},{4,8},{8,12},{12,0},{16,20},{20,24},{24,28},{28,16},{32,36},... | collective-permute-start | bytes 2359304 | tf_op jit(solution)/shard_map/ppermute | solution.py:45
  77.1 3.4 %collective-permute-done.5 = bf16[64,3072]{1,0:T(8,128)(2,1)S(1)} collective-permute-done((bf16[64,3072]{1,0:T(8,128)(2,1)}, bf16[64,3072]{1,0:T(8,128)(2,1)S(1)}, u32[]{:S(2)}, u32[]{:S(2)}) %collective-permute-start.5) | collective-permute-done | bytes 393248 | tf_op jit(solution)/shard_map/ppermute | solution.py:45
  80.6 8.4 %collective-permute-done.8 = bf16[64,3072]{1,0:T(8,128)(2,1)S(1)} collective-permute-done((bf16[64,3072]{1,0:T(8,128)(2,1)S(1)}, bf16[64,3072]{1,0:T(8,128)(2,1)S(1)}, u32[]{:S(2)}, u32[]{:S(2)}) %collective-permute-start.8) | collective-permute-done | bytes 393248 | tf_op jit(solution)/shard_map/ppermute | solution.py:45
  89.1 3.4 %collective-permute-start.9 = (bf16[128,3072]{1,0:T(8,128)(2,1)S(1)}, bf16[128,3072]{1,0:T(8,128)(2,1)}, u32[]{:S(2)}, u32[]{:S(2)}) collective-permute-start(bf16[128,3072]{1,0:T(8,128)(2,1)S(1)} %pad_maximum_fusion.refs_1_.refs_2_), channel_id=1, source_target_pairs={{0,4},{4,8},{8,12},{12,0},{16,20},{20,24},{24,28},{28,16},{32,36},... | collective-permute-start | bytes 2359304 | tf_op jit(solution)/shard_map/ppermute | solution.py:45
  94.8 3.1 %collective-permute-start.13 = (bf16[128,3072]{1,0:T(8,128)(2,1)}, bf16[128,3072]{1,0:T(8,128)(2,1)}, u32[]{:S(2)}, u32[]{:S(2)}) collective-permute-start(bf16[128,3072]{1,0:T(8,128)(2,1)} %collective-permute-done.12.refs_2_.refs_3_), channel_id=1, source_target_pairs={{0,4},{4,8},{8,12},{12,0},{16,20},{20,24},{24,28},{28,16},{32,36},... | collective-permute-start | bytes 2359304 | tf_op jit(solution)/shard_map/ppermute | solution.py:45
  97.9 3.5 %collective-permute-done.9.refs_2_.refs_3_ = bf16[128,3072]{1,0:T(8,128)(2,1)} collective-permute-done((bf16[128,3072]{1,0:T(8,128)(2,1)S(1)}, bf16[128,3072]{1,0:T(8,128)(2,1)}, u32[]{:S(2)}, u32[]{:S(2)}) %collective-permute-start.9) | collective-permute-done | bytes 786464 | tf_op jit(solution)/shard_map/ppermute | solution.py:45
  101.5 3.2 %collective-permute-start.10 = (bf16[128,3072]{1,0:T(8,128)(2,1)}, bf16[128,3072]{1,0:T(8,128)(2,1)}, u32[]{:S(2)}, u32[]{:S(2)}) collective-permute-start(bf16[128,3072]{1,0:T(8,128)(2,1)} %collective-permute-done.9.refs_2_.refs_3_), channel_id=1, source_target_pairs={{0,4},{4,8},{8,12},{12,0},{16,20},{20,24},{24,28},{28,16},{32,36},... | collective-permute-start | bytes 2359304 | tf_op jit(solution)/shard_map/ppermute | solution.py:45
  104.7 9.4 %collective-permute-done.29.refs_2_.refs_3_ = bf16[64,3072]{1,0:T(8,128)(2,1)} collective-permute-done((bf16[64,3072]{1,0:T(8,128)(2,1)S(1)}, bf16[64,3072]{1,0:T(8,128)(2,1)}, u32[]{:S(2)}, u32[]{:S(2)}) %collective-permute-start.29) | collective-permute-done | bytes 393248 | tf_op jit(solution)/shard_map/ppermute | solution.py:45
  114.1 3.2 %collective-permute-start.30 = (bf16[64,3072]{1,0:T(8,128)(2,1)}, bf16[64,3072]{1,0:T(8,128)(2,1)}, u32[]{:S(2)}, u32[]{:S(2)}) collective-permute-start(bf16[64,3072]{1,0:T(8,128)(2,1)} %collective-permute-done.29.refs_2_.refs_3_), channel_id=1, source_target_pairs={{0,4},{4,8},{8,12},{12,0},{16,20},{20,24},{24,28},{28,16},{32,36},... | collective-permute-start | bytes 1179656 | tf_op jit(solution)/shard_map/ppermute | solution.py:45
  118.3 3.2 %collective-permute-start.27 = (bf16[64,3072]{1,0:T(8,128)(2,1)}, bf16[64,3072]{1,0:T(8,128)(2,1)}, u32[]{:S(2)}, u32[]{:S(2)}) collective-permute-start(bf16[64,3072]{1,0:T(8,128)(2,1)} %collective-permute-done.26.refs_2_.refs_7_), channel_id=1, source_target_pairs={{0,4},{4,8},{8,12},{12,0},{16,20},{20,24},{24,28},{28,16},{32,36},... | collective-permute-start | bytes 1179656 | tf_op jit(solution)/shard_map/ppermute | solution.py:45
  121.9 17.6 %collective-permute-done.30.refs_3_.refs_4_ = bf16[64,3072]{1,0:T(8,128)(2,1)} collective-permute-done((bf16[64,3072]{1,0:T(8,128)(2,1)}, bf16[64,3072]{1,0:T(8,128)(2,1)}, u32[]{:S(2)}, u32[]{:S(2)}) %collective-permute-start.30) | collective-permute-done | bytes 393248 | tf_op jit(solution)/shard_map/ppermute | solution.py:45
  139.5 3.1 %collective-permute-start.31 = (bf16[64,3072]{1,0:T(8,128)(2,1)}, bf16[64,3072]{1,0:T(8,128)(2,1)S(1)}, u32[]{:S(2)}, u32[]{:S(2)}) collective-permute-start(bf16[64,3072]{1,0:T(8,128)(2,1)} %collective-permute-done.30.refs_3_.refs_4_), channel_id=1, source_target_pairs={{0,4},{4,8},{8,12},{12,0},{16,20},{20,24},{24,28},{28,16},{32,36},... | collective-permute-start | bytes 1179656 | tf_op jit(solution)/shard_map/ppermute | solution.py:45
  143.7 3.1 %collective-permute-start.28 = (bf16[64,3072]{1,0:T(8,128)(2,1)}, bf16[64,3072]{1,0:T(8,128)(2,1)S(1)}, u32[]{:S(2)}, u32[]{:S(2)}) collective-permute-start(bf16[64,3072]{1,0:T(8,128)(2,1)} %collective-permute-done.27.refs_3_.refs_8_), channel_id=1, source_target_pairs={{0,4},{4,8},{8,12},{12,0},{16,20},{20,24},{24,28},{28,16},{32,36},... | collective-permute-start | bytes 1179656 | tf_op jit(solution)/shard_map/ppermute | solution.py:45
  146.9 4.1 %fusion.4.refs_14_.refs_6_ = bf16[2048,512]{1,0:T(8,128)(2,1)} fusion(bf16[1,1,2048,512]{3,2,1,0:T(8,128)(2,1)} %param.10, bf16[1,1,2048,512]{3,2,1,0:T(8,128)(2,1)S(1)} %copy-done.2), kind=kLoop, calls=%fused_computation.6 | loop fusion | flops 8388608 | bytes 6291456 | tf_op jit(solution)/shard_map/convert_element_type | solution.py:295
  151.1 5.3 %collective-permute-done.31.refs_4_.refs_5_ = bf16[64,3072]{1,0:T(8,128)(2,1)S(1)} collective-permute-done((bf16[64,3072]{1,0:T(8,128)(2,1)}, bf16[64,3072]{1,0:T(8,128)(2,1)S(1)}, u32[]{:S(2)}, u32[]{:S(2)}) %collective-permute-start.31) | collective-permute-done | bytes 393248 | tf_op jit(solution)/shard_map/ppermute | solution.py:45
  156.4 4.2 %collective-permute-done.28.refs_4_.refs_9_ = bf16[64,3072]{1,0:T(8,128)(2,1)S(1)} collective-permute-done((bf16[64,3072]{1,0:T(8,128)(2,1)}, bf16[64,3072]{1,0:T(8,128)(2,1)S(1)}, u32[]{:S(2)}, u32[]{:S(2)}) %collective-permute-start.28) | collective-permute-done | bytes 393248 | tf_op jit(solution)/shard_map/ppermute | solution.py:45
  160.6 7.4 %weight_grad_part.9.refs_7_ = f32[512,1536]{1,0:T(8,128)} custom-call(s32[1]{0:T(128)} %bitcast.46.refs_0_, s32[16]{0:T(128)S(1)} %concatenate.16.refs_1_, bf16[64,3072]{1,0:T(8,128)(2,1)S(1)} %copy-done.18, bf16[64,3072]{1,0:T(8,128)(2,1)} %collective-permute-done.29.refs_2_.refs_3_, bf16[64,3072]{1,0:T(8,128)(2,1)} %collective-permute-done.30.refs_3_.refs_4_, ...), custom_call_target="tpu_custom_call" | custom-call | flops 1610612736 | bytes 10485760 | tf_op jit(solution)/shard_map/weight_grad_part/pallas_call | solution.py:223
  169.0 6.9 %weight_grad_part.10.refs_7_ = f32[512,1536]{1,0:T(8,128)} custom-call(s32[1]{0:T(128)} %bitcast.46.refs_0_, s32[8]{0:T(128)S(1)} %stack.140.refs_0_.refs_1_, bf16[128,3072]{1,0:T(8,128)(2,1)S(1)} %pad_maximum_fusion.1.refs_1_.refs_2_, bf16[128,3072]{1,0:T(8,128)(2,1)} %collective-permute-done.12.refs_2_.refs_3_, ...), custom_call_target="tpu_custom_call", output_to_operand_aliasing={{}: (7, {})} | custom-call | flops 805306368 | bytes 8388608 | tf_op jit(solution)/shard_map/weight_grad_part/pallas_call | solution.py:223
  175.9 1.5 collective-permute-done.11.refs_4_.refs_5_
  177.4 6.9 %weight_grad_part.11 = f32[512,1536]{1,0:T(8,128)} custom-call(s32[1]{0:T(128)} %bitcast.46.refs_0_, s32[8]{0:T(128)S(1)} %stack.128.refs_0_.refs_1_, bf16[128,3072]{1,0:T(8,128)(2,1)S(1)} %copy-done.9, bf16[128,3072]{1,0:T(8,128)(2,1)} %collective-permute-done.9.refs_2_.refs_3_, ...), custom_call_target="tpu_custom_call", output_to_operand_aliasing={{}: (7, {})} | custom-call | flops 805306368 | bytes 8388608 | tf_op jit(solution)/shard_map/weight_grad_part/pallas_call | solution.py:223
  184.3 4.5 %collective-permute-start.32 = (f32[512,1536]{1,0:T(8,128)}, f32[512,1536]{1,0:T(8,128)}, u32[]{:S(2)}, u32[]{:S(2)}) collective-permute-start(f32[512,1536]{1,0:T(8,128)} %weight_grad_part.11), channel_id=1, source_target_pairs={{0,128},{4,132},{8,136},{12,140},{16,144},{20,148},{24,152},{28,15... | collective-permute-start | bytes 9437192 | tf_op jit(solution)/shard_map/ppermute | solution.py:45
  188.9 4.8 %copy.23 = bf16[1,512,3072]{1,2,0:T(8,128)(2,1)} copy(bf16[1,512,3072]{2,1,0:T(8,128)(2,1)} %param.11) | data formatting | bytes 6291456 | tf_op args[5]
  193.9 1.6 copy-done.4
  196.5 4.7 %hidden_grads.5 = (bf16[2048,512]{1,0:T(8,128)(2,1)}, bf16[2048,512]{1,0:T(8,128)(2,1)}) custom-call(s32[4]{0:T(128)S(1)} %pad_add_fusion.2.refs_0_, bf16[64,3072]{1,0:T(8,128)(2,1)S(1)} %copy-done.18, bf16[64,3072]{1,0:T(8,128)(2,1)} %collective-permute-done.29.refs_2_.refs_3_, bf16[64,3072]{1,0:T(8,128)(2,1)} %collective-permute-done.30.refs_3_.refs_4_, ...), custom_call_target="tpu_custom_call" | custom-call | flops 805306368 | bytes 5767168 | tf_op jit(solution)/shard_map/hidden_grads/pallas_call | solution.py:149
  201.2 4.7 %hidden_grads.6 = (bf16[2048,512]{1,0:T(8,128)(2,1)}, bf16[2048,512]{1,0:T(8,128)(2,1)}) custom-call(s32[4]{0:T(128)S(1)} %pad_add_fusion.1.refs_0_, bf16[64,3072]{1,0:T(8,128)(2,1)S(1)} %copy-done.22, bf16[64,3072]{1,0:T(8,128)(2,1)} %collective-permute-done.26.refs_2_.refs_7_, ...), custom_call_target="tpu_custom_call", output_to_operand_aliasing={{0}: (8, {}), {1}: (9, {})} | custom-call | flops 805306368 | bytes 5767168 | tf_op jit(solution)/shard_map/hidden_grads/pallas_call | solution.py:149
  206.0 7.6 %weight_grad_part.6.refs_7_ = f32[512,1536]{1,0:T(8,128)} custom-call(s32[1]{0:T(128)} %bitcast.45.refs_0_, s32[16]{0:T(128)S(1)} %concatenate.16.refs_1_, bf16[64,3072]{1,0:T(8,128)(2,1)S(1)} %copy-done.18, bf16[64,3072]{1,0:T(8,128)(2,1)} %collective-permute-done.29.refs_2_.refs_3_, bf16[64,3072]{1,0:T(8,128)(2,1)} %collective-permute-done.30.refs_3_.refs_4_, ...), custom_call_target="tpu_custom_call" | custom-call | flops 1610612736 | bytes 10485760 | tf_op jit(solution)/shard_map/weight_grad_part/pallas_call | solution.py:223
  213.6 7.0 %weight_grad_part.7.refs_7_ = f32[512,1536]{1,0:T(8,128)} custom-call(s32[1]{0:T(128)} %bitcast.45.refs_0_, s32[8]{0:T(128)S(1)} %stack.140.refs_0_.refs_1_, bf16[128,3072]{1,0:T(8,128)(2,1)S(1)} %pad_maximum_fusion.1.refs_1_.refs_2_, bf16[128,3072]{1,0:T(8,128)(2,1)} %collective-permute-done.12.refs_2_.refs_3_, ...), custom_call_target="tpu_custom_call", output_to_operand_aliasing={{}: (7, {})} | custom-call | flops 805306368 | bytes 8388608 | tf_op jit(solution)/shard_map/weight_grad_part/pallas_call | solution.py:223
  220.6 6.2 %hidden_grads.7 = (bf16[2048,512]{1,0:T(8,128)(2,1)}, bf16[2048,512]{1,0:T(8,128)(2,1)}) custom-call(s32[8]{0:T(128)S(1)} %stack.149.refs_0_, bf16[128,3072]{1,0:T(8,128)(2,1)S(1)} %copy-done.7, bf16[128,3072]{1,0:T(8,128)(2,1)S(1)} %copy-done.13, ...), custom_call_target="tpu_custom_call", output_to_operand_aliasing={{0}: (8, {}), {1}: (9, {})} | custom-call | flops 1610612736 | bytes 8388608 | tf_op jit(solution)/shard_map/hidden_grads/pallas_call | solution.py:149
  226.8 6.2 %hidden_grads.8 = (bf16[2048,512]{1,0:T(8,128)(2,1)}, bf16[2048,512]{1,0:T(8,128)(2,1)}) custom-call(s32[8]{0:T(128)S(1)} %stack.140.refs_0_.refs_1_, bf16[128,3072]{1,0:T(8,128)(2,1)S(1)} %pad_maximum_fusion.1.refs_1_.refs_2_, bf16[128,3072]{1,0:T(8,128)(2,1)} %collective-permute-done.12.refs_2_.refs_3_, ...), custom_call_target="tpu_custom_call", output_to_operand_aliasing={{0}: (8, {}), {1}: (9, {})} | custom-call | flops 1610612736 | bytes 8388608 | tf_op jit(solution)/shard_map/hidden_grads/pallas_call | solution.py:149
  233.1 7.0 %weight_grad_part.8 = f32[512,1536]{1,0:T(8,128)} custom-call(s32[1]{0:T(128)} %bitcast.45.refs_0_, s32[8]{0:T(128)S(1)} %stack.128.refs_0_.refs_1_, bf16[128,3072]{1,0:T(8,128)(2,1)S(1)} %copy-done.10, bf16[128,3072]{1,0:T(8,128)(2,1)} %collective-permute-done.9.refs_2_.refs_3_, ...), custom_call_target="tpu_custom_call", output_to_operand_aliasing={{}: (7, {})} | custom-call | flops 805306368 | bytes 8388608 | tf_op jit(solution)/shard_map/weight_grad_part/pallas_call | solution.py:223
  240.1 6.5 %hidden_grads.9 = (bf16[2048,512]{1,0:T(8,128)(2,1)}, bf16[2048,512]{1,0:T(8,128)(2,1)}) custom-call(s32[8]{0:T(128)S(1)} %stack.128.refs_0_.refs_1_, bf16[128,3072]{1,0:T(8,128)(2,1)S(1)} %copy-done.10, bf16[128,3072]{1,0:T(8,128)(2,1)} %collective-permute-done.9.refs_2_.refs_3_, ...), custom_call_target="tpu_custom_call", output_to_operand_aliasing={{0}: (8, {}), {1}: (9, {})} | custom-call | flops 1610612736 | bytes 8388608 | tf_op jit(solution)/shard_map/hidden_grads/pallas_call | solution.py:149
  246.6 3.8 %fusion.5 = bf16[1,512,1536]{2,1,0:T(8,128)(2,1)} fusion(f32[512,1536]{1,0:T(8,128)S(1)} %copy-done.28, f32[512,1536]{1,0:T(8,128)} %collective-permute-done.32), kind=kLoop, calls=%fused_computation.8 | loop fusion | flops 2359296 | bytes 7864320 | tf_op jit(solution)/shard_map/broadcast_in_dim | solution.py:313
  (122 shorter events, 22.9 us)
Async XLA Ops:
  6.3 24.2 %collective-permute-start = (bf16[64,3072]{1,0:T(8,128)(2,1)}, bf16[64,3072]{1,0:T(8,128)(2,1)S(1)}, u32[]{:S(2)}, u32[]{:S(2)}) collective-permute-start(bf16[64,3072]{1,0:T(8,128)(2,1)} %get-tuple-element.18), channel_id=1, source_target_pairs={{0,67},{4,71},{8,75},{12,79},{16,83},{20,87},{24,91},{28,95},{32,9... | collective-permute-start | bytes 1179656 | tf_op jit(solution)/shard_map/ppermute | solution.py:45
  12.7 22.1 %collective-permute-start.15 = (bf16[16,3072]{1,0:T(8,128)(2,1)}, bf16[16,3072]{1,0:T(8,128)(2,1)S(1)}, u32[]{:S(2)}, u32[]{:S(2)}) collective-permute-start(bf16[16,3072]{1,0:T(8,128)(2,1)} %get-tuple-element.20), channel_id=1, source_target_pairs={{0,16},{4,20},{8,24},{12,28},{16,32},{20,36},{24,40},{28,44},{32,4... | collective-permute-start | bytes 294920 | tf_op jit(solution)/shard_map/ppermute | solution.py:45
  13.9 22.1 %collective-permute-start.16 = (bf16[16,3072]{1,0:T(8,128)(2,1)}, bf16[16,3072]{1,0:T(8,128)(2,1)S(1)}, u32[]{:S(2)}, u32[]{:S(2)}) collective-permute-start(bf16[16,3072]{1,0:T(8,128)(2,1)} %get-tuple-element.21), channel_id=1, source_target_pairs={{0,32},{4,36},{8,40},{12,44},{16,48},{20,52},{24,56},{28,60},{32,0... | collective-permute-start | bytes 294920 | tf_op jit(solution)/shard_map/ppermute | solution.py:45
  16.4 19.6 %collective-permute-start.17 = (bf16[16,3072]{1,0:T(8,128)(2,1)}, bf16[16,3072]{1,0:T(8,128)(2,1)S(1)}, u32[]{:S(2)}, u32[]{:S(2)}) collective-permute-start(bf16[16,3072]{1,0:T(8,128)(2,1)} %get-tuple-element.22), channel_id=1, source_target_pairs={{0,48},{4,52},{8,56},{12,60},{16,0},{20,4},{24,8},{28,12},{32,16},... | collective-permute-start | bytes 294920 | tf_op jit(solution)/shard_map/ppermute | solution.py:45
  31.1 8.0 %collective-permute-start.1 = (bf16[16,3072]{1,0:T(8,128)(2,1)S(1)}, bf16[16,3072]{1,0:T(8,128)(2,1)S(1)}, u32[]{:S(2)}, u32[]{:S(2)}) collective-permute-start(bf16[16,3072]{1,0:T(8,128)(2,1)S(1)} %get-tuple-element.35), channel_id=1, source_target_pairs={{0,16},{4,20},{8,24},{12,28},{16,32},{20,36},{24,40},{28,44},{32,4... | collective-permute-start | bytes 294920 | tf_op jit(solution)/shard_map/ppermute | solution.py:45
  32.4 6.8 %collective-permute-start.2 = (bf16[16,3072]{1,0:T(8,128)(2,1)S(1)}, bf16[16,3072]{1,0:T(8,128)(2,1)S(1)}, u32[]{:S(2)}, u32[]{:S(2)}) collective-permute-start(bf16[16,3072]{1,0:T(8,128)(2,1)S(1)} %get-tuple-element.34), channel_id=1, source_target_pairs={{0,32},{4,36},{8,40},{12,44},{16,48},{20,52},{24,56},{28,60},{32,0... | collective-permute-start | bytes 294920 | tf_op jit(solution)/shard_map/ppermute | solution.py:45
  34.8 4.6 %collective-permute-start.3 = (bf16[16,3072]{1,0:T(8,128)(2,1)S(1)}, bf16[16,3072]{1,0:T(8,128)(2,1)S(1)}, u32[]{:S(2)}, u32[]{:S(2)}) collective-permute-start(bf16[16,3072]{1,0:T(8,128)(2,1)S(1)} %get-tuple-element.33), channel_id=1, source_target_pairs={{0,48},{4,52},{8,56},{12,60},{16,0},{20,4},{24,8},{28,12},{32,16},... | collective-permute-start | bytes 294920 | tf_op jit(solution)/shard_map/ppermute | solution.py:45
  38.5 9.1 %collective-permute-start.20 = (bf16[64,3072]{1,0:T(8,128)(2,1)}, bf16[64,3072]{1,0:T(8,128)(2,1)S(1)}, u32[]{:S(2)}, u32[]{:S(2)}) collective-permute-start(bf16[64,3072]{1,0:T(8,128)(2,1)} %assemble.3.refs_1_.refs_2_), channel_id=1, source_target_pairs={{0,1},{4,5},{8,9},{12,13},{16,17},{20,21},{24,25},{28,29},{32,33},... | collective-permute-start | bytes 1179656 | tf_op jit(solution)/shard_map/ppermute | solution.py:45
  38.5 11.2 %collective-permute-start.18 = (bf16[64,3072]{1,0:T(8,128)(2,1)}, bf16[64,3072]{1,0:T(8,128)(2,1)S(1)}, u32[]{:S(2)}, u32[]{:S(2)}) collective-permute-start(bf16[64,3072]{1,0:T(8,128)(2,1)} %assemble.3.refs_1_.refs_2_), channel_id=1, source_target_pairs={{1,2},{5,6},{9,10},{13,14},{17,18},{21,22},{25,26},{29,30},{33,34}... | collective-permute-start | bytes 1179656 | tf_op jit(solution)/shard_map/ppermute | solution.py:45
  41.9 14.2 %collective-permute-start.6 = (bf16[64,3072]{1,0:T(8,128)(2,1)}, bf16[64,3072]{1,0:T(8,128)(2,1)}, u32[]{:S(2)}, u32[]{:S(2)}) collective-permute-start(bf16[64,3072]{1,0:T(8,128)(2,1)} %assemble.2), channel_id=1, source_target_pairs={{0,1},{4,5},{8,9},{12,13},{16,17},{20,21},{24,25},{28,29},{32,33},... | collective-permute-start | bytes 1179656 | tf_op jit(solution)/shard_map/ppermute | solution.py:45
  47.5 24.7 %copy-start.19 = (bf16[64,3072]{1,0:T(8,128)(2,1)}, bf16[64,3072]{1,0:T(8,128)(2,1)S(1)}, u32[]{:S(2)}) copy-start(bf16[64,3072]{1,0:T(8,128)(2,1)S(1)} %collective-permute-done.20.refs_1_.refs_6_) | copy-start | bytes 1179652
  47.6 13.2 %collective-permute-start.21 = (bf16[64,3072]{1,0:T(8,128)(2,1)S(1)}, bf16[64,3072]{1,0:T(8,128)(2,1)S(1)}, u32[]{:S(2)}, u32[]{:S(2)}) collective-permute-start(bf16[64,3072]{1,0:T(8,128)(2,1)S(1)} %collective-permute-done.20.refs_1_.refs_6_), channel_id=1, source_target_pairs={{1,2},{5,6},{9,10},{13,14},{17,18},{21,22},{25,26},{29,30},{33,34}... | collective-permute-start | bytes 1179656 | tf_op jit(solution)/shard_map/ppermute | solution.py:45
  48.2 13.8 %collective-permute-start.4 = (bf16[64,3072]{1,0:T(8,128)(2,1)}, bf16[64,3072]{1,0:T(8,128)(2,1)}, u32[]{:S(2)}, u32[]{:S(2)}) collective-permute-start(bf16[64,3072]{1,0:T(8,128)(2,1)} %assemble.2), channel_id=1, source_target_pairs={{1,2},{5,6},{9,10},{13,14},{17,18},{21,22},{25,26},{29,30},{33,34}... | collective-permute-start | bytes 1179656 | tf_op jit(solution)/shard_map/ppermute | solution.py:45
  49.7 14.7 %collective-permute-start.19 = (bf16[64,3072]{1,0:T(8,128)(2,1)S(1)}, bf16[64,3072]{1,0:T(8,128)(2,1)S(1)}, u32[]{:S(2)}, u32[]{:S(2)}) collective-permute-start(bf16[64,3072]{1,0:T(8,128)(2,1)S(1)} %collective-permute-done.18), channel_id=1, source_target_pairs={{1,0},{5,4},{9,8},{13,12},{17,16},{21,20},{25,24},{29,28},{33,32},... | collective-permute-start | bytes 1179656 | tf_op jit(solution)/shard_map/ppermute | solution.py:45
  57.3 37.5 %collective-permute-start.12 = (bf16[128,3072]{1,0:T(8,128)(2,1)S(1)}, bf16[128,3072]{1,0:T(8,128)(2,1)}, u32[]{:S(2)}, u32[]{:S(2)}) collective-permute-start(bf16[128,3072]{1,0:T(8,128)(2,1)S(1)} %pad_maximum_fusion.1.refs_1_.refs_2_), channel_id=1, source_target_pairs={{0,4},{4,8},{8,12},{12,0},{16,20},{20,24},{24,28},{28,16},{32,36},... | collective-permute-start | bytes 2359304 | tf_op jit(solution)/shard_map/ppermute | solution.py:45
  60.1 15.8 %collective-permute-start.7 = (bf16[64,3072]{1,0:T(8,128)(2,1)}, bf16[64,3072]{1,0:T(8,128)(2,1)S(1)}, u32[]{:S(2)}, u32[]{:S(2)}) collective-permute-start(bf16[64,3072]{1,0:T(8,128)(2,1)} %collective-permute-done.6), channel_id=1, source_target_pairs={{1,2},{5,6},{9,10},{13,14},{17,18},{21,22},{25,26},{29,30},{33,34}... | collective-permute-start | bytes 1179656 | tf_op jit(solution)/shard_map/ppermute | solution.py:45
  60.8 11.5 %collective-permute-start.22 = (bf16[64,3072]{1,0:T(8,128)(2,1)S(1)}, bf16[64,3072]{1,0:T(8,128)(2,1)S(1)}, u32[]{:S(2)}, u32[]{:S(2)}) collective-permute-start(bf16[64,3072]{1,0:T(8,128)(2,1)S(1)} %collective-permute-done.21), channel_id=1, source_target_pairs={{1,0},{5,4},{9,8},{13,12},{17,16},{21,20},{25,24},{29,28},{33,32},... | collective-permute-start | bytes 1179656 | tf_op jit(solution)/shard_map/ppermute | solution.py:45
  62.1 18.5 %collective-permute-start.5 = (bf16[64,3072]{1,0:T(8,128)(2,1)}, bf16[64,3072]{1,0:T(8,128)(2,1)S(1)}, u32[]{:S(2)}, u32[]{:S(2)}) collective-permute-start(bf16[64,3072]{1,0:T(8,128)(2,1)} %collective-permute-done.4), channel_id=1, source_target_pairs={{1,0},{5,4},{9,8},{13,12},{17,16},{21,20},{25,24},{29,28},{33,32},... | collective-permute-start | bytes 1179656 | tf_op jit(solution)/shard_map/ppermute | solution.py:45
  72.3 22.5 %copy-start.5 = (bf16[128,3072]{1,0:T(8,128)(2,1)}, bf16[128,3072]{1,0:T(8,128)(2,1)S(1)}, u32[]{:S(2)}) copy-start(bf16[128,3072]{1,0:T(8,128)(2,1)S(1)} %pad_maximum_fusion.2.refs_1_.refs_10_) | copy-start | bytes 2359300
  72.3 22.1 %copy-start.18 = (bf16[64,3072]{1,0:T(8,128)(2,1)S(1)}, bf16[64,3072]{1,0:T(8,128)(2,1)}, u32[]{:S(2)}) copy-start(bf16[64,3072]{1,0:T(8,128)(2,1)} %assemble.3.refs_1_.refs_2_) | copy-start | bytes 1179652
  72.4 22.2 %copy-start.20 = (bf16[64,3072]{1,0:T(8,128)(2,1)S(1)}, bf16[64,3072]{1,0:T(8,128)(2,1)}, u32[]{:S(2)}) copy-start(bf16[64,3072]{1,0:T(8,128)(2,1)} %copy-done.19) | copy-start | bytes 1179652
  72.4 74.6 %copy-start.2 = (bf16[1,1,2048,512]{3,2,1,0:T(8,128)(2,1)S(1)}, bf16[1,1,2048,512]{3,2,1,0:T(8,128)(2,1)}, u32[]{:S(2)}) copy-start(bf16[1,1,2048,512]{3,2,1,0:T(8,128)(2,1)} %param.9) | copy-start | bytes 6291460
  72.4 21.0 %collective-permute-start.23 = (bf16[128,3072]{1,0:T(8,128)(2,1)S(1)}, bf16[128,3072]{1,0:T(8,128)(2,1)S(1)}, u32[]{:S(2)}, u32[]{:S(2)}) collective-permute-start(bf16[128,3072]{1,0:T(8,128)(2,1)S(1)} %pad_maximum_fusion.2.refs_1_.refs_10_), channel_id=1, source_target_pairs={{0,4},{4,8},{8,12},{12,0},{16,20},{20,24},{24,28},{28,16},{32,36},... | collective-permute-start | bytes 2359304 | tf_op jit(solution)/shard_map/ppermute | solution.py:45
  75.8 13.1 %collective-permute-start.8 = (bf16[64,3072]{1,0:T(8,128)(2,1)S(1)}, bf16[64,3072]{1,0:T(8,128)(2,1)S(1)}, u32[]{:S(2)}, u32[]{:S(2)}) collective-permute-start(bf16[64,3072]{1,0:T(8,128)(2,1)S(1)} %collective-permute-done.7), channel_id=1, source_target_pairs={{1,0},{5,4},{9,8},{13,12},{17,16},{21,20},{25,24},{29,28},{33,32},... | collective-permute-start | bytes 1179656 | tf_op jit(solution)/shard_map/ppermute | solution.py:45
  89.1 12.4 %collective-permute-start.9 = (bf16[128,3072]{1,0:T(8,128)(2,1)S(1)}, bf16[128,3072]{1,0:T(8,128)(2,1)}, u32[]{:S(2)}, u32[]{:S(2)}) collective-permute-start(bf16[128,3072]{1,0:T(8,128)(2,1)S(1)} %pad_maximum_fusion.refs_1_.refs_2_), channel_id=1, source_target_pairs={{0,4},{4,8},{8,12},{12,0},{16,20},{20,24},{24,28},{28,16},{32,36},... | collective-permute-start | bytes 2359304 | tf_op jit(solution)/shard_map/ppermute | solution.py:45
  93.4 28.1 %collective-permute-start.24 = (bf16[128,3072]{1,0:T(8,128)(2,1)S(1)}, bf16[128,3072]{1,0:T(8,128)(2,1)}, u32[]{:S(2)}, u32[]{:S(2)}) collective-permute-start(bf16[128,3072]{1,0:T(8,128)(2,1)S(1)} %collective-permute-done.23.refs_2_.refs_11_), channel_id=1, source_target_pairs={{0,4},{4,8},{8,12},{12,0},{16,20},{20,24},{24,28},{28,16},{32,36},... | collective-permute-start | bytes 2359304 | tf_op jit(solution)/shard_map/ppermute | solution.py:45
  94.5 19.6 %collective-permute-start.29 = (bf16[64,3072]{1,0:T(8,128)(2,1)S(1)}, bf16[64,3072]{1,0:T(8,128)(2,1)}, u32[]{:S(2)}, u32[]{:S(2)}) collective-permute-start(bf16[64,3072]{1,0:T(8,128)(2,1)S(1)} %copy-done.18), channel_id=1, source_target_pairs={{0,4},{4,8},{8,12},{12,0},{16,20},{20,24},{24,28},{28,16},{32,36},... | collective-permute-start | bytes 1179656 | tf_op jit(solution)/shard_map/ppermute | solution.py:45
  94.5 23.8 %collective-permute-start.26 = (bf16[64,3072]{1,0:T(8,128)(2,1)S(1)}, bf16[64,3072]{1,0:T(8,128)(2,1)}, u32[]{:S(2)}, u32[]{:S(2)}) collective-permute-start(bf16[64,3072]{1,0:T(8,128)(2,1)S(1)} %copy-done.20), channel_id=1, source_target_pairs={{0,4},{4,8},{8,12},{12,0},{16,20},{20,24},{24,28},{28,16},{32,36},... | collective-permute-start | bytes 1179656 | tf_op jit(solution)/shard_map/ppermute | solution.py:45
  94.8 52.0 %collective-permute-start.13 = (bf16[128,3072]{1,0:T(8,128)(2,1)}, bf16[128,3072]{1,0:T(8,128)(2,1)}, u32[]{:S(2)}, u32[]{:S(2)}) collective-permute-start(bf16[128,3072]{1,0:T(8,128)(2,1)} %collective-permute-done.12.refs_2_.refs_3_), channel_id=1, source_target_pairs={{0,4},{4,8},{8,12},{12,0},{16,20},{20,24},{24,28},{28,16},{32,36},... | collective-permute-start | bytes 2359304 | tf_op jit(solution)/shard_map/ppermute | solution.py:45
  101.5 45.4 %collective-permute-start.10 = (bf16[128,3072]{1,0:T(8,128)(2,1)}, bf16[128,3072]{1,0:T(8,128)(2,1)}, u32[]{:S(2)}, u32[]{:S(2)}) collective-permute-start(bf16[128,3072]{1,0:T(8,128)(2,1)} %collective-permute-done.9.refs_2_.refs_3_), channel_id=1, source_target_pairs={{0,4},{4,8},{8,12},{12,0},{16,20},{20,24},{24,28},{28,16},{32,36},... | collective-permute-start | bytes 2359304 | tf_op jit(solution)/shard_map/ppermute | solution.py:45
  114.1 25.4 %collective-permute-start.30 = (bf16[64,3072]{1,0:T(8,128)(2,1)}, bf16[64,3072]{1,0:T(8,128)(2,1)}, u32[]{:S(2)}, u32[]{:S(2)}) collective-permute-start(bf16[64,3072]{1,0:T(8,128)(2,1)} %collective-permute-done.29.refs_2_.refs_3_), channel_id=1, source_target_pairs={{0,4},{4,8},{8,12},{12,0},{16,20},{20,24},{24,28},{28,16},{32,36},... | collective-permute-start | bytes 1179656 | tf_op jit(solution)/shard_map/ppermute | solution.py:45
  118.3 25.4 %collective-permute-start.27 = (bf16[64,3072]{1,0:T(8,128)(2,1)}, bf16[64,3072]{1,0:T(8,128)(2,1)}, u32[]{:S(2)}, u32[]{:S(2)}) collective-permute-start(bf16[64,3072]{1,0:T(8,128)(2,1)} %collective-permute-done.26.refs_2_.refs_7_), channel_id=1, source_target_pairs={{0,4},{4,8},{8,12},{12,0},{16,20},{20,24},{24,28},{28,16},{32,36},... | collective-permute-start | bytes 1179656 | tf_op jit(solution)/shard_map/ppermute | solution.py:45
  121.5 39.0 %collective-permute-start.25 = (bf16[128,3072]{1,0:T(8,128)(2,1)}, bf16[128,3072]{1,0:T(8,128)(2,1)}, u32[]{:S(2)}, u32[]{:S(2)}) collective-permute-start(bf16[128,3072]{1,0:T(8,128)(2,1)} %collective-permute-done.24.refs_3_.refs_12_), channel_id=1, source_target_pairs={{0,4},{4,8},{8,12},{12,0},{16,20},{20,24},{24,28},{28,16},{32,36},... | collective-permute-start | bytes 2359304 | tf_op jit(solution)/shard_map/ppermute | solution.py:45
  121.8 38.7 %copy-start.6 = (bf16[128,3072]{1,0:T(8,128)(2,1)S(1)}, bf16[128,3072]{1,0:T(8,128)(2,1)}, u32[]{:S(2)}) copy-start(bf16[128,3072]{1,0:T(8,128)(2,1)} %copy-done.5) | copy-start | bytes 2359300
  121.9 38.7 %copy-start.12 = (bf16[128,3072]{1,0:T(8,128)(2,1)S(1)}, bf16[128,3072]{1,0:T(8,128)(2,1)}, u32[]{:S(2)}) copy-start(bf16[128,3072]{1,0:T(8,128)(2,1)} %copy-done.11) | copy-start | bytes 2359300
  121.9 38.7 %copy-start.21 = (bf16[64,3072]{1,0:T(8,128)(2,1)S(1)}, bf16[64,3072]{1,0:T(8,128)(2,1)}, u32[]{:S(2)}) copy-start(bf16[64,3072]{1,0:T(8,128)(2,1)} %copy-done.19) | copy-start | bytes 1179652
  139.5 16.9 %collective-permute-start.31 = (bf16[64,3072]{1,0:T(8,128)(2,1)}, bf16[64,3072]{1,0:T(8,128)(2,1)S(1)}, u32[]{:S(2)}, u32[]{:S(2)}) collective-permute-start(bf16[64,3072]{1,0:T(8,128)(2,1)} %collective-permute-done.30.refs_3_.refs_4_), channel_id=1, source_target_pairs={{0,4},{4,8},{8,12},{12,0},{16,20},{20,24},{24,28},{28,16},{32,36},... | collective-permute-start | bytes 1179656 | tf_op jit(solution)/shard_map/ppermute | solution.py:45
  143.7 16.9 %collective-permute-start.28 = (bf16[64,3072]{1,0:T(8,128)(2,1)}, bf16[64,3072]{1,0:T(8,128)(2,1)S(1)}, u32[]{:S(2)}, u32[]{:S(2)}) collective-permute-start(bf16[64,3072]{1,0:T(8,128)(2,1)} %collective-permute-done.27.refs_3_.refs_8_), channel_id=1, source_target_pairs={{0,4},{4,8},{8,12},{12,0},{16,20},{20,24},{24,28},{28,16},{32,36},... | collective-permute-start | bytes 1179656 | tf_op jit(solution)/shard_map/ppermute | solution.py:45
  146.8 22.2 %collective-permute-start.14 = (bf16[128,3072]{1,0:T(8,128)(2,1)}, bf16[128,3072]{1,0:T(8,128)(2,1)S(1)}, u32[]{:S(2)}, u32[]{:S(2)}) collective-permute-start(bf16[128,3072]{1,0:T(8,128)(2,1)} %collective-permute-done.13.refs_3_.refs_4_), channel_id=1, source_target_pairs={{0,4},{4,8},{8,12},{12,0},{16,20},{20,24},{24,28},{28,16},{32,36},... | collective-permute-start | bytes 2359304 | tf_op jit(solution)/shard_map/ppermute | solution.py:45
  146.9 30.6 %collective-permute-start.11 = (bf16[128,3072]{1,0:T(8,128)(2,1)}, bf16[128,3072]{1,0:T(8,128)(2,1)S(1)}, u32[]{:S(2)}, u32[]{:S(2)}) collective-permute-start(bf16[128,3072]{1,0:T(8,128)(2,1)} %collective-permute-done.10.refs_3_.refs_4_), channel_id=1, source_target_pairs={{0,4},{4,8},{8,12},{12,0},{16,20},{20,24},{24,28},{28,16},{32,36},... | collective-permute-start | bytes 2359304 | tf_op jit(solution)/shard_map/ppermute | solution.py:45
  156.3 11.7 %copy-start.23 = (bf16[64,3072]{1,0:T(8,128)(2,1)}, bf16[64,3072]{1,0:T(8,128)(2,1)S(1)}, u32[]{:S(2)}) copy-start(bf16[64,3072]{1,0:T(8,128)(2,1)S(1)} %collective-permute-done.31.refs_4_.refs_5_) | copy-start | bytes 1179652
  160.6 7.5 %copy-start.26 = (bf16[64,3072]{1,0:T(8,128)(2,1)}, bf16[64,3072]{1,0:T(8,128)(2,1)S(1)}, u32[]{:S(2)}) copy-start(bf16[64,3072]{1,0:T(8,128)(2,1)S(1)} %collective-permute-done.28.refs_4_.refs_9_) | copy-start | bytes 1179652
  160.6 8.4 %copy-start = (bf16[2048,512]{1,0:T(8,128)(2,1)S(1)}, bf16[2048,512]{1,0:T(8,128)(2,1)}, u32[]{:S(2)}) copy-start(bf16[2048,512]{1,0:T(8,128)(2,1)} %fusion.4.refs_14_.refs_6_) | copy-start | bytes 6291460
  168.0 9.4 %copy-start.9 = (bf16[128,3072]{1,0:T(8,128)(2,1)S(1)}, bf16[128,3072]{1,0:T(8,128)(2,1)}, u32[]{:S(2)}) copy-start(bf16[128,3072]{1,0:T(8,128)(2,1)} %copy-done.8) | copy-start | bytes 2359300
  177.4 6.9 %copy-start.14 = (bf16[128,3072]{1,0:T(8,128)(2,1)}, bf16[128,3072]{1,0:T(8,128)(2,1)S(1)}, u32[]{:S(2)}) copy-start(bf16[128,3072]{1,0:T(8,128)(2,1)S(1)} %collective-permute-done.11.refs_4_.refs_5_) | copy-start | bytes 2359300
  184.3 62.2 %collective-permute-start.32 = (f32[512,1536]{1,0:T(8,128)}, f32[512,1536]{1,0:T(8,128)}, u32[]{:S(2)}, u32[]{:S(2)}) collective-permute-start(f32[512,1536]{1,0:T(8,128)} %weight_grad_part.11), channel_id=1, source_target_pairs={{0,128},{4,132},{8,136},{12,140},{16,144},{20,148},{24,152},{28,15... | collective-permute-start | bytes 9437192 | tf_op jit(solution)/shard_map/ppermute | solution.py:45
  206.0 7.6 %copy-start.1 = (bf16[2048,512]{1,0:T(8,128)(2,1)S(1)}, bf16[2048,512]{1,0:T(8,128)(2,1)}, u32[]{:S(2)}) copy-start(bf16[2048,512]{1,0:T(8,128)(2,1)} %fusion.4.refs_14_.refs_6_) | copy-start | bytes 6291460
  206.0 7.6 %copy-start.17 = (bf16[128,3072]{1,0:T(8,128)(2,1)S(1)}, bf16[128,3072]{1,0:T(8,128)(2,1)}, u32[]{:S(2)}) copy-start(bf16[128,3072]{1,0:T(8,128)(2,1)} %copy-done.16) | copy-start | bytes 2359300
  (20 other events, 63.4 us)

commit v2 on v0

v2 whole, which is shorter than its diff:
```python
import functools

import jax
import jax.numpy as jnp
from jax import lax
from jax.experimental import pallas as pl
from jax.experimental.pallas import tpu as pltpu
from jax.sharding import PartitionSpec as P

AX = ("dp", "expert", "tensor")
NX, NY, NZ = 4, 4, 4
SLOT = 16
HALF = NX * SLOT
ANY = pl.ANY
VMEM_LIMIT = 62 * 1024 * 1024
PARAMS = pltpu.CompilerParams(vmem_limit_bytes=VMEM_LIMIT)


def chip_perm(fn):
    pairs = []
    for c in range(2):
        for z in range(2 * NZ):
            for x in range(NX):
                for y in range(NY):
                    to = fn(c, x, y, z)
                    if to is not None:
                        pairs.append((flat(c, x, y, z), flat(*to)))
    return pairs


def flat(c, x, y, z):
    x, y, z = x % NX, y % NY, z % (2 * NZ)
    return (c * 2 * NX + (z // NZ) * NX + x) * NY * NZ + y * NZ + z % NZ


X_STEP = [chip_perm(lambda c, x, y, z, k=k: (c, x + k, y, z)) for k in range(NX)]
Y_ON = chip_perm(lambda c, x, y, z: (c, x, y + 1 - 2 * c, z))
Y_BACK = chip_perm(lambda c, x, y, z: (c, x, y - 1 + 2 * c, z))
Z_MIRROR = chip_perm(lambda c, x, y, z: (c, x, y, 2 * NZ - 1 - z))
Z_PAIR = chip_perm(lambda c, x, y, z: (c, x, y, z ^ 1))
Z_MIDDLE = chip_perm(lambda c, x, y, z: (c, x, y, z ^ 3) if z % NZ in (1, 2) else None)
DP_SWAP = chip_perm(lambda c, x, y, z: (1 - c, x, y, z))


def send(a, pairs):
    return lax.ppermute(a, AX, pairs)


def dispatch_kernel(place, cot, scales, ids, *outs):
    tok = cot.shape[0]
    x, zhi = place[0], place[1]
    above = lax.broadcasted_iota(jnp.int32, (tok, tok), 0)
    along = lax.broadcasted_iota(jnp.int32, (tok, tok), 1)
    row = jnp.broadcast_to(ids[...], (tok, tok))
    eye = above == along
    col = jnp.sum(jnp.where(eye, row, 0).astype(jnp.float32), axis=1, keepdims=True)
    col = jnp.broadcast_to(col, (tok, tok)).astype(jnp.int32)
    same = jnp.where((col == row) & (above < along), 1.0, 0.0)
    slot = jnp.sum(same, axis=0, keepdims=True).astype(jnp.int32)
    row = ids[...]
    other = jnp.where((row >> 2) == zhi, 0, SLOT)
    target = ((row - x) & (NX - 1)) * (2 * SLOT) + other + slot
    pick = lax.broadcasted_iota(jnp.int32, (2 * HALF, tok), 0) == target
    pick = jnp.where(pick, 1.0, 0.0).astype(jnp.bfloat16)
    scale = jnp.sum(jnp.where(eye, jnp.broadcast_to(scales[...], (tok, tok)), 0.0), axis=1, keepdims=True)
    scaled = (cot[...].astype(jnp.float32) * scale).astype(jnp.bfloat16)
    out = jnp.dot(pick, scaled, preferred_element_type=jnp.float32).astype(jnp.bfloat16)
    for k, ref in enumerate(outs):
        ref[...] = out[k * 2 * SLOT:(k + 1) * 2 * SLOT]


def dispatch(place, cot, scales, ids):
    tok, width = cot.shape
    block = jax.ShapeDtypeStruct((2 * SLOT, width), jnp.bfloat16)
    vmem = pl.BlockSpec(memory_space=pltpu.VMEM)
    return pl.pallas_call(
        dispatch_kernel,
        out_shape=(block,) * NX,
        in_specs=[pl.BlockSpec(memory_space=pltpu.SMEM)] + [vmem] * 3,
        out_specs=(vmem,) * NX,
        compiler_params=PARAMS,
        name="dispatch",
    )(place, cot, scales, ids.reshape(1, tok))


def assemble_kernel(place, b0, b1, b2, b3, mark, u, v):
    del mark
    x = place[0]
    for k, ref in enumerate((b0, b1, b2, b3)):
        at = pl.multiple_of(((x - k) & (NX - 1)) * SLOT, SLOT)
        u[pl.ds(at, SLOT), :] = ref[:SLOT]
        v[pl.ds(at, SLOT), :] = ref[SLOT:]


def assemble(place, blocks, mark):
    vmem = pl.BlockSpec(memory_space=pltpu.VMEM)
    return pl.pallas_call(
        assemble_kernel,
        out_shape=(jax.ShapeDtypeStruct((HALF, blocks[0].shape[1]), jnp.bfloat16),) * 2,
        in_specs=[pl.BlockSpec(memory_space=pltpu.SMEM)] + [vmem] * NX + [pl.BlockSpec(memory_space=ANY)],
        out_specs=(vmem,) * 2,
        compiler_params=PARAMS,
        name="assemble",
    )(place, *blocks, mark)


def starts_of(sizes):
    at = [0]
    for m in sizes:
        at.append(at[-1] + m)
    return at


COLS = 512


def stage_kernel(counts, sizes, hidden, sums, span, factor, waits, outs, acc, got, *refs):
    n = len(counts)
    refs = list(refs[waits:])

    def take(k, there=True):
        return [refs.pop(0) for _ in range(k)] if there else [None] * k

    first, offs = take(2)
    rows = take(n)
    gate, up = take(2)
    (wt,) = take(1, hidden)
    take(2, outs)
    (acc_in,) = take(1, acc)
    (got_in,) = take(1, got)
    gg, gu = take(2, hidden)
    (sum_out,) = take(1, sums)
    done, rows_s, gate_s, up_s, row_sems, blk_sems = take(6)
    wt_s, gg_s, gu_s, out_sems, w_sem = take(5, hidden)
    hid_t, sum_s, sum_sems = take(3, sums)
    (acc_s,) = take(1, acc)
    (got_s,) = take(1, got)
    total = sum(counts)
    col0 = first[0] * COLS

    blk_copies, out_copies = [], []
    for b, (at, m) in enumerate(zip(starts_of(sizes), sizes)):
        here = pl.ds(at, m)
        there = pl.ds(pl.multiple_of(offs[b], SLOT), m)
        for k, (src, dst) in enumerate(((gate, gate_s), (up, up_s))):
            blk_copies.append((at, pltpu.make_async_copy(src.at[there], dst.at[here], blk_sems.at[k, b])))
            blk_copies[-1][1].start()
        if hidden:
            for k, (src, dst) in enumerate(((gg_s, gg), (gu_s, gu))):
                out_copies.append((at, pltpu.make_async_copy(src.at[here], dst.at[there], out_sems.at[k, b])))
    if hidden:
        w_copy = pltpu.make_async_copy(wt, wt_s, w_sem.at[0])
        w_copy.start()
    row_copies = []
    for i, (at, m) in enumerate(zip(starts_of(counts), counts)):
        src = rows[i]
        if not hidden:
            src = src.at[:, pl.ds(pl.multiple_of(col0, COLS), span * COLS)]
        row_copies.append((at, pltpu.make_async_copy(src, rows_s.at[pl.ds(at, m)], row_sems.at[i])))
        row_copies[-1][1].start()
    acc_copies, got_copies = [], []
    for j in range(span):
        if acc:
            there = pl.ds(pl.multiple_of(col0 + j * COLS, COLS), COLS)
            acc_copies.append(pltpu.make_async_copy(acc_in.at[:, there], acc_s.at[j], sum_sems.at[0, j]))
            acc_copies[-1].start()
        if got:
            there = pl.ds(j * COLS, COLS)
            got_copies.append(pltpu.make_async_copy(got_in.at[:, there], got_s.at[j], sum_sems.at[2, j]))
            got_copies[-1].start()

    def arrived(copies, end):
        for at, c in copies:
            if at < end:
                c.wait()
        return [(at, c) for at, c in copies if at >= end]

    for begin in range(0, total, 256):
        end = min(begin + 256, total)
        here = pl.ds(begin, end - begin)
        blk_copies = arrived(blk_copies, end)
        g = gate_s[here, :].astype(jnp.float32)
        u = up_s[here, :].astype(jnp.float32)
        sig = jax.nn.sigmoid(g)
        silu = g * sig
        if sums:
            hid_t[:, here] = (silu * u).astype(jnp.bfloat16).T
        if hidden and begin == 0:
            w_copy.wait()
        row_copies = arrived(row_copies, end)
        if hidden:
            grad = jnp.dot(rows_s[here, :], wt_s[...], preferred_element_type=jnp.float32)
            gg_s[here, :] = (grad * u * sig * (1.0 + g * (1.0 - sig))).astype(jnp.bfloat16)
            gu_s[here, :] = (grad * silu).astype(jnp.bfloat16)
            for at, c in out_copies:
                if begin <= at < end:
                    c.start()
    sum_copies = []
    for j in range(span if sums else 0):
        part = jnp.dot(hid_t[...], rows_s[:, pl.ds(j * COLS, COLS)], preferred_element_type=jnp.float32)
        if acc:
            acc_copies[j].wait()
            part = acc_s[j] + part
        if got:
            got_copies[j].wait()
            part = part + got_s[j].astype(jnp.float32)
        if factor:
            part = part * factor
        sum_s[j] = part.astype(sum_s.dtype)
        sum_copies.append(
            pltpu.make_async_copy(sum_s.at[j], sum_out.at[:, pl.ds(j * COLS, COLS)], sum_sems.at[1, j])
        )
        sum_copies[-1].start()
    done[0] = 0
    for c in sum_copies + [c for _, c in out_copies]:
        c.wait()


def stage(parts, gate, up, wt=None, outs=None, sums=None, acc=None, got=None, first=None, factor=None, marks=()):
    rows = [p[0] for p in parts]
    sizes = tuple(m for p in parts for m, _ in p[1])
    offs = jnp.stack([at for p in parts for _, at in p[1]]).astype(jnp.int32)
    counts = tuple(r.shape[0] for r in rows)
    total, width, units = sum(counts), rows[0].shape[1], gate.shape[1]
    span = width // COLS // (1 if first is None else 2)
    first = jnp.zeros((1,), jnp.int32) if first is None else first
    hidden = wt is not None
    n, waits = len(rows), len(marks)
    smem, any_ = pl.BlockSpec(memory_space=pltpu.SMEM), pl.BlockSpec(memory_space=ANY)
    args = [*marks, first, offs, *rows, gate, up]
    out_shape = [jax.ShapeDtypeStruct((1,), jnp.int32)]
    out_specs = [smem]
    scratch = [
        pltpu.VMEM((total, width if hidden else span * COLS), jnp.bfloat16),
        pltpu.VMEM((total, units), jnp.bfloat16),
        pltpu.VMEM((total, units), jnp.bfloat16),
        pltpu.SemaphoreType.DMA((n,)),
        pltpu.SemaphoreType.DMA((2, len(sizes))),
    ]
    if sums is not None:
        out_shape = [jax.ShapeDtypeStruct((units, span * COLS), sums)] + out_shape
        out_specs = [any_] + out_specs
    aliases = {}
    if hidden:
        args.append(wt)
        out_shape = [jax.ShapeDtypeStruct(gate.shape, jnp.bfloat16)] * 2 + out_shape
        out_specs = [any_] * 2 + out_specs
        if outs is not None:
            aliases = {len(args): 0, len(args) + 1: 1}
            args += list(outs)
        scratch += [
            pltpu.VMEM((width, units), jnp.bfloat16),
            pltpu.VMEM((total, units), jnp.bfloat16),
            pltpu.VMEM((total, units), jnp.bfloat16),
            pltpu.SemaphoreType.DMA((2, len(sizes))),
            pltpu.SemaphoreType.DMA((1,)),
        ]
    if sums is not None:
        scratch += [
            pltpu.VMEM((units, total), jnp.bfloat16),
            pltpu.VMEM((span, units, COLS), sums),
            pltpu.SemaphoreType.DMA((3, span)),
        ]
    for a in (acc, got):
        if a is not None:
            args.append(a)
            scratch.append(pltpu.VMEM((span, units, COLS), a.dtype))
    moved = sum(a.size * a.dtype.itemsize for a in args[waits + 2:waits + 2 + n]) + 8 * total * units
    moved += 2 * width * units if hidden else 0
    moved += 4 * units * span * COLS if sums is not None else 0
    results = pl.pallas_call(
        functools.partial(
            stage_kernel, counts, sizes, hidden, sums is not None, span, factor, waits,
            outs is not None, acc is not None, got is not None,
        ),
        out_shape=tuple(out_shape),
        in_specs=[smem] * (waits + 2) + [any_] * (len(args) - waits - 2),
        out_specs=tuple(out_specs),
        scratch_shapes=scratch,
        input_output_aliases=aliases,
        compiler_params=PARAMS,
        cost_estimate=pl.CostEstimate(
            flops=2 * total * units * width * (int(hidden) + int(sums is not None)),
            bytes_accessed=moved,
            transcendentals=total * units,
        ),
        name="stage",
    )(*args)
    return results


def after_kernel(*refs):
    del refs


def after(arrays, *marks):
    n = len(arrays)
    return list(pl.pallas_call(
        after_kernel,
        out_shape=tuple(jax.ShapeDtypeStruct(a.shape, a.dtype) for a in arrays),
        in_specs=[pl.BlockSpec(memory_space=pltpu.HBM)] * (n + len(marks)),
        out_specs=(pl.BlockSpec(memory_space=pltpu.HBM),) * n,
        input_output_aliases={i: i for i in range(n)},
        compiler_params=PARAMS,
        cost_estimate=pl.CostEstimate(flops=0, bytes_accessed=0, transcendentals=0),
        name="after",
    )(*arrays, *marks))


def pack_kernel(plan, n, inner, *refs):
    ins, outs, sems = refs[:n], refs[-1 - len(plan):-1], refs[-1]

    def copy(pick):
        copies = []
        for ref, blocks in zip(outs, plan):
            for i, block in enumerate(blocks):
                src, at = block[min(pick, len(block) - 1)]
                src = ins[src].at[pl.ds(at * HALF, HALF)]
                copies.append(pltpu.make_async_copy(src, ref.at[pl.ds(i * HALF, HALF)], sems.at[len(copies)]))
                copies[-1].start()
        for c in copies:
            c.wait()

    @pl.when(inner[0] == 1)
    def _():
        copy(0)

    @pl.when(inner[0] == 0)
    def _():
        copy(1)


def pack(inner, arrays, plan, marks=()):
    width = arrays[0].shape[1]
    return pl.pallas_call(
        functools.partial(pack_kernel, plan, len(arrays)),
        out_shape=tuple(jax.ShapeDtypeStruct((len(b) * HALF, width), jnp.bfloat16) for b in plan),
        in_specs=[pl.BlockSpec(memory_space=pltpu.SMEM)]
        + [pl.BlockSpec(memory_space=ANY)] * (len(arrays) + len(marks)),
        out_specs=(pl.BlockSpec(memory_space=pltpu.VMEM),) * len(plan),
        scratch_shapes=[pltpu.SemaphoreType.DMA((sum(len(b) for b in plan),))],
        compiler_params=PARAMS,
        cost_estimate=pl.CostEstimate(flops=0, bytes_accessed=8 * HALF * width, transcendentals=0),
        name="pack",
    )(inner, *arrays, *marks)


def per_device(cotangent, scales, routes, gate, up, weight):
    dp = lax.axis_index("dp")
    expert = lax.axis_index("expert")
    tensor = lax.axis_index("tensor")
    x, zhi = expert & 3, expert >> 2
    y, z = tensor >> 2, tensor & 3
    gate, up, weight = gate[0, 0], up[0, 0], weight[0]
    inner = ((z == 1) | (z == 2)).astype(jnp.int32).reshape(1)

    wt = weight.T
    place = jnp.stack([x, zhi]).astype(jnp.int32)
    blocks = list(dispatch(place, cotangent[0], scales, routes))
    u_own, v_send = assemble(place, blocks[:1] + [send(blocks[k], X_STEP[k]) for k in range(1, NX)], wt)

    far1 = jnp.where(z < 2, 2, 1)
    far2 = jnp.where(z < 2, 3, 0)

    def blocks_of(items):
        at = []
        for kind, yy, zz in items:
            src, hi = (zz, zhi) if kind == 0 else (NZ - 1 - zz, 1 - zhi)
            at.append((HALF, (yy * NZ + src) * (2 * HALF) + hi * HALF))
        return at

    s = 1 - 2 * dp

    def ring(own, what):
        on = send(own, Y_ON)
        back = send(own, Y_BACK)
        return [
            (a, blocks_of([(kind, yy & 3, zz) for kind, zz in what]))
            for a, yy in ((own, y), (on, y - s), (back, y + s))
        ]

    def pass_on(parts, what, *marks):
        if marks:
            parts[1] = (after([parts[1][0]], *marks)[0], parts[1][1])
        parts.append((send(parts[1][0], Y_ON), blocks_of([(kind, (y - 2 * s) & 3, zz) for kind, zz in what])))

    theirs = ((1 - dp) * 3).astype(jnp.int32).reshape(1)
    mine = (dp * 3).astype(jnp.int32).reshape(1)
    f32 = jnp.float32

    v_own = send(v_send, Z_MIRROR)
    u_near = send(u_own, Z_PAIR)
    u_mid1 = send(u_own, Z_MIDDLE)
    wa = [(0, z)]
    a = ring(u_own, wa)
    pass_on(a, wa)
    b_own, x2 = pack(
        inner, [u_near, v_own, u_mid1],
        ((((0, 0),), ((1, 0),)), (((2, 0),), ((1, 0),))),
        [p[0] for p in a[1:]],
    )
    mid2 = send(b_own, Z_MIDDLE)
    pair2 = send(x2, Z_PAIR)
    wb = [(0, z ^ 1), (1, z)]
    b = ring(b_own, wb)
    *outs, m1 = stage(a, gate, up, wt)
    c_own, v_near = pack(
        inner, [x2, pair2],
        ((((0, 0), (1, 0)), ((1, 1),)), (((1, 1),),)),
        [m1] + [p[0] for p in b[1:]],
    )
    mid3 = send(v_near, Z_MIDDLE)
    pair3 = send(mid2, Z_PAIR)
    pass_on(b, wb)
    wc = [(0, far1), (1, z ^ 1)]
    c = ring(c_own, wc)
    (d_own,) = pack(
        inner, [mid2, pair3],
        ((((0, 0), (1, 0)), ((0, 1), (1, 1))),),
        [p[0] for p in b[3:] + c[1:]],
    )
    pass_on(c, wc)
    wd = [(0, far2), (1, far1)]
    d = ring(d_own, wd)
    pair4 = send(mid3, Z_PAIR)
    *outs, m2 = stage(b, gate, up, wt, outs, marks=(m1,))
    (e_own,) = pack(inner, [mid3, pair4], ((((0, 0), (1, 0)),),), [m2] + [p[0] for p in c[3:]])
    we = [(1, far2)]
    e = ring(e_own, we)
    *outs, m3 = stage(c, gate, up, wt, outs, marks=(m2,))
    pass_on(d, wd, m3)
    acc, m4 = stage(a + b + c, gate, up, sums=f32, marks=(m3,))
    pass_on(e, we, m4)
    *outs, m5 = stage(d[:3] + e[:3], gate, up, wt, outs, marks=(m4,))
    rest = d[:3] + e[:3] + d[3:] + e[3:]
    give, m6 = stage(rest, gate, up, sums=jnp.bfloat16, acc=acc, first=theirs, marks=(m5,))
    got = send(give, DP_SWAP)
    *outs, m7 = stage(rest[6:], gate, up, wt, outs, marks=(m6,))
    n_tok = 2 * 64 * 8 * 16
    factor = 1.0 / n_tok ** 0.5
    weight_grad, _ = stage(
        rest, gate, up, sums=jnp.bfloat16, acc=acc, got=got, first=mine, factor=factor, marks=(m7,)
    )
    return (outs[0][None, None], outs[1][None, None], weight_grad[None])


def solution(mesh):
    in_specs = (
        P("dp", ("expert", "tensor"), None),
        P("dp", ("expert", "tensor")),
        P("dp", ("expert", "tensor"), None),
        P("dp", "expert", None, "tensor"),
        P("dp", "expert", None, "tensor"),
        P("expert", "tensor", None),
    )
    out_specs = (
        P("dp", "expert", None, "tensor"),
        P("dp", "expert", None, "tensor"),
        P("expert", "tensor", "dp"),
    )
    return jax.shard_map(
        per_device, mesh=mesh, in_specs=in_specs, out_specs=out_specs, check_vma=False
    )
```

time: 382 us -> 191 us (0.50)
  waiting for transfers between devices: 303 us -> 43.4 us
  Pallas kernels: 0 us -> 81.4 us
  starting transfers between devices: 0.08 us -> 45.6 us
  matrix products: 28.1 us -> 0 us
  blocking collectives: 28.1 us -> 0 us
  local copies, waits for them, and re-layouts: 0.01 us -> 16 us
  between operations: 14.1 us -> 1.18 us
  other arithmetic: 8.47 us -> 1.96 us
    all_gather x1 -> x0, waiting for transfers between devices: 276 us -> none  [per_device(): rows = lax.all_gather(received, 'tensor', axis=0, tiled=True)]
    pallas_call x0 -> x16, Pallas kernels: none -> 81.4 us  [the longest x8 65.7 us: stage(): pl.pallas_call(functools.partial(stage_kernel, counts, sizes, hidden, sum...]
    ppermute x0 -> x27, starting transfers between devices: none -> 45.6 us  [send(): return lax.ppermute(a, AX, pairs)]
    ppermute x0 -> x27, waiting for transfers between devices: none -> 43.4 us  [send(): return lax.ppermute(a, AX, pairs)]
    dot_general x2 -> x0, matrix products: 28.1 us -> none  [the longest x1 15.3 us: local_grads(): lax.dot_general(rows, weight_local, (((1,), (1,)), ((), ())), preferred_e...]
    all_to_all x1 -> x0, blocking collectives: 28.1 us -> none  [per_device(): lax.all_to_all(send_buf, 'expert', split_axis=0, concat_axis=0, tiled=True)]
    psum x1 -> x0, waiting for transfers between devices: 27.2 us -> none  [per_device(): summed = lax.psum(partial_w, 'dp')]
    unnamed x2 -> x39, local copies, waits for them, and re-layouts: 0.01 us -> 12.8 us
  transfers between devices with their start and end apart: 2 -> 27, of which waited for: 2 -> 8; matrix products, arithmetic and copies ran while one was open for 4% -> 5% of each run, Pallas kernels for 0% -> 30%
where the time goes in v2:
time: 191 us; the launch traced here: 189 us
  Pallas kernels  81.4 us (43%)
  starting transfers between devices  45.6 us (24%)
  waiting for transfers between devices  43.4 us (23%)
  local copies, waits for them, and re-layouts  16 us (8%)
  other arithmetic  1.96 us (1%)
    pallas_call x8, Pallas kernels, stage(): pl.pallas_call(functools.partial(stage_kernel, counts, sizes, hidden, sum...  65.7 us
    ppermute x27, starting transfers between devices, send(): return lax.ppermute(a, AX, pairs)  45.6 us
    ppermute x27, waiting for transfers between devices, send(): return lax.ppermute(a, AX, pairs)  43.4 us
    unnamed x39, local copies, waits for them, and re-layouts  12.8 us
    pallas_call x4, Pallas kernels, pack(): pl.pallas_call(functools.partial(pack_kernel, plan, len(arrays)), out_sha...  9.83 us
  transfers between devices with their start and end apart: 27, of which 8 were waited for; matrix products, arithmetic and copies ran while one was open for 5% of the time, Pallas kernels for 30%

profile of v2, /device:TPU:1, one launch (start us, length us, event | category | flops | bytes accessed | tf_op | source)
XLA Modules:
  0.0 189.4 jit_solution(11645474107658899454)
XLA Ops:
  1.3 2.3 %dispatch.1 = (bf16[32,3072]{1,0:T(8,128)(2,1)}, bf16[32,3072]{1,0:T(8,128)(2,1)}, bf16[32,3072]{1,0:T(8,128)(2,1)}, bf16[32,3072]{1,0:T(8,128)(2,1)}) custom-call(s32[2]{0:T(128)} %pad_add_fusion.1.place, bf16[64,3072]{1,0:T(8,128)(2,1)} %bitcast.71, f32[1,64]{1,0:T(1,128)} %scales.1, s32[1,64]{1,0:T(1,128)} %bitcast.72), custom_call_target="tpu_custom_call" | custom-call | tf_op jit(solution)/shard_map/dispatch/pallas_call | solution.py:76
  3.6 2.0 %collective-permute-start = (bf16[32,3072]{1,0:T(8,128)(2,1)}, bf16[32,3072]{1,0:T(8,128)(2,1)S(1)}, u32[]{:S(2)}, u32[]{:S(2)}) collective-permute-start(bf16[32,3072]{1,0:T(8,128)(2,1)} %get-tuple-element.34), channel_id=1, source_target_pairs={{0,16},{4,20},{8,24},{12,28},{16,32},{20,36},{24,40},{28,44},{32,4... | collective-permute-start | bytes 589832 | tf_op jit(solution)/shard_map/ppermute | solution.py:46
  5.6 2.4 %collective-permute-start.1 = (bf16[32,3072]{1,0:T(8,128)(2,1)}, bf16[32,3072]{1,0:T(8,128)(2,1)S(1)}, u32[]{:S(2)}, u32[]{:S(2)}) collective-permute-start(bf16[32,3072]{1,0:T(8,128)(2,1)} %get-tuple-element.35), channel_id=1, source_target_pairs={{0,32},{4,36},{8,40},{12,44},{16,48},{20,52},{24,56},{28,60},{32,0... | collective-permute-start | bytes 589832 | tf_op jit(solution)/shard_map/ppermute | solution.py:46
  8.1 1.2 collective-permute-start.2
  9.3 4.6 %copy.19 = bf16[1,512,3072]{1,2,0:T(8,128)(2,1)} copy(bf16[1,512,3072]{2,1,0:T(8,128)(2,1)} %param.11) | data formatting | bytes 6291456 | tf_op args[5]
  13.9 2.9 %collective-permute-done.1.b2 = bf16[32,3072]{1,0:T(8,128)(2,1)S(1)} collective-permute-done((bf16[32,3072]{1,0:T(8,128)(2,1)}, bf16[32,3072]{1,0:T(8,128)(2,1)S(1)}, u32[]{:S(2)}, u32[]{:S(2)}) %collective-permute-start.1) | collective-permute-done | bytes 196640 | tf_op jit(solution)/shard_map/ppermute | solution.py:46
  17.6 2.2 %assemble.1 = (bf16[64,3072]{1,0:T(8,128)(2,1)}, bf16[64,3072]{1,0:T(8,128)(2,1)}) custom-call(s32[2]{0:T(128)} %pad_add_fusion.1.place, bf16[32,3072]{1,0:T(8,128)(2,1)} %get-tuple-element.33.b0, bf16[32,3072]{1,0:T(8,128)(2,1)} %copy-done.16, bf16[32,3072]{1,0:T(8,128)(2,1)} %copy-done.17, bf16[32,3072]{1,0:T(8,128)(2,1)} %copy-done.18, ...), custom_call_target="tpu_custom_call" | custom-call | tf_op jit(solution)/shard_map/assemble/pallas_call | solution.py:97
  19.7 2.8 %collective-permute-start.3 = (bf16[64,3072]{1,0:T(8,128)(2,1)}, bf16[64,3072]{1,0:T(8,128)(2,1)S(1)}, u32[]{:S(2)}, u32[]{:S(2)}) collective-permute-start(bf16[64,3072]{1,0:T(8,128)(2,1)} %get-tuple-element.37.refs_2_.refs_3_), channel_id=1, source_target_pairs={{0,4},{4,8},{8,12},{12,0},{16,20},{20,24},{24,28},{28,16},{32,36},... | collective-permute-start | bytes 1179656 | tf_op jit(solution)/shard_map/ppermute | solution.py:46
  22.5 1.6 collective-permute-start.6
  24.8 4.8 %collective-permute-start.7 = (bf16[64,3072]{1,0:T(8,128)(2,1)}, bf16[64,3072]{1,0:T(8,128)(2,1)S(1)}, u32[]{:S(2)}, u32[]{:S(2)}) collective-permute-start(bf16[64,3072]{1,0:T(8,128)(2,1)} %get-tuple-element.39), channel_id=1, source_target_pairs={{0,67},{4,71},{8,75},{12,79},{16,83},{20,87},{24,91},{28,95},{32,9... | collective-permute-start | bytes 1179656 | tf_op jit(solution)/shard_map/ppermute | solution.py:46
  29.5 3.2 %collective-permute-start.5 = (bf16[64,3072]{1,0:T(8,128)(2,1)S(1)}, bf16[64,3072]{1,0:T(8,128)(2,1)S(1)}, u32[]{:S(2)}, u32[]{:S(2)}) collective-permute-start(bf16[64,3072]{1,0:T(8,128)(2,1)S(1)} %collective-permute-done.3.refs_3_.refs_4_), channel_id=1, source_target_pairs={{0,4},{4,8},{8,12},{12,0},{16,20},{20,24},{24,28},{28,16},{32,36},... | collective-permute-start | bytes 1179656 | tf_op jit(solution)/shard_map/ppermute | solution.py:46
  32.8 1.5 collective-permute-done.4.refs_4_.refs_5_
  34.3 10.0 %collective-permute-done.7.refs_1_ = bf16[64,3072]{1,0:T(8,128)(2,1)S(1)} collective-permute-done((bf16[64,3072]{1,0:T(8,128)(2,1)}, bf16[64,3072]{1,0:T(8,128)(2,1)S(1)}, u32[]{:S(2)}, u32[]{:S(2)}) %collective-permute-start.7) | collective-permute-done | bytes 393248 | tf_op jit(solution)/shard_map/ppermute | solution.py:46
  44.4 0.7 copy-done.15
  45.8 2.5 %pack.4 = (bf16[128,3072]{1,0:T(8,128)(2,1)}, bf16[128,3072]{1,0:T(8,128)(2,1)}) custom-call(s32[1]{0:T(128)} %bitcast.20.inner, bf16[64,3072]{1,0:T(8,128)(2,1)} %copy-done.13, bf16[64,3072]{1,0:T(8,128)(2,1)} %copy-done.15, bf16[64,3072]{1,0:T(8,128)(2,1)} %copy-done.14, bf16[64,3072]{1,0:T(8,128)(2,1)} %copy-done.8, bf16[64,3072]{1,0:T(8,128)(2,1)} %copy-done.9, ...), custom_call_target="tpu_custom_call" | custom-call | bytes 1572864 | tf_op jit(solution)/shard_map/pack/pallas_call | solution.py:335
  48.5 1.9 %collective-permute-start.12 = (bf16[128,3072]{1,0:T(8,128)(2,1)}, bf16[128,3072]{1,0:T(8,128)(2,1)}, u32[]{:S(2)}, u32[]{:S(2)}) collective-permute-start(bf16[128,3072]{1,0:T(8,128)(2,1)} %get-tuple-element.44.refs_0_), channel_id=1, source_target_pairs={{0,1},{4,5},{8,9},{12,13},{16,17},{20,21},{24,25},{28,29},{32,33},... | collective-permute-start | bytes 2359304 | tf_op jit(solution)/shard_map/ppermute | solution.py:46
  50.4 3.8 %collective-permute-start.9 = (bf16[128,3072]{1,0:T(8,128)(2,1)}, bf16[128,3072]{1,0:T(8,128)(2,1)S(1)}, u32[]{:S(2)}, u32[]{:S(2)}) collective-permute-start(bf16[128,3072]{1,0:T(8,128)(2,1)} %get-tuple-element.40.refs_3_.refs_7_), channel_id=1, source_target_pairs={{0,4},{4,8},{8,12},{12,0},{16,20},{20,24},{24,28},{28,16},{32,36},... | collective-permute-start | bytes 2359304 | tf_op jit(solution)/shard_map/ppermute | solution.py:46
  54.2 1.6 collective-permute-start.16
  56.5 5.7 %stage.8 = (bf16[2048,512]{1,0:T(8,128)(2,1)}, bf16[2048,512]{1,0:T(8,128)(2,1)}, s32[1]{0:T(128)}) custom-call(s32[1]{0:T(128)} %constant.12.clone.1.refs_0_.refs_1_, s32[4]{0:T(128)} %pad_add_fusion.refs_1_, bf16[64,3072]{1,0:T(8,128)(2,1)} %get-tuple-element.37.refs_2_.refs_3_, bf16[64,3072]{1,0:T(8,128)(2,1)} %copy-done.8, bf16[64,3072]{1,0:T(8,128)(2,1)} %copy-done.9, ...), custom_call_target="tpu_custom_call" | custom-call | flops 805306368 | bytes 5767168 | tf_op jit(solution)/shard_map/stage/pallas_call | solution.py:271
  62.2 1.0 collective-permute-done.10.refs_5_.refs_4_.refs_9_
  63.2 7.5 %collective-permute-done.9.refs_4_.refs_3_.refs_8_ = bf16[128,3072]{1,0:T(8,128)(2,1)S(1)} collective-permute-done((bf16[128,3072]{1,0:T(8,128)(2,1)}, bf16[128,3072]{1,0:T(8,128)(2,1)S(1)}, u32[]{:S(2)}, u32[]{:S(2)}) %collective-permute-start.9) | collective-permute-done | bytes 786464 | tf_op jit(solution)/shard_map/ppermute | solution.py:46
  70.6 0.9 copy-done.7
  71.5 2.9 %pack.5 = (bf16[128,3072]{1,0:T(8,128)(2,1)}, bf16[64,3072]{1,0:T(8,128)(2,1)}) custom-call(s32[1]{0:T(128)} %bitcast.20.inner, bf16[128,3072]{1,0:T(8,128)(2,1)} %get-tuple-element.44.refs_0_, bf16[128,3072]{1,0:T(8,128)(2,1)} %collective-permute-done.12.refs_1_, s32[1]{0:T(128)} %get-tuple-element.38.refs_0_.refs_2_, bf16[128,3072]{1,0:T(8,128)(2,1)} %copy-done.7, ...), custom_call_target="tpu_custom_call" | custom-call | bytes 1572864 | tf_op jit(solution)/shard_map/pack/pallas_call | solution.py:335
  74.5 3.4 %collective-permute-start.13 = (bf16[128,3072]{1,0:T(8,128)(2,1)}, bf16[128,3072]{1,0:T(8,128)(2,1)}, u32[]{:S(2)}, u32[]{:S(2)}) collective-permute-start(bf16[128,3072]{1,0:T(8,128)(2,1)} %get-tuple-element.45.refs_3_.refs_11_), channel_id=1, source_target_pairs={{0,4},{4,8},{8,12},{12,0},{16,20},{20,24},{24,28},{28,16},{32,36},... | collective-permute-start | bytes 2359304 | tf_op jit(solution)/shard_map/ppermute | solution.py:46
  77.8 2.7 %collective-permute-start.11 = (bf16[128,3072]{1,0:T(8,128)(2,1)}, bf16[128,3072]{1,0:T(8,128)(2,1)S(1)}, u32[]{:S(2)}, u32[]{:S(2)}) collective-permute-start(bf16[128,3072]{1,0:T(8,128)(2,1)} %copy-done.7), channel_id=1, source_target_pairs={{0,4},{4,8},{8,12},{12,0},{16,20},{20,24},{24,28},{28,16},{32,36},... | collective-permute-start | bytes 2359304 | tf_op jit(solution)/shard_map/ppermute | solution.py:46
  81.2 11.7 %collective-permute-done.13.refs_4_.refs_12_.refs_3_ = bf16[128,3072]{1,0:T(8,128)(2,1)} collective-permute-done((bf16[128,3072]{1,0:T(8,128)(2,1)}, bf16[128,3072]{1,0:T(8,128)(2,1)}, u32[]{:S(2)}, u32[]{:S(2)}) %collective-permute-start.13) | collective-permute-done | bytes 786464 | tf_op jit(solution)/shard_map/ppermute | solution.py:46
  92.9 3.3 %collective-permute-start.15 = (bf16[128,3072]{1,0:T(8,128)(2,1)}, bf16[128,3072]{1,0:T(8,128)(2,1)}, u32[]{:S(2)}, u32[]{:S(2)}) collective-permute-start(bf16[128,3072]{1,0:T(8,128)(2,1)} %collective-permute-done.13.refs_4_.refs_12_.refs_3_), channel_id=1, source_target_pairs={{0,4},{4,8},{8,12},{12,0},{16,20},{20,24},{24,28},{28,16},{32,36},... | collective-permute-start | bytes 2359304 | tf_op jit(solution)/shard_map/ppermute | solution.py:46
  96.2 7.7 %collective-permute-done.11.refs_6_.refs_10_.refs_2_ = bf16[128,3072]{1,0:T(8,128)(2,1)S(1)} collective-permute-done((bf16[128,3072]{1,0:T(8,128)(2,1)}, bf16[128,3072]{1,0:T(8,128)(2,1)S(1)}, u32[]{:S(2)}, u32[]{:S(2)}) %collective-permute-start.11) | collective-permute-done | bytes 786464 | tf_op jit(solution)/shard_map/ppermute | solution.py:46
  104.0 0.9 copy-done.5
  105.1 2.0 %pack.6.refs_3_ = bf16[128,3072]{1,0:T(8,128)(2,1)} custom-call(s32[1]{0:T(128)} %bitcast.20.inner, bf16[128,3072]{1,0:T(8,128)(2,1)} %collective-permute-done.16.refs_0_, bf16[128,3072]{1,0:T(8,128)(2,1)} %collective-permute-done.17.refs_1_, bf16[128,3072]{1,0:T(8,128)(2,1)} %copy-done.5, ...), custom_call_target="tpu_custom_call" | custom-call | bytes 1572864 | tf_op jit(solution)/shard_map/pack/pallas_call | solution.py:335
  107.1 3.1 %collective-permute-start.18 = (bf16[128,3072]{1,0:T(8,128)(2,1)}, bf16[128,3072]{1,0:T(8,128)(2,1)S(1)}, u32[]{:S(2)}, u32[]{:S(2)}) collective-permute-start(bf16[128,3072]{1,0:T(8,128)(2,1)} %pack.6.refs_3_), channel_id=1, source_target_pairs={{0,4},{4,8},{8,12},{12,0},{16,20},{20,24},{24,28},{28,16},{32,36},... | collective-permute-start | bytes 2359304 | tf_op jit(solution)/shard_map/ppermute | solution.py:46
  111.6 8.2 %stage.9 = (bf16[2048,512]{1,0:T(8,128)(2,1)}, bf16[2048,512]{1,0:T(8,128)(2,1)}, s32[1]{0:T(128)}) custom-call(s32[1]{0:T(128)} %get-tuple-element.38.refs_0_.refs_2_, s32[1]{0:T(128)} %constant.12.clone.1.refs_0_.refs_1_, s32[8]{0:T(128)} %stack.187.refs_2_, ...), custom_call_target="tpu_custom_call", output_to_operand_aliasing={{0}: (10, {}), {1}: (11, {})} | custom-call | flops 1610612736 | bytes 8388608 | tf_op jit(solution)/shard_map/stage/pallas_call | solution.py:271
  119.8 1.0 collective-permute-done.21.refs_1_
  120.8 2.3 %pack.7.refs_6_ = bf16[64,3072]{1,0:T(8,128)(2,1)} custom-call(s32[1]{0:T(128)} %bitcast.20.inner, bf16[64,3072]{1,0:T(8,128)(2,1)} %copy-done.12, bf16[64,3072]{1,0:T(8,128)(2,1)} %collective-permute-done.21.refs_1_, s32[1]{0:T(128)} %get-tuple-element.43.refs_0_.refs_2_, bf16[128,3072]{1,0:T(8,128)(2,1)} %collective-permute-done.15.refs_6_.refs_14_.refs_3_), custom_call_target="tpu_custom_call" | custom-call | bytes 1572864 | tf_op jit(solution)/shard_map/pack/pallas_call | solution.py:335
  123.1 1.8 collective-permute-start.22
  124.9 8.2 %stage.10 = (bf16[2048,512]{1,0:T(8,128)(2,1)}, bf16[2048,512]{1,0:T(8,128)(2,1)}, s32[1]{0:T(128)}) custom-call(s32[1]{0:T(128)} %get-tuple-element.43.refs_0_.refs_2_, s32[1]{0:T(128)} %constant.12.clone.1.refs_0_.refs_1_, s32[8]{0:T(128)} %stack.196.refs_2_, ...), custom_call_target="tpu_custom_call", output_to_operand_aliasing={{0}: (10, {}), {1}: (11, {})} | custom-call | flops 1610612736 | bytes 8388608 | tf_op jit(solution)/shard_map/stage/pallas_call | solution.py:271
  133.1 0.9 copy-done
  135.5 1.4 collective-permute-start.23
  136.9 11.9 %stage.11 = (f32[512,3072]{1,0:T(8,128)}, s32[1]{0:T(128)}) custom-call(s32[1]{0:T(128)} %get-tuple-element.48.refs_0_.refs_1_, s32[1]{0:T(128)} %constant.12.clone.1.refs_0_.refs_1_, s32[20]{0:T(128)} %stack.197.refs_2_, bf16[64,3072]{1,0:T(8,128)(2,1)} %get-tuple-element.37.refs_2_.refs_3_, bf16[64,3072]{1,0:T(8,128)(2,1)} %copy-done.8, ...), custom_call_target="tpu_custom_call" | custom-call | flops 4026531840 | bytes 19398656 | tf_op jit(solution)/shard_map/stage/pallas_call | solution.py:271
  149.5 1.3 collective-permute-start.25
  152.1 0.9 copy-done.1
  153.0 9.2 %stage.12 = (bf16[2048,512]{1,0:T(8,128)(2,1)}, bf16[2048,512]{1,0:T(8,128)(2,1)}, s32[1]{0:T(128)}) custom-call(s32[1]{0:T(128)} %get-tuple-element.49.refs_1_.refs_0_, s32[1]{0:T(128)} %constant.12.clone.1.refs_0_.refs_1_, s32[9]{0:T(128)} %stack.207.refs_2_, bf16[128,3072]{1,0:T(8,128)(2,1)} %pack.6.refs_3_, ...), custom_call_target="tpu_custom_call", output_to_operand_aliasing={{0}: (12, {}), {1}: (13, {})} | custom-call | flops 1811939328 | bytes 9043968 | tf_op jit(solution)/shard_map/stage/pallas_call | solution.py:271
  162.2 0.9 copy-done.2
  163.1 7.8 %stage.13 = (bf16[512,1536]{1,0:T(8,128)(2,1)}, s32[1]{0:T(128)}) custom-call(s32[1]{0:T(128)} %get-tuple-element.53.refs_0_, s32[1]{0:T(128)} %bitcast.38.refs_1_, s32[12]{0:T(128)} %stack.211.refs_2_, bf16[128,3072]{1,0:T(8,128)(2,1)} %pack.6.refs_3_, bf16[128,3072]{1,0:T(8,128)(2,1)} %after.2.refs_4_, bf16[128,3072]{1,0:T(8,128)(2,1)} %copy-done.1, ...), custom_call_target="tpu_custom_call" | custom-call | flops 2415919104 | bytes 11010048 | tf_op jit(solution)/shard_map/stage/pallas_call | solution.py:271
  170.9 1.7 collective-permute-start.26
  173.2 5.8 %stage.14 = (bf16[2048,512]{1,0:T(8,128)(2,1)}, bf16[2048,512]{1,0:T(8,128)(2,1)}, s32[1]{0:T(128)}) custom-call(s32[1]{0:T(128)} %get-tuple-element.55.refs_0_, s32[1]{0:T(128)} %constant.12.clone.1.refs_0_.refs_1_, s32[3]{0:T(128)} %pad_add_fusion.2.refs_2_, bf16[128,3072]{1,0:T(8,128)(2,1)} %copy-done.2, ...), custom_call_target="tpu_custom_call", output_to_operand_aliasing={{0}: (8, {}), {1}: (9, {})} | custom-call | flops 603979776 | bytes 5111808 | tf_op jit(solution)/shard_map/stage/pallas_call | solution.py:271
  179.0 1.2 copy-done.11
  180.3 9.0 %stage.15 = (bf16[512,1536]{1,0:T(8,128)(2,1)}, s32[1]{0:T(128)}) custom-call(s32[1]{0:T(128)} %get-tuple-element.60.refs_0_, s32[1]{0:T(128)} %bitcast.44.refs_1_, s32[12]{0:T(128)} %stack.211.refs_2_, bf16[128,3072]{1,0:T(8,128)(2,1)} %pack.6.refs_3_, bf16[128,3072]{1,0:T(8,128)(2,1)} %after.2.refs_4_, bf16[128,3072]{1,0:T(8,128)(2,1)} %copy-done.1, ...), custom_call_target="tpu_custom_call" | custom-call | flops 2415919104 | bytes 11010048 | tf_op jit(solution)/shard_map/stage/pallas_call | solution.py:271
  (69 shorter events, 9.9 us)
Async XLA Ops:
  3.6 10.3 %collective-permute-start = (bf16[32,3072]{1,0:T(8,128)(2,1)}, bf16[32,3072]{1,0:T(8,128)(2,1)S(1)}, u32[]{:S(2)}, u32[]{:S(2)}) collective-permute-start(bf16[32,3072]{1,0:T(8,128)(2,1)} %get-tuple-element.34), channel_id=1, source_target_pairs={{0,16},{4,20},{8,24},{12,28},{16,32},{20,36},{24,40},{28,44},{32,4... | collective-permute-start | bytes 589832 | tf_op jit(solution)/shard_map/ppermute | solution.py:46
  5.6 11.2 %collective-permute-start.1 = (bf16[32,3072]{1,0:T(8,128)(2,1)}, bf16[32,3072]{1,0:T(8,128)(2,1)S(1)}, u32[]{:S(2)}, u32[]{:S(2)}) collective-permute-start(bf16[32,3072]{1,0:T(8,128)(2,1)} %get-tuple-element.35), channel_id=1, source_target_pairs={{0,32},{4,36},{8,40},{12,44},{16,48},{20,52},{24,56},{28,60},{32,0... | collective-permute-start | bytes 589832 | tf_op jit(solution)/shard_map/ppermute | solution.py:46
  8.1 8.7 %collective-permute-start.2 = (bf16[32,3072]{1,0:T(8,128)(2,1)}, bf16[32,3072]{1,0:T(8,128)(2,1)S(1)}, u32[]{:S(2)}, u32[]{:S(2)}) collective-permute-start(bf16[32,3072]{1,0:T(8,128)(2,1)} %get-tuple-element.36), channel_id=1, source_target_pairs={{0,48},{4,52},{8,56},{12,60},{16,0},{20,4},{24,8},{28,12},{32,16},... | collective-permute-start | bytes 589832 | tf_op jit(solution)/shard_map/ppermute | solution.py:46
  13.9 2.9 %copy-start.16 = (bf16[32,3072]{1,0:T(8,128)(2,1)}, bf16[32,3072]{1,0:T(8,128)(2,1)S(1)}, u32[]{:S(2)}) copy-start(bf16[32,3072]{1,0:T(8,128)(2,1)S(1)} %collective-permute-done.b1) | copy-start | bytes 589828
  16.8 0.7 copy-start.17
  16.8 0.7 copy-start.18
  19.7 9.8 %collective-permute-start.3 = (bf16[64,3072]{1,0:T(8,128)(2,1)}, bf16[64,3072]{1,0:T(8,128)(2,1)S(1)}, u32[]{:S(2)}, u32[]{:S(2)}) collective-permute-start(bf16[64,3072]{1,0:T(8,128)(2,1)} %get-tuple-element.37.refs_2_.refs_3_), channel_id=1, source_target_pairs={{0,4},{4,8},{8,12},{12,0},{16,20},{20,24},{24,28},{28,16},{32,36},... | collective-permute-start | bytes 1179656 | tf_op jit(solution)/shard_map/ppermute | solution.py:46
  22.5 11.8 %collective-permute-start.4 = (bf16[64,3072]{1,0:T(8,128)(2,1)}, bf16[64,3072]{1,0:T(8,128)(2,1)S(1)}, u32[]{:S(2)}, u32[]{:S(2)}) collective-permute-start(bf16[64,3072]{1,0:T(8,128)(2,1)} %get-tuple-element.37.refs_2_.refs_3_), channel_id=1, source_target_pairs={{0,12},{4,0},{8,4},{12,8},{16,28},{20,16},{24,20},{28,24},{32,44},... | collective-permute-start | bytes 1179656 | tf_op jit(solution)/shard_map/ppermute | solution.py:46
  22.5 11.8 %collective-permute-start.6 = (bf16[64,3072]{1,0:T(8,128)(2,1)}, bf16[64,3072]{1,0:T(8,128)(2,1)S(1)}, u32[]{:S(2)}, u32[]{:S(2)}) collective-permute-start(bf16[64,3072]{1,0:T(8,128)(2,1)} %get-tuple-element.37.refs_2_.refs_3_), channel_id=1, source_target_pairs={{0,1},{4,5},{8,9},{12,13},{16,17},{20,21},{24,25},{28,29},{32,33},... | collective-permute-start | bytes 1179656 | tf_op jit(solution)/shard_map/ppermute | solution.py:46
  24.1 10.2 %collective-permute-start.8 = (bf16[64,3072]{1,0:T(8,128)(2,1)}, bf16[64,3072]{1,0:T(8,128)(2,1)S(1)}, u32[]{:S(2)}, u32[]{:S(2)}) collective-permute-start(bf16[64,3072]{1,0:T(8,128)(2,1)} %get-tuple-element.37.refs_2_.refs_3_), channel_id=1, source_target_pairs={{1,2},{5,6},{9,10},{13,14},{17,18},{21,22},{25,26},{29,30},{33,34}... | collective-permute-start | bytes 1179656 | tf_op jit(solution)/shard_map/ppermute | solution.py:46
  24.8 19.6 %collective-permute-start.7 = (bf16[64,3072]{1,0:T(8,128)(2,1)}, bf16[64,3072]{1,0:T(8,128)(2,1)S(1)}, u32[]{:S(2)}, u32[]{:S(2)}) collective-permute-start(bf16[64,3072]{1,0:T(8,128)(2,1)} %get-tuple-element.39), channel_id=1, source_target_pairs={{0,67},{4,71},{8,75},{12,79},{16,83},{20,87},{24,91},{28,95},{32,9... | collective-permute-start | bytes 1179656 | tf_op jit(solution)/shard_map/ppermute | solution.py:46
  29.5 15.6 %copy-start.8 = (bf16[64,3072]{1,0:T(8,128)(2,1)}, bf16[64,3072]{1,0:T(8,128)(2,1)S(1)}, u32[]{:S(2)}) copy-start(bf16[64,3072]{1,0:T(8,128)(2,1)S(1)} %collective-permute-done.3.refs_3_.refs_4_) | copy-start | bytes 1179652
  29.5 14.8 %collective-permute-start.5 = (bf16[64,3072]{1,0:T(8,128)(2,1)S(1)}, bf16[64,3072]{1,0:T(8,128)(2,1)S(1)}, u32[]{:S(2)}, u32[]{:S(2)}) collective-permute-start(bf16[64,3072]{1,0:T(8,128)(2,1)S(1)} %collective-permute-done.3.refs_3_.refs_4_), channel_id=1, source_target_pairs={{0,4},{4,8},{8,12},{12,0},{16,20},{20,24},{24,28},{28,16},{32,36},... | collective-permute-start | bytes 1179656 | tf_op jit(solution)/shard_map/ppermute | solution.py:46
  34.3 10.8 %copy-start.9 = (bf16[64,3072]{1,0:T(8,128)(2,1)}, bf16[64,3072]{1,0:T(8,128)(2,1)S(1)}, u32[]{:S(2)}) copy-start(bf16[64,3072]{1,0:T(8,128)(2,1)S(1)} %collective-permute-done.4.refs_4_.refs_5_) | copy-start | bytes 1179652
  34.3 10.8 %copy-start.13 = (bf16[64,3072]{1,0:T(8,128)(2,1)}, bf16[64,3072]{1,0:T(8,128)(2,1)S(1)}, u32[]{:S(2)}) copy-start(bf16[64,3072]{1,0:T(8,128)(2,1)S(1)} %collective-permute-done.6.refs_0_) | copy-start | bytes 1179652
  34.3 10.8 %copy-start.14 = (bf16[64,3072]{1,0:T(8,128)(2,1)}, bf16[64,3072]{1,0:T(8,128)(2,1)S(1)}, u32[]{:S(2)}) copy-start(bf16[64,3072]{1,0:T(8,128)(2,1)S(1)} %collective-permute-done.8.refs_2_) | copy-start | bytes 1179652
  44.3 0.7 copy-start.15
  45.1 0.8 copy-start.10
  48.4 14.7 %collective-permute-start.10 = (bf16[128,3072]{1,0:T(8,128)(2,1)}, bf16[128,3072]{1,0:T(8,128)(2,1)S(1)}, u32[]{:S(2)}, u32[]{:S(2)}) collective-permute-start(bf16[128,3072]{1,0:T(8,128)(2,1)} %get-tuple-element.40.refs_3_.refs_7_), channel_id=1, source_target_pairs={{0,12},{4,0},{8,4},{12,8},{16,28},{20,16},{24,20},{28,24},{32,44},... | collective-permute-start | bytes 2359304 | tf_op jit(solution)/shard_map/ppermute | solution.py:46
  48.5 14.7 %collective-permute-start.12 = (bf16[128,3072]{1,0:T(8,128)(2,1)}, bf16[128,3072]{1,0:T(8,128)(2,1)}, u32[]{:S(2)}, u32[]{:S(2)}) collective-permute-start(bf16[128,3072]{1,0:T(8,128)(2,1)} %get-tuple-element.44.refs_0_), channel_id=1, source_target_pairs={{0,1},{4,5},{8,9},{12,13},{16,17},{20,21},{24,25},{28,29},{32,33},... | collective-permute-start | bytes 2359304 | tf_op jit(solution)/shard_map/ppermute | solution.py:46
  50.4 20.2 %collective-permute-start.9 = (bf16[128,3072]{1,0:T(8,128)(2,1)}, bf16[128,3072]{1,0:T(8,128)(2,1)S(1)}, u32[]{:S(2)}, u32[]{:S(2)}) collective-permute-start(bf16[128,3072]{1,0:T(8,128)(2,1)} %get-tuple-element.40.refs_3_.refs_7_), channel_id=1, source_target_pairs={{0,4},{4,8},{8,12},{12,0},{16,20},{20,24},{24,28},{28,16},{32,36},... | collective-permute-start | bytes 2359304 | tf_op jit(solution)/shard_map/ppermute | solution.py:46
  54.2 26.3 %collective-permute-start.16 = (bf16[128,3072]{1,0:T(8,128)(2,1)}, bf16[128,3072]{1,0:T(8,128)(2,1)}, u32[]{:S(2)}, u32[]{:S(2)}) collective-permute-start(bf16[128,3072]{1,0:T(8,128)(2,1)} %get-tuple-element.40.refs_3_.refs_7_), channel_id=1, source_target_pairs={{1,2},{5,6},{9,10},{13,14},{17,18},{21,22},{25,26},{29,30},{33,34}... | collective-permute-start | bytes 2359304 | tf_op jit(solution)/shard_map/ppermute | solution.py:46
  63.2 7.5 %copy-start.6 = (bf16[128,3072]{1,0:T(8,128)(2,1)}, bf16[128,3072]{1,0:T(8,128)(2,1)S(1)}, u32[]{:S(2)}) copy-start(bf16[128,3072]{1,0:T(8,128)(2,1)S(1)} %collective-permute-done.10.refs_5_.refs_4_.refs_9_) | copy-start | bytes 2359300
  70.6 0.9 copy-start.7
  74.5 18.5 %collective-permute-start.13 = (bf16[128,3072]{1,0:T(8,128)(2,1)}, bf16[128,3072]{1,0:T(8,128)(2,1)}, u32[]{:S(2)}, u32[]{:S(2)}) collective-permute-start(bf16[128,3072]{1,0:T(8,128)(2,1)} %get-tuple-element.45.refs_3_.refs_11_), channel_id=1, source_target_pairs={{0,4},{4,8},{8,12},{12,0},{16,20},{20,24},{24,28},{28,16},{32,36},... | collective-permute-start | bytes 2359304 | tf_op jit(solution)/shard_map/ppermute | solution.py:46
  77.8 26.1 %collective-permute-start.14 = (bf16[128,3072]{1,0:T(8,128)(2,1)}, bf16[128,3072]{1,0:T(8,128)(2,1)S(1)}, u32[]{:S(2)}, u32[]{:S(2)}) collective-permute-start(bf16[128,3072]{1,0:T(8,128)(2,1)} %get-tuple-element.45.refs_3_.refs_11_), channel_id=1, source_target_pairs={{0,12},{4,0},{8,4},{12,8},{16,28},{20,16},{24,20},{28,24},{32,44},... | collective-permute-start | bytes 2359304 | tf_op jit(solution)/shard_map/ppermute | solution.py:46
  77.8 26.1 %collective-permute-start.11 = (bf16[128,3072]{1,0:T(8,128)(2,1)}, bf16[128,3072]{1,0:T(8,128)(2,1)S(1)}, u32[]{:S(2)}, u32[]{:S(2)}) collective-permute-start(bf16[128,3072]{1,0:T(8,128)(2,1)} %copy-done.7), channel_id=1, source_target_pairs={{0,4},{4,8},{8,12},{12,0},{16,20},{20,24},{24,28},{28,16},{32,36},... | collective-permute-start | bytes 2359304 | tf_op jit(solution)/shard_map/ppermute | solution.py:46
  80.5 23.4 %collective-permute-start.17 = (bf16[128,3072]{1,0:T(8,128)(2,1)}, bf16[128,3072]{1,0:T(8,128)(2,1)}, u32[]{:S(2)}, u32[]{:S(2)}) collective-permute-start(bf16[128,3072]{1,0:T(8,128)(2,1)} %collective-permute-done.16.refs_0_), channel_id=1, source_target_pairs={{0,1},{4,5},{8,9},{12,13},{16,17},{20,21},{24,25},{28,29},{32,33},... | collective-permute-start | bytes 2359304 | tf_op jit(solution)/shard_map/ppermute | solution.py:46
  80.5 29.7 %collective-permute-start.20 = (bf16[64,3072]{1,0:T(8,128)(2,1)}, bf16[64,3072]{1,0:T(8,128)(2,1)S(1)}, u32[]{:S(2)}, u32[]{:S(2)}) collective-permute-start(bf16[64,3072]{1,0:T(8,128)(2,1)} %get-tuple-element.50), channel_id=1, source_target_pairs={{1,2},{5,6},{9,10},{13,14},{17,18},{21,22},{25,26},{29,30},{33,34}... | collective-permute-start | bytes 1179656 | tf_op jit(solution)/shard_map/ppermute | solution.py:46
  92.9 27.8 %collective-permute-start.15 = (bf16[128,3072]{1,0:T(8,128)(2,1)}, bf16[128,3072]{1,0:T(8,128)(2,1)}, u32[]{:S(2)}, u32[]{:S(2)}) collective-permute-start(bf16[128,3072]{1,0:T(8,128)(2,1)} %collective-permute-done.13.refs_4_.refs_12_.refs_3_), channel_id=1, source_target_pairs={{0,4},{4,8},{8,12},{12,0},{16,20},{20,24},{24,28},{28,16},{32,36},... | collective-permute-start | bytes 2359304 | tf_op jit(solution)/shard_map/ppermute | solution.py:46
  104.0 0.9 copy-start.5
  104.0 1.1 copy-start.4
  107.1 26.0 %collective-permute-start.18 = (bf16[128,3072]{1,0:T(8,128)(2,1)}, bf16[128,3072]{1,0:T(8,128)(2,1)S(1)}, u32[]{:S(2)}, u32[]{:S(2)}) collective-permute-start(bf16[128,3072]{1,0:T(8,128)(2,1)} %pack.6.refs_3_), channel_id=1, source_target_pairs={{0,4},{4,8},{8,12},{12,0},{16,20},{20,24},{24,28},{28,16},{32,36},... | collective-permute-start | bytes 2359304 | tf_op jit(solution)/shard_map/ppermute | solution.py:46
  110.2 9.6 %copy-start.12 = (bf16[64,3072]{1,0:T(8,128)(2,1)}, bf16[64,3072]{1,0:T(8,128)(2,1)S(1)}, u32[]{:S(2)}) copy-start(bf16[64,3072]{1,0:T(8,128)(2,1)S(1)} %collective-permute-done.20.refs_0_) | copy-start | bytes 1179652
  110.2 10.5 %collective-permute-start.21 = (bf16[64,3072]{1,0:T(8,128)(2,1)S(1)}, bf16[64,3072]{1,0:T(8,128)(2,1)}, u32[]{:S(2)}, u32[]{:S(2)}) collective-permute-start(bf16[64,3072]{1,0:T(8,128)(2,1)S(1)} %collective-permute-done.20.refs_0_), channel_id=1, source_target_pairs={{0,1},{4,5},{8,9},{12,13},{16,17},{20,21},{24,25},{28,29},{32,33},... | collective-permute-start | bytes 1179656 | tf_op jit(solution)/shard_map/ppermute | solution.py:46
  111.6 40.5 %collective-permute-start.19 = (bf16[128,3072]{1,0:T(8,128)(2,1)}, bf16[128,3072]{1,0:T(8,128)(2,1)S(1)}, u32[]{:S(2)}, u32[]{:S(2)}) collective-permute-start(bf16[128,3072]{1,0:T(8,128)(2,1)} %pack.6.refs_3_), channel_id=1, source_target_pairs={{0,12},{4,0},{8,4},{12,8},{16,28},{20,16},{24,20},{28,24},{32,44},... | collective-permute-start | bytes 2359304 | tf_op jit(solution)/shard_map/ppermute | solution.py:46
  123.1 25.7 %collective-permute-start.22 = (bf16[64,3072]{1,0:T(8,128)(2,1)}, bf16[64,3072]{1,0:T(8,128)(2,1)}, u32[]{:S(2)}, u32[]{:S(2)}) collective-permute-start(bf16[64,3072]{1,0:T(8,128)(2,1)} %pack.7.refs_6_), channel_id=1, source_target_pairs={{0,4},{4,8},{8,12},{12,0},{16,20},{20,24},{24,28},{28,16},{32,36},... | collective-permute-start | bytes 1179656 | tf_op jit(solution)/shard_map/ppermute | solution.py:46
  124.9 10.6 %copy-start.3 = (bf16[64,3072]{1,0:T(8,128)(2,1)S(1)}, bf16[64,3072]{1,0:T(8,128)(2,1)}, u32[]{:S(2)}) copy-start(bf16[64,3072]{1,0:T(8,128)(2,1)} %pack.7.refs_6_) | copy-start | bytes 1179652
  133.1 0.9 copy-start
  134.7 27.4 %collective-permute-start.24 = (bf16[128,3072]{1,0:T(8,128)(2,1)}, bf16[128,3072]{1,0:T(8,128)(2,1)S(1)}, u32[]{:S(2)}, u32[]{:S(2)}) collective-permute-start(bf16[128,3072]{1,0:T(8,128)(2,1)} %after.2.refs_4_), channel_id=1, source_target_pairs={{0,4},{4,8},{8,12},{12,0},{16,20},{20,24},{24,28},{28,16},{32,36},... | collective-permute-start | bytes 2359304 | tf_op jit(solution)/shard_map/ppermute | solution.py:46
  135.5 16.6 %collective-permute-start.23 = (bf16[64,3072]{1,0:T(8,128)(2,1)S(1)}, bf16[64,3072]{1,0:T(8,128)(2,1)}, u32[]{:S(2)}, u32[]{:S(2)}) collective-permute-start(bf16[64,3072]{1,0:T(8,128)(2,1)S(1)} %copy-done.3), channel_id=1, source_target_pairs={{0,12},{4,0},{8,4},{12,8},{16,28},{20,16},{24,20},{28,24},{32,44},... | collective-permute-start | bytes 1179656 | tf_op jit(solution)/shard_map/ppermute | solution.py:46
  149.5 12.7 %collective-permute-start.25 = (bf16[64,3072]{1,0:T(8,128)(2,1)}, bf16[64,3072]{1,0:T(8,128)(2,1)}, u32[]{:S(2)}, u32[]{:S(2)}) collective-permute-start(bf16[64,3072]{1,0:T(8,128)(2,1)} %after.3.refs_7_), channel_id=1, source_target_pairs={{0,4},{4,8},{8,12},{12,0},{16,20},{20,24},{24,28},{28,16},{32,36},... | collective-permute-start | bytes 1179656 | tf_op jit(solution)/shard_map/ppermute | solution.py:46
  152.1 0.9 copy-start.1
  162.1 0.9 copy-start.2
  170.9 8.2 %collective-permute-start.26 = (bf16[512,1536]{1,0:T(8,128)(2,1)}, bf16[512,1536]{1,0:T(8,128)(2,1)S(1)}, u32[]{:S(2)}, u32[]{:S(2)}) collective-permute-start(bf16[512,1536]{1,0:T(8,128)(2,1)} %get-tuple-element.61), channel_id=1, source_target_pairs={{0,128},{4,132},{8,136},{12,140},{16,144},{20,148},{24,152},{28,15... | collective-permute-start | bytes 4718600 | tf_op jit(solution)/shard_map/ppermute | solution.py:46
  179.0 1.2 copy-start.11

commit v3 on v2

v3 whole, which is shorter than its diff:
```python
import functools

import jax
import jax.numpy as jnp
from jax import lax
from jax.experimental import pallas as pl
from jax.experimental.pallas import tpu as pltpu
from jax.sharding import PartitionSpec as P

AX = ("dp", "expert", "tensor")
NX, NY, NZ = 4, 4, 4
SLOT = 16
HALF = NX * SLOT
ANY = pl.ANY
VMEM_LIMIT = 62 * 1024 * 1024
PARAMS = pltpu.CompilerParams(vmem_limit_bytes=VMEM_LIMIT)


def chip_perm(fn):
    pairs = []
    for c in range(2):
        for z in range(2 * NZ):
            for x in range(NX):
                for y in range(NY):
                    to = fn(c, x, y, z)
                    if to is not None:
                        pairs.append((flat(c, x, y, z), flat(*to)))
    return pairs


def flat(c, x, y, z):
    x, y, z = x % NX, y % NY, z % (2 * NZ)
    return (c * 2 * NX + (z // NZ) * NX + x) * NY * NZ + y * NZ + z % NZ


X_STEP = [chip_perm(lambda c, x, y, z, k=k: (c, x + k, y, z)) for k in range(NX)]
Y_ON = chip_perm(lambda c, x, y, z: (c, x, y + 1 - 2 * c, z))
Y_BACK = chip_perm(lambda c, x, y, z: (c, x, y - 1 + 2 * c, z))
Z_MIRROR = chip_perm(lambda c, x, y, z: (c, x, y, 2 * NZ - 1 - z))
Z_PAIR = chip_perm(lambda c, x, y, z: (c, x, y, z ^ 1))
Z_MIDDLE = chip_perm(lambda c, x, y, z: (c, x, y, z ^ 3) if z % NZ in (1, 2) else None)
DP_SWAP = chip_perm(lambda c, x, y, z: (1 - c, x, y, z))


def send(a, pairs):
    return lax.ppermute(a, AX, pairs)


def dispatch_kernel(place, cot, scales, ids, *outs):
    tok = cot.shape[0]
    x, zhi = place[0], place[1]
    above = lax.broadcasted_iota(jnp.int32, (tok, tok), 0)
    along = lax.broadcasted_iota(jnp.int32, (tok, tok), 1)
    row = jnp.broadcast_to(ids[...], (tok, tok))
    eye = above == along
    col = jnp.sum(jnp.where(eye, row, 0).astype(jnp.float32), axis=1, keepdims=True)
    col = jnp.broadcast_to(col, (tok, tok)).astype(jnp.int32)
    same = jnp.where((col == row) & (above < along), 1.0, 0.0)
    slot = jnp.sum(same, axis=0, keepdims=True).astype(jnp.int32)
    row = ids[...]
    other = jnp.where((row >> 2) == zhi, 0, SLOT)
    target = ((row - x) & (NX - 1)) * (2 * SLOT) + other + slot
    pick = lax.broadcasted_iota(jnp.int32, (2 * HALF, tok), 0) == target
    pick = jnp.where(pick, 1.0, 0.0).astype(jnp.bfloat16)
    scale = jnp.sum(jnp.where(eye, jnp.broadcast_to(scales[...], (tok, tok)), 0.0), axis=1, keepdims=True)
    scaled = (cot[...].astype(jnp.float32) * scale).astype(jnp.bfloat16)
    out = jnp.dot(pick, scaled, preferred_element_type=jnp.float32).astype(jnp.bfloat16)
    for k, ref in enumerate(outs):
        ref[...] = out[k * 2 * SLOT:(k + 1) * 2 * SLOT]


def dispatch(place, cot, scales, ids):
    tok, width = cot.shape
    block = jax.ShapeDtypeStruct((2 * SLOT, width), jnp.bfloat16)
    vmem = pl.BlockSpec(memory_space=pltpu.VMEM)
    return pl.pallas_call(
        dispatch_kernel,
        out_shape=(block,) * NX,
        in_specs=[pl.BlockSpec(memory_space=pltpu.SMEM)] + [vmem] * 3,
        out_specs=(vmem,) * NX,
        compiler_params=PARAMS,
        name="dispatch",
    )(place, cot, scales, ids.reshape(1, tok))


def assemble_kernel(place, b0, b1, b2, b3, mark, u, v1, v2, v_s):
    del mark
    x = place[0]
    for k, ref in enumerate((b0, b1, b2, b3)):
        at = pl.multiple_of(((x - k) & (NX - 1)) * SLOT, SLOT)
        u[pl.ds(at, SLOT), :] = ref[:SLOT]
        v_s[pl.ds(at, SLOT), :] = ref[SLOT:]
    v1[...] = v_s[:HALF // 2]
    v2[...] = v_s[HALF // 2:]


def assemble(place, blocks, mark):
    width = blocks[0].shape[1]
    vmem = pl.BlockSpec(memory_space=pltpu.VMEM)
    return pl.pallas_call(
        assemble_kernel,
        out_shape=tuple(jax.ShapeDtypeStruct((m, width), jnp.bfloat16) for m in (HALF, HALF // 2, HALF // 2)),
        in_specs=[pl.BlockSpec(memory_space=pltpu.SMEM)] + [vmem] * NX + [pl.BlockSpec(memory_space=ANY)],
        out_specs=(vmem,) * 3,
        scratch_shapes=[pltpu.VMEM((HALF, width), jnp.bfloat16)],
        compiler_params=PARAMS,
        name="assemble",
    )(place, *blocks, mark)


def starts_of(sizes):
    at = [0]
    for m in sizes:
        at.append(at[-1] + m)
    return at


COLS = 512
SMEM_SPEC = pl.BlockSpec(memory_space=pltpu.SMEM)
ANY_SPEC = pl.BlockSpec(memory_space=ANY)
MARK = jax.ShapeDtypeStruct((1,), jnp.int32)


def hidden_kernel(offs, gate, up, hid_t, done, hid_s):
    blocks = hid_t.shape[1] // HALF
    for b in range(0, blocks, 2):
        for i in range(2):
            there = pl.ds(pl.multiple_of(offs[b + i], HALF), HALF)
            g = gate[there, :].astype(jnp.float32)
            u = up[there, :].astype(jnp.float32)
            hid_s[pl.ds(i * HALF, HALF), :] = (g * jax.nn.sigmoid(g) * u).astype(jnp.bfloat16)
        hid_t[:, pl.ds(b * HALF, 2 * HALF)] = hid_s[...].T
    done[0] = 0


def hidden_rows(offs, gate, up):
    slots, units = gate.shape
    vmem = pl.BlockSpec(memory_space=pltpu.VMEM)
    return pl.pallas_call(
        hidden_kernel,
        out_shape=(jax.ShapeDtypeStruct((units, slots), jnp.bfloat16), MARK),
        in_specs=[SMEM_SPEC, vmem, vmem],
        out_specs=(vmem, SMEM_SPEC),
        scratch_shapes=[pltpu.VMEM((2 * HALF, units), jnp.bfloat16)],
        compiler_params=PARAMS,
        cost_estimate=pl.CostEstimate(
            flops=0, bytes_accessed=6 * slots * units, transcendentals=slots * units
        ),
        name="hidden_rows",
    )(offs, gate, up)


def hidden_grad_kernel(counts, ids, waits, outs, *refs):
    n = len(counts)
    refs = list(refs[waits:])

    def take(k, there=True):
        return [refs.pop(0) for _ in range(k)] if there else [None] * k

    (offs,) = take(1)
    rows = take(n)
    gate, up, wt = take(3)
    take(2, outs)
    gg, gu, done, rows_s, wt_s, gate_s, up_s, gg_s, gu_s, row_sems, in_sems, out_sems, w_sem = take(13)
    total = sum(counts)
    in_copies, out_copies = [], []
    for b in range(total // HALF):
        here = pl.ds(b * HALF, HALF)
        there = pl.ds(pl.multiple_of(offs[ids[b]], HALF), HALF)
        for k, (src, dst) in enumerate(((gate, gate_s), (up, up_s))):
            in_copies.append((b * HALF, pltpu.make_async_copy(src.at[there], dst.at[here], in_sems.at[k, b])))
            in_copies[-1][1].start()
        for k, (src, dst) in enumerate(((gg_s, gg), (gu_s, gu))):
            out_copies.append((b * HALF, pltpu.make_async_copy(src.at[here], dst.at[there], out_sems.at[k, b])))
    w_copy = pltpu.make_async_copy(wt, wt_s, w_sem.at[0])
    w_copy.start()
    for i, (at, m) in enumerate(zip(starts_of(counts), counts)):
        in_copies.append((at, pltpu.make_async_copy(rows[i], rows_s.at[pl.ds(at, m)], row_sems.at[i])))
        in_copies[-1][1].start()
    for begin in range(0, total, 256):
        end = min(begin + 256, total)
        here = pl.ds(begin, end - begin)
        for at, c in in_copies:
            if begin <= at < end:
                c.wait()
        if begin == 0:
            w_copy.wait()
        grad = jnp.dot(rows_s[here, :], wt_s[...], preferred_element_type=jnp.float32)
        g = gate_s[here, :].astype(jnp.float32)
        u = up_s[here, :].astype(jnp.float32)
        sig = jax.nn.sigmoid(g)
        gg_s[here, :] = (grad * u * sig * (1.0 + g * (1.0 - sig))).astype(jnp.bfloat16)
        gu_s[here, :] = (grad * (g * sig)).astype(jnp.bfloat16)
        for at, c in out_copies:
            if begin <= at < end:
                c.start()
    done[0] = 0
    for _, c in out_copies:
        c.wait()


def hidden_grads(parts, offs, gate, up, wt, outs, *marks):
    rows = [p[0] for p in parts]
    ids = tuple(i for p in parts for i in p[1])
    counts = tuple(r.shape[0] for r in rows)
    total, n, waits = sum(counts), len(rows), len(marks)
    width, units = wt.shape
    args = [*marks, offs, *rows, gate, up, wt]
    aliases = {}
    if outs:
        aliases = {len(args): 0, len(args) + 1: 1}
        args += list(outs)
    tile = pltpu.VMEM((total, units), jnp.bfloat16)
    *outs, mark = pl.pallas_call(
        functools.partial(hidden_grad_kernel, counts, ids, waits, bool(outs)),
        out_shape=(jax.ShapeDtypeStruct(gate.shape, jnp.bfloat16),) * 2 + (MARK,),
        in_specs=[SMEM_SPEC] * (waits + 1) + [ANY_SPEC] * (len(args) - waits - 1),
        out_specs=(ANY_SPEC, ANY_SPEC, SMEM_SPEC),
        scratch_shapes=[
            pltpu.VMEM((total, width), jnp.bfloat16),
            pltpu.VMEM((width, units), jnp.bfloat16),
            tile, tile, tile, tile,
            pltpu.SemaphoreType.DMA((n,)),
            pltpu.SemaphoreType.DMA((2, total // HALF)),
            pltpu.SemaphoreType.DMA((2, total // HALF)),
            pltpu.SemaphoreType.DMA((1,)),
        ],
        input_output_aliases=aliases,
        compiler_params=PARAMS,
        cost_estimate=pl.CostEstimate(
            flops=2 * total * units * width,
            bytes_accessed=2 * (total * width + width * units + 4 * total * units),
            transcendentals=total * units,
        ),
        name="hidden_grads",
    )(*args)
    return outs, mark


def weight_sum_kernel(counts, lane, span, factor, waits, acc, got, *refs):
    n = len(counts)
    refs = list(refs[waits:])

    def take(k, there=True):
        return [refs.pop(0) for _ in range(k)] if there else [None] * k

    (first,) = take(1)
    rows = take(n)
    (hid,) = take(1)
    (acc_in,) = take(1, acc)
    (got_in,) = take(1, got)
    out, done, rows_s, hid_s, out_s, row_sems, sems = take(7)
    (acc_s,) = take(1, acc)
    (got_s,) = take(1, got)
    total = sum(counts)
    col0 = first[0] * COLS
    in_copies = [pltpu.make_async_copy(hid.at[:, pl.ds(lane, total)], hid_s, sems.at[3, 0])]
    for i, (at, m) in enumerate(zip(starts_of(counts), counts)):
        src = rows[i].at[:, pl.ds(pl.multiple_of(col0, COLS), span * COLS)]
        in_copies.append(pltpu.make_async_copy(src, rows_s.at[pl.ds(at, m)], row_sems.at[i]))
    acc_copies, got_copies, out_copies = [], [], []
    for j in range(span):
        here = pl.ds(j * COLS, COLS)
        if acc:
            there = pl.ds(pl.multiple_of(col0 + j * COLS, COLS), COLS)
            acc_copies.append(pltpu.make_async_copy(acc_in.at[:, there], acc_s.at[j], sems.at[0, j]))
        if got:
            got_copies.append(pltpu.make_async_copy(got_in.at[:, here], got_s.at[j], sems.at[2, j]))
        out_copies.append(pltpu.make_async_copy(out_s.at[j], out.at[:, here], sems.at[1, j]))
    for c in in_copies + acc_copies + got_copies:
        c.start()
    for c in in_copies:
        c.wait()
    for j in range(span):
        part = jnp.dot(hid_s[...], rows_s[:, pl.ds(j * COLS, COLS)], preferred_element_type=jnp.float32)
        if acc:
            acc_copies[j].wait()
            part = acc_s[j] + part
        if got:
            got_copies[j].wait()
            part = part + got_s[j].astype(jnp.float32)
        if factor:
            part = part * factor
        out_s[j] = part.astype(out_s.dtype)
        out_copies[j].start()
    done[0] = 0
    for c in out_copies:
        c.wait()


def weight_sums(parts, hid, lane, kind, *marks, acc=None, got=None, first=None, factor=None):
    rows = [p[0] for p in parts]
    counts = tuple(r.shape[0] for r in rows)
    total, n, waits = sum(counts), len(rows), len(marks)
    units, width = hid.shape[0], rows[0].shape[1]
    span = width // COLS // (1 if first is None else 2)
    first = jnp.zeros((1,), jnp.int32) if first is None else first
    args = [*marks, first, *rows, hid]
    scratch = [
        pltpu.VMEM((total, span * COLS), jnp.bfloat16),
        pltpu.VMEM((units, total), jnp.bfloat16),
        pltpu.VMEM((span, units, COLS), kind),
        pltpu.SemaphoreType.DMA((n,)),
        pltpu.SemaphoreType.DMA((4, span)),
    ]
    for a in (acc, got):
        if a is not None:
            args.append(a)
            scratch.append(pltpu.VMEM((span, units, COLS), a.dtype))
    return pl.pallas_call(
        functools.partial(
            weight_sum_kernel, counts, lane, span, factor, waits, acc is not None, got is not None
        ),
        out_shape=(jax.ShapeDtypeStruct((units, span * COLS), kind), MARK),
        in_specs=[SMEM_SPEC] * (waits + 1) + [ANY_SPEC] * (len(args) - waits - 1),
        out_specs=(ANY_SPEC, SMEM_SPEC),
        scratch_shapes=scratch,
        compiler_params=PARAMS,
        cost_estimate=pl.CostEstimate(
            flops=2 * total * units * span * COLS,
            bytes_accessed=2 * total * (units + span * COLS) + 4 * units * span * COLS,
            transcendentals=0,
        ),
        name="weight_sums",
    )(*args)


def after_kernel(*refs):
    del refs


def after(arrays, *marks):
    n = len(arrays)
    return list(pl.pallas_call(
        after_kernel,
        out_shape=tuple(jax.ShapeDtypeStruct(a.shape, a.dtype) for a in arrays),
        in_specs=[pl.BlockSpec(memory_space=pltpu.HBM)] * (n + len(marks)),
        out_specs=(pl.BlockSpec(memory_space=pltpu.HBM),) * n,
        input_output_aliases={i: i for i in range(n)},
        compiler_params=PARAMS,
        cost_estimate=pl.CostEstimate(flops=0, bytes_accessed=0, transcendentals=0),
        name="after",
    )(*arrays, *marks))


def pack_kernel(plan, n, inner, *refs):
    ins, outs, sems = refs[:n], refs[-1 - len(plan):-1], refs[-1]

    def copy(pick):
        copies = []
        for ref, blocks in zip(outs, plan):
            to = 0
            for m, *choice in blocks:
                src, at = choice[min(pick, len(choice) - 1)]
                src = ins[src].at[pl.ds(at, m)]
                copies.append(pltpu.make_async_copy(src, ref.at[pl.ds(to, m)], sems.at[len(copies)]))
                copies[-1].start()
                to += m
        for c in copies:
            c.wait()

    @pl.when(inner[0] == 1)
    def _():
        copy(0)

    @pl.when(inner[0] == 0)
    def _():
        copy(1)


def pack(inner, arrays, plan, *marks):
    width = arrays[0].shape[1]
    sizes = [sum(b[0] for b in blocks) for blocks in plan]
    return pl.pallas_call(
        functools.partial(pack_kernel, plan, len(arrays)),
        out_shape=tuple(jax.ShapeDtypeStruct((m, width), jnp.bfloat16) for m in sizes),
        in_specs=[SMEM_SPEC] + [ANY_SPEC] * (len(arrays) + len(marks)),
        out_specs=(pl.BlockSpec(memory_space=pltpu.VMEM),) * len(plan),
        scratch_shapes=[pltpu.SemaphoreType.DMA((sum(len(b) for b in plan),))],
        compiler_params=PARAMS,
        cost_estimate=pl.CostEstimate(flops=0, bytes_accessed=4 * sum(sizes) * width, transcendentals=0),
        name="pack",
    )(inner, *arrays, *marks)


def per_device(cotangent, scales, routes, gate, up, weight):
    dp = lax.axis_index("dp")
    expert = lax.axis_index("expert")
    tensor = lax.axis_index("tensor")
    x, zhi = expert & 3, expert >> 2
    y, z = tensor >> 2, tensor & 3
    gate, up, weight = gate[0, 0], up[0, 0], weight[0]
    inner = ((z == 1) | (z == 2)).astype(jnp.int32).reshape(1)

    wt = weight.T
    place = jnp.stack([x, zhi]).astype(jnp.int32)
    blocks = list(dispatch(place, cotangent[0], scales, routes))
    u_own, v1, v2 = assemble(place, blocks[:1] + [send(blocks[k], X_STEP[k]) for k in range(1, NX)], wt)

    far1 = jnp.where(z < 2, 2, 1)
    far2 = jnp.where(z < 2, 3, 0)

    s = 1 - 2 * dp
    wa, wn = [(0, z)], [(0, z ^ 1)]
    wb, wc, wd = [(1, z), (0, far1)], [(1, z ^ 1), (0, far2)], [(1, far1), (1, far2)]
    order = []

    def parts_of(arrays, what, ys):
        parts = []
        for a, yy in zip(arrays, ys):
            ids = []
            for kind, zz in what:
                src, hi = (zz, zhi) if kind == 0 else (NZ - 1 - zz, 1 - zhi)
                ids.append(len(order))
                order.append(((yy & 3) * NZ + src) * (2 * HALF) + hi * HALF)
            parts.append((a, tuple(ids)))
        return parts

    def ring(own):
        return [own, send(own, Y_ON), send(own, Y_BACK)]

    y3, y4 = [y, y - s, y + s], [y - 2 * s]
    theirs = ((1 - dp) * 3).astype(jnp.int32).reshape(1)
    mine = (dp * 3).astype(jnp.int32).reshape(1)

    v1 = send(v1, Z_MIRROR)
    a = ring(u_own)
    u_near = send(u_own, Z_PAIR)
    u_mid1 = send(u_own, Z_MIDDLE)
    u_near, u_mid1 = after([u_near, u_mid1], v1, *a[1:])
    v2 = send(v2, Z_MIRROR)
    n = ring(u_near)
    u_mid2 = send(u_near, Z_MIDDLE)
    u_out1 = send(u_mid1, Z_PAIR)
    an = parts_of(a, wa, y3) + parts_of(n, wn, y3)
    an4 = parts_of([None], wa + wn, y4)
    b3, b4 = parts_of([None] * 3, wb, y3), parts_of([None], wb, y4)
    c3, c4 = parts_of([None] * 3, wc, y3), parts_of([None], wc, y4)
    d3, d4 = parts_of([None] * 3, wd, y3), parts_of([None], wd, y4)
    offs = jnp.stack(order).astype(jnp.int32)

    def fill(parts, arrays):
        return [(a, p[1]) for a, p in zip(arrays, parts)]

    hid, h = hidden_rows(offs, gate, up)
    b_own, x3, v_own, on4 = pack(
        inner, [v1, v2, u_mid1, u_out1, u_mid2, a[1], n[1]],
        (
            ((32, (0, 0)), (32, (1, 0)), (64, (2, 0), (3, 0))),
            ((32, (0, 0)), (32, (1, 0)), (64, (4, 0))),
            ((32, (0, 0)), (32, (1, 0))),
            ((64, (5, 0)), (64, (6, 0))),
        ),
        h, n[2],
    )
    pair3 = send(x3, Z_PAIR)
    mid3 = send(v_own, Z_MIDDLE)
    b = ring(b_own)
    an4 = fill(an4, [send(on4, Y_ON)])
    outs, m1 = hidden_grads(an, offs, gate, up, wt, None)
    c_own, v_near = pack(
        inner, [pair3, x3],
        (((64, (0, 0)), (64, (1, 64), (0, 64))), ((64, (0, 0)),)),
        m1, b[1],
    )
    mid4 = send(v_near, Z_MIDDLE)
    pair4 = send(mid3, Z_PAIR)
    c = ring(c_own)
    b3, b4 = fill(b3, b), fill(b4, [send(b[1], Y_ON)])
    pair5 = send(mid4, Z_PAIR)
    outs, m2 = hidden_grads(an4 + b3, offs, gate, up, wt, outs, m1)
    acc, m3 = weight_sums(an + an4 + b3, hid, 0, jnp.float32, m2)
    (d_own,) = pack(
        inner, [mid3, pair4, mid4, pair5],
        (((64, (0, 0), (1, 0)), (64, (2, 0), (3, 0))),),
        m3, c[1],
    )
    c3, c4 = fill(c3, c), fill(c4, [send(c[1], Y_ON)])
    d = ring(d_own)
    outs, m4 = hidden_grads(b4 + c3, offs, gate, up, wt, outs, m3)
    acc, m5 = weight_sums(b4 + c3, hid, 14 * HALF, jnp.float32, m4, acc=acc)
    d[1], = after([d[1]], m5)
    d3, d4 = fill(d3, d), fill(d4, [send(d[1], Y_ON)])
    outs, m6 = hidden_grads(c4 + d3, offs, gate, up, wt, outs, m5)
    rest, lane = c4 + d3 + d4, 22 * HALF
    give, m7 = weight_sums(rest, hid, lane, jnp.bfloat16, m6, acc=acc, first=theirs)
    got = send(give, DP_SWAP)
    outs, m8 = hidden_grads(d4, offs, gate, up, wt, outs, m7)
    factor = 1.0 / (2 * 64 * 8 * 16) ** 0.5
    weight_grad, _ = weight_sums(
        rest, hid, lane, jnp.bfloat16, m8, acc=acc, got=got, first=mine, factor=factor
    )
    return (outs[0][None, None], outs[1][None, None], weight_grad[None])


def solution(mesh):
    in_specs = (
        P("dp", ("expert", "tensor"), None),
        P("dp", ("expert", "tensor")),
        P("dp", ("expert", "tensor"), None),
        P("dp", "expert", None, "tensor"),
        P("dp", "expert", None, "tensor"),
        P("expert", "tensor", None),
    )
    out_specs = (
        P("dp", "expert", None, "tensor"),
        P("dp", "expert", None, "tensor"),
        P("expert", "tensor", "dp"),
    )
    return jax.shard_map(
        per_device, mesh=mesh, in_specs=in_specs, out_specs=out_specs, check_vma=False
    )
```

time: 191 us -> 179 us (0.937)
  waiting for transfers between devices: 43.4 us -> 26.9 us
  Pallas kernels: 81.4 us -> 88 us
  local copies, waits for them, and re-layouts: 16 us -> 13.8 us
  starting transfers between devices: 45.6 us -> 47.6 us
    ppermute x27 -> x29, waiting for transfers between devices: 43.4 us -> 26.9 us  [send(): return lax.ppermute(a, AX, pairs)]
    pallas_call x9 -> x11, Pallas kernels: 67.9 us -> 75.3 us  [the longest x5 36.7 us: hidden_grads(): pl.pallas_call(functools.partial(hidden_grad_kernel, counts, ids, waits,...]
    another operation x5 -> x1, local copies, waits for them, and re-layouts: 3.24 us -> 0.63 us  [per_device(): offs = jnp.stack(order).astype(jnp.int32)]
    ppermute x27 -> x29, starting transfers between devices: 45.6 us -> 47.6 us  [send(): return lax.ppermute(a, AX, pairs)]
    unnamed x39 -> x47, local copies, waits for them, and re-layouts: 12.8 us -> 13.2 us
    pallas_call x4 -> x3, Pallas kernels: 9.83 us -> 9.78 us  [pack(): pl.pallas_call(functools.partial(pack_kernel, plan, len(arrays)), out_sha...]
  transfers between devices with their start and end apart: 27 -> 29, of which waited for: 8 -> 8; matrix products, arithmetic and copies ran while one was open for 5% -> 3% of each run, Pallas kernels for 30% -> 37%
where the time goes in v3:
time: 179 us; the launch traced here: 178 us
  Pallas kernels  88 us (49%)
  starting transfers between devices  47.6 us (27%)
  waiting for transfers between devices  26.9 us (15%)
  local copies, waits for them, and re-layouts  13.8 us (8%)
    ppermute x29, starting transfers between devices, send(): return lax.ppermute(a, AX, pairs)  47.6 us
    pallas_call x5, Pallas kernels, hidden_grads(): pl.pallas_call(functools.partial(hidden_grad_kernel, counts, ids, waits,...  36.7 us
    pallas_call x4, Pallas kernels, weight_sums(): pl.pallas_call(functools.partial(weight_sum_kernel, counts, lane, span, f...  31.8 us
    ppermute x29, waiting for transfers between devices, send(): return lax.ppermute(a, AX, pairs)  26.9 us
    unnamed x47, local copies, waits for them, and re-layouts  13.2 us
    pallas_call x3, Pallas kernels, pack(): pl.pallas_call(functools.partial(pack_kernel, plan, len(arrays)), out_sha...  9.78 us
    pallas_call x1, Pallas kernels, hidden_rows(): pl.pallas_call(hidden_kernel, out_shape=(jax.ShapeDtypeStruct((units, slo...  4.65 us
  transfers between devices with their start and end apart: 29, of which 8 were waited for; matrix products, arithmetic and copies ran while one was open for 3% of the time, Pallas kernels for 37%

profile of v3, /device:TPU:1, one launch (start us, length us, event | category | flops | bytes accessed | tf_op | source)
XLA Modules:
  0.0 178.2 jit_solution(3260076656639914378)
XLA Ops:
  1.3 2.3 %dispatch.1 = (bf16[32,3072]{1,0:T(8,128)(2,1)}, bf16[32,3072]{1,0:T(8,128)(2,1)}, bf16[32,3072]{1,0:T(8,128)(2,1)}, bf16[32,3072]{1,0:T(8,128)(2,1)}) custom-call(s32[2]{0:T(128)} %pad_add_fusion.place, bf16[64,3072]{1,0:T(8,128)(2,1)} %bitcast.67, f32[1,64]{1,0:T(1,128)} %scales.1, s32[1,64]{1,0:T(1,128)} %bitcast.68), custom_call_target="tpu_custom_call" | custom-call | tf_op jit(solution)/shard_map/dispatch/pallas_call | solution.py:76
  3.6 2.0 %collective-permute-start = (bf16[32,3072]{1,0:T(8,128)(2,1)}, bf16[32,3072]{1,0:T(8,128)(2,1)S(1)}, u32[]{:S(2)}, u32[]{:S(2)}) collective-permute-start(bf16[32,3072]{1,0:T(8,128)(2,1)} %get-tuple-element.43), channel_id=1, source_target_pairs={{0,16},{4,20},{8,24},{12,28},{16,32},{20,36},{24,40},{28,44},{32,4... | collective-permute-start | bytes 589832 | tf_op jit(solution)/shard_map/ppermute | solution.py:46
  5.6 2.5 %collective-permute-start.1 = (bf16[32,3072]{1,0:T(8,128)(2,1)}, bf16[32,3072]{1,0:T(8,128)(2,1)S(1)}, u32[]{:S(2)}, u32[]{:S(2)}) collective-permute-start(bf16[32,3072]{1,0:T(8,128)(2,1)} %get-tuple-element.44), channel_id=1, source_target_pairs={{0,32},{4,36},{8,40},{12,44},{16,48},{20,52},{24,56},{28,60},{32,0... | collective-permute-start | bytes 589832 | tf_op jit(solution)/shard_map/ppermute | solution.py:46
  8.1 1.1 collective-permute-start.2
  9.2 4.7 %copy.20 = bf16[1,512,3072]{1,2,0:T(8,128)(2,1)} copy(bf16[1,512,3072]{2,1,0:T(8,128)(2,1)} %param.11) | data formatting | bytes 6291456 | tf_op args[5]
  13.9 2.9 %collective-permute-done.1.b2 = bf16[32,3072]{1,0:T(8,128)(2,1)S(1)} collective-permute-done((bf16[32,3072]{1,0:T(8,128)(2,1)}, bf16[32,3072]{1,0:T(8,128)(2,1)S(1)}, u32[]{:S(2)}, u32[]{:S(2)}) %collective-permute-start.1) | collective-permute-done | bytes 196640 | tf_op jit(solution)/shard_map/ppermute | solution.py:46
  17.6 2.2 %assemble.1 = (bf16[64,3072]{1,0:T(8,128)(2,1)}, bf16[32,3072]{1,0:T(8,128)(2,1)}, bf16[32,3072]{1,0:T(8,128)(2,1)}) custom-call(s32[2]{0:T(128)} %pad_add_fusion.place, bf16[32,3072]{1,0:T(8,128)(2,1)} %get-tuple-element.42.b0, bf16[32,3072]{1,0:T(8,128)(2,1)} %copy-done.19, bf16[32,3072]{1,0:T(8,128)(2,1)} %copy-done.20, bf16[32,3072]{1,0:T(8,128)(2,1)} %copy-done.21, ...), custom_call_target="tpu_custom_call" | custom-call | tf_op jit(solution)/shard_map/assemble/pallas_call | solution.py:100
  19.7 0.7 collective-permute-start.6
  20.4 4.6 %collective-permute-start.5 = (bf16[64,3072]{1,0:T(8,128)(2,1)}, bf16[64,3072]{1,0:T(8,128)(2,1)S(1)}, u32[]{:S(2)}, u32[]{:S(2)}) collective-permute-start(bf16[64,3072]{1,0:T(8,128)(2,1)} %get-tuple-element.46.refs_1_.refs_2_), channel_id=1, source_target_pairs={{0,1},{4,5},{8,9},{12,13},{16,17},{20,21},{24,25},{28,29},{32,33},... | collective-permute-start | bytes 1179656 | tf_op jit(solution)/shard_map/ppermute | solution.py:46
  25.0 1.3 collective-permute-start.4
  26.3 1.4 collective-permute-start.3
  27.7 3.8 %collective-permute-start.7 = (bf16[32,3072]{1,0:T(8,128)(2,1)}, bf16[32,3072]{1,0:T(8,128)(2,1)S(1)}, u32[]{:S(2)}, u32[]{:S(2)}) collective-permute-start(bf16[32,3072]{1,0:T(8,128)(2,1)} %get-tuple-element.47), channel_id=1, source_target_pairs={{0,67},{4,71},{8,75},{12,79},{16,83},{20,87},{24,91},{28,95},{32,9... | collective-permute-start | bytes 589832 | tf_op jit(solution)/shard_map/ppermute | solution.py:46
  31.5 7.3 %collective-permute-done.7.refs_2_.refs_0_ = bf16[32,3072]{1,0:T(8,128)(2,1)S(1)} collective-permute-done((bf16[32,3072]{1,0:T(8,128)(2,1)}, bf16[32,3072]{1,0:T(8,128)(2,1)S(1)}, u32[]{:S(2)}, u32[]{:S(2)}) %collective-permute-start.7) | collective-permute-done | bytes 196640 | tf_op jit(solution)/shard_map/ppermute | solution.py:46
  39.8 0.8 copy-done.4
  40.6 2.9 %collective-permute-start.11 = (bf16[64,3072]{1,0:T(8,128)(2,1)}, bf16[64,3072]{1,0:T(8,128)(2,1)S(1)}, u32[]{:S(2)}, u32[]{:S(2)}) collective-permute-start(bf16[64,3072]{1,0:T(8,128)(2,1)} %get-tuple-element.51.refs_2_), channel_id=1, source_target_pairs={{0,1},{4,5},{8,9},{12,13},{16,17},{20,21},{24,25},{28,29},{32,33},... | collective-permute-start | bytes 1179656 | tf_op jit(solution)/shard_map/ppermute | solution.py:46
  44.2 1.4 collective-permute-start.9
  45.6 1.5 collective-permute-start.8
  48.2 4.7 %hidden_rows.1 = (bf16[512,2048]{1,0:T(8,128)(2,1)}, s32[1]{0:T(128)}) custom-call(s32[32]{0:T(128)} %stack.140.refs_0_.offs.refs_1_, bf16[2048,512]{1,0:T(8,128)(2,1)} %bitcast.53, bf16[2048,512]{1,0:T(8,128)(2,1)} %bitcast.59), custom_call_target="tpu_custom_call" | custom-call | bytes 6291456 | tf_op jit(solution)/shard_map/hidden_rows/pallas_call | solution.py:139
  53.1 1.9 %collective-permute-done.8.refs_5_.refs_6_ = bf16[64,3072]{1,0:T(8,128)(2,1)S(1)} collective-permute-done((bf16[64,3072]{1,0:T(8,128)(2,1)}, bf16[64,3072]{1,0:T(8,128)(2,1)S(1)}, u32[]{:S(2)}, u32[]{:S(2)}) %collective-permute-start.8) | collective-permute-done | bytes 393248 | tf_op jit(solution)/shard_map/ppermute | solution.py:46
  55.0 0.7 copy-done.8
  55.7 4.1 %pack.3 = (bf16[128,3072]{1,0:T(8,128)(2,1)}, bf16[128,3072]{1,0:T(8,128)(2,1)}, bf16[64,3072]{1,0:T(8,128)(2,1)}, bf16[128,3072]{1,0:T(8,128)(2,1)}) custom-call(s32[1]{0:T(128)} %bitcast.40.inner, bf16[32,3072]{1,0:T(8,128)(2,1)} %copy-done.12, bf16[32,3072]{1,0:T(8,128)(2,1)} %copy-done.22, bf16[64,3072]{1,0:T(8,128)(2,1)} %get-tuple-element.51.refs_2_, ...), custom_call_target="tpu_custom_call" | custom-call | bytes 5505024 | tf_op jit(solution)/shard_map/pack/pallas_call | solution.py:374
  59.9 3.8 %collective-permute-start.17 = (bf16[128,3072]{1,0:T(8,128)(2,1)}, bf16[128,3072]{1,0:T(8,128)(2,1)S(1)}, u32[]{:S(2)}, u32[]{:S(2)}) collective-permute-start(bf16[128,3072]{1,0:T(8,128)(2,1)} %get-tuple-element.60.refs_1_), channel_id=1, source_target_pairs={{0,1},{4,5},{8,9},{12,13},{16,17},{20,21},{24,25},{28,29},{32,33},... | collective-permute-start | bytes 2359304 | tf_op jit(solution)/shard_map/ppermute | solution.py:46
  64.5 1.0 collective-permute-start.15
  66.2 6.7 %hidden_grads.5 = (bf16[2048,512]{1,0:T(8,128)(2,1)}, bf16[2048,512]{1,0:T(8,128)(2,1)}, s32[1]{0:T(128)}) custom-call(s32[32]{0:T(128)} %stack.140.refs_0_.offs.refs_1_, bf16[64,3072]{1,0:T(8,128)(2,1)} %get-tuple-element.46.refs_1_.refs_2_, bf16[64,3072]{1,0:T(8,128)(2,1)} %copy-done.4, bf16[64,3072]{1,0:T(8,128)(2,1)} %copy-done.6, ...), custom_call_target="tpu_custom_call" | custom-call | flops 1207959552 | bytes 7077888 | tf_op jit(solution)/shard_map/hidden_grads/pallas_call | solution.py:214
  72.9 5.1 %collective-permute-done.17.refs_0_ = bf16[128,3072]{1,0:T(8,128)(2,1)S(1)} collective-permute-done((bf16[128,3072]{1,0:T(8,128)(2,1)}, bf16[128,3072]{1,0:T(8,128)(2,1)S(1)}, u32[]{:S(2)}, u32[]{:S(2)}) %collective-permute-start.17) | collective-permute-done | bytes 786464 | tf_op jit(solution)/shard_map/ppermute | solution.py:46
  78.0 0.9 copy-done.13
  79.2 3.0 %pack.4 = (bf16[128,3072]{1,0:T(8,128)(2,1)}, bf16[64,3072]{1,0:T(8,128)(2,1)}) custom-call(s32[1]{0:T(128)} %bitcast.40.inner, bf16[128,3072]{1,0:T(8,128)(2,1)} %copy-done.13, bf16[128,3072]{1,0:T(8,128)(2,1)} %get-tuple-element.60.refs_1_, s32[1]{0:T(128)} %get-tuple-element.49.refs_0_.refs_2_, bf16[128,3072]{1,0:T(8,128)(2,1)} %copy-done.5), custom_call_target="tpu_custom_call" | custom-call | bytes 2359296 | tf_op jit(solution)/shard_map/pack/pallas_call | solution.py:374
  82.2 0.7 collective-permute-start.23
  83.2 5.5 %collective-permute-start.22 = (bf16[64,3072]{1,0:T(8,128)(2,1)S(1)}, bf16[64,3072]{1,0:T(8,128)(2,1)S(1)}, u32[]{:S(2)}, u32[]{:S(2)}) collective-permute-start(bf16[64,3072]{1,0:T(8,128)(2,1)S(1)} %collective-permute-done.21.refs_0_), channel_id=1, source_target_pairs={{0,1},{4,5},{8,9},{12,13},{16,17},{20,21},{24,25},{28,29},{32,33},... | collective-permute-start | bytes 1179656 | tf_op jit(solution)/shard_map/ppermute | solution.py:46
  88.7 3.3 %collective-permute-done.13.refs_2_.refs_8_ = bf16[128,3072]{1,0:T(8,128)(2,1)} collective-permute-done((bf16[128,3072]{1,0:T(8,128)(2,1)}, bf16[128,3072]{1,0:T(8,128)(2,1)}, u32[]{:S(2)}, u32[]{:S(2)}) %collective-permute-start.13) | collective-permute-done | bytes 786464 | tf_op jit(solution)/shard_map/ppermute | solution.py:46
  92.0 2.7 %collective-permute-start.16 = (bf16[128,3072]{1,0:T(8,128)(2,1)}, bf16[128,3072]{1,0:T(8,128)(2,1)}, u32[]{:S(2)}, u32[]{:S(2)}) collective-permute-start(bf16[128,3072]{1,0:T(8,128)(2,1)} %copy-done.5), channel_id=1, source_target_pairs={{0,4},{4,8},{8,12},{12,0},{16,20},{20,24},{24,28},{28,16},{32,36},... | collective-permute-start | bytes 2359304 | tf_op jit(solution)/shard_map/ppermute | solution.py:46
  94.7 8.2 %hidden_grads.6 = (bf16[2048,512]{1,0:T(8,128)(2,1)}, bf16[2048,512]{1,0:T(8,128)(2,1)}, s32[1]{0:T(128)}) custom-call(s32[1]{0:T(128)} %get-tuple-element.49.refs_0_.refs_2_, s32[32]{0:T(128)} %stack.140.refs_0_.offs.refs_1_, bf16[128,3072]{1,0:T(8,128)(2,1)} %collective-permute-done.13.refs_2_.refs_8_, ...), custom_call_target="tpu_custom_call", output_to_operand_aliasing={{0}: (9, {}), {1}: (10, {})} | custom-call | flops 1610612736 | bytes 8388608 | tf_op jit(solution)/shard_map/hidden_grads/pallas_call | solution.py:214
  103.0 8.6 %weight_sums.4 = (f32[512,3072]{1,0:T(8,128)}, s32[1]{0:T(128)}) custom-call(s32[1]{0:T(128)} %get-tuple-element.57.refs_0_, s32[1]{0:T(128)} %constant.29.clone.1.refs_1_, bf16[64,3072]{1,0:T(8,128)(2,1)} %get-tuple-element.46.refs_1_.refs_2_, bf16[64,3072]{1,0:T(8,128)(2,1)} %copy-done.4, bf16[64,3072]{1,0:T(8,128)(2,1)} %copy-done.6, ...), custom_call_target="tpu_custom_call" | custom-call | flops 2818572288 | bytes 12713984 | tf_op jit(solution)/shard_map/weight_sums/pallas_call | solution.py:310
  111.7 0.7 copy-done.18
  112.7 2.7 %pack.5.refs_3_ = bf16[128,3072]{1,0:T(8,128)(2,1)} custom-call(s32[1]{0:T(128)} %bitcast.40.inner, bf16[64,3072]{1,0:T(8,128)(2,1)} %copy-done.16, bf16[64,3072]{1,0:T(8,128)(2,1)} %copy-done.18, bf16[64,3072]{1,0:T(8,128)(2,1)} %copy-done.17, bf16[64,3072]{1,0:T(8,128)(2,1)} %collective-permute-done.24.refs_3_, s32[1]{0:T(128)} %get-tuple-element.59.refs_0_.refs_4_, ...), custom_call_target="tpu_custom_call" | custom-call | bytes 1572864 | tf_op jit(solution)/shard_map/pack/pallas_call | solution.py:374
  115.5 1.3 collective-permute-start.26
  116.9 1.3 collective-permute-start.20
  118.2 8.2 %hidden_grads.7 = (bf16[2048,512]{1,0:T(8,128)(2,1)}, bf16[2048,512]{1,0:T(8,128)(2,1)}, s32[1]{0:T(128)}) custom-call(s32[1]{0:T(128)} %get-tuple-element.59.refs_0_.refs_4_, s32[32]{0:T(128)} %stack.140.refs_0_.offs.refs_1_, bf16[128,3072]{1,0:T(8,128)(2,1)} %collective-permute-done.16.refs_2_, ...), custom_call_target="tpu_custom_call", output_to_operand_aliasing={{0}: (9, {}), {1}: (10, {})} | custom-call | flops 1610612736 | bytes 8388608 | tf_op jit(solution)/shard_map/hidden_grads/pallas_call | solution.py:214
  126.4 9.3 %weight_sums.5 = (f32[512,3072]{1,0:T(8,128)}, s32[1]{0:T(128)}) custom-call(s32[1]{0:T(128)} %get-tuple-element.64.refs_0_, s32[1]{0:T(128)} %constant.29.clone.1.refs_1_, bf16[128,3072]{1,0:T(8,128)(2,1)} %collective-permute-done.16.refs_2_, bf16[128,3072]{1,0:T(8,128)(2,1)} %get-tuple-element.61.refs_3_, bf16[128,3072]{1,0:T(8,128)(2,1)} %copy-done.3, ...), custom_call_target="tpu_custom_call" | custom-call | flops 1610612736 | bytes 9961472 | tf_op jit(solution)/shard_map/weight_sums/pallas_call | solution.py:310
  135.7 0.9 copy-done
  137.6 6.1 %collective-permute-done.20.refs_2_ = bf16[128,3072]{1,0:T(8,128)(2,1)} collective-permute-done((bf16[128,3072]{1,0:T(8,128)(2,1)}, bf16[128,3072]{1,0:T(8,128)(2,1)}, u32[]{:S(2)}, u32[]{:S(2)}) %collective-permute-start.20) | collective-permute-done | bytes 786464 | tf_op jit(solution)/shard_map/ppermute | solution.py:46
  143.7 8.1 %hidden_grads.8 = (bf16[2048,512]{1,0:T(8,128)(2,1)}, bf16[2048,512]{1,0:T(8,128)(2,1)}, s32[1]{0:T(128)}) custom-call(s32[1]{0:T(128)} %get-tuple-element.66.refs_1_.refs_0_, s32[32]{0:T(128)} %stack.140.refs_0_.offs.refs_1_, bf16[128,3072]{1,0:T(8,128)(2,1)} %collective-permute-done.20.refs_2_, ...), custom_call_target="tpu_custom_call", output_to_operand_aliasing={{0}: (9, {}), {1}: (10, {})} | custom-call | flops 1610612736 | bytes 8388608 | tf_op jit(solution)/shard_map/hidden_grads/pallas_call | solution.py:214
  152.0 0.9 copy-done.1
  152.9 6.4 %weight_sums.6 = (bf16[512,1536]{1,0:T(8,128)(2,1)}, s32[1]{0:T(128)}) custom-call(s32[1]{0:T(128)} %get-tuple-element.71.refs_0_, s32[1]{0:T(128)} %bitcast.41.refs_1_, bf16[128,3072]{1,0:T(8,128)(2,1)} %collective-permute-done.20.refs_2_, bf16[128,3072]{1,0:T(8,128)(2,1)} %pack.5.refs_3_, bf16[128,3072]{1,0:T(8,128)(2,1)} %after.3.refs_4_, ...), custom_call_target="tpu_custom_call" | custom-call | flops 1006632960 | bytes 5767168 | tf_op jit(solution)/shard_map/weight_sums/pallas_call | solution.py:310
  159.3 4.5 %collective-permute-start.28 = (bf16[512,1536]{1,0:T(8,128)(2,1)}, bf16[512,1536]{1,0:T(8,128)(2,1)S(1)}, u32[]{:S(2)}, u32[]{:S(2)}) collective-permute-start(bf16[512,1536]{1,0:T(8,128)(2,1)} %get-tuple-element.79), channel_id=1, source_target_pairs={{0,128},{4,132},{8,136},{12,140},{16,144},{20,148},{24,152},{28,15... | collective-permute-start | bytes 4718600 | tf_op jit(solution)/shard_map/ppermute | solution.py:46
  163.8 5.5 %hidden_grads.9 = (bf16[2048,512]{1,0:T(8,128)(2,1)}, bf16[2048,512]{1,0:T(8,128)(2,1)}, s32[1]{0:T(128)}) custom-call(s32[1]{0:T(128)} %get-tuple-element.73.refs_0_, s32[32]{0:T(128)} %stack.140.refs_0_.offs.refs_1_, bf16[128,3072]{1,0:T(8,128)(2,1)} %copy-done.1, bf16[2048,512]{1,0:T(8,128)(2,1)} %bitcast.58, ...), custom_call_target="tpu_custom_call", output_to_operand_aliasing={{0}: (6, {}), {1}: (7, {})} | custom-call | flops 402653184 | bytes 4456448 | tf_op jit(solution)/shard_map/hidden_grads/pallas_call | solution.py:214
  169.3 1.2 copy-done.11
  170.5 7.5 %weight_sums.7 = (bf16[512,1536]{1,0:T(8,128)(2,1)}, s32[1]{0:T(128)}) custom-call(s32[1]{0:T(128)} %get-tuple-element.78.refs_0_, s32[1]{0:T(128)} %bitcast.44.refs_1_, bf16[128,3072]{1,0:T(8,128)(2,1)} %collective-permute-done.20.refs_2_, bf16[128,3072]{1,0:T(8,128)(2,1)} %pack.5.refs_3_, bf16[128,3072]{1,0:T(8,128)(2,1)} %after.3.refs_4_, ...), custom_call_target="tpu_custom_call" | custom-call | flops 1006632960 | bytes 5767168 | tf_op jit(solution)/shard_map/weight_sums/pallas_call | solution.py:310
  (76 shorter events, 8.3 us)
Async XLA Ops:
  3.6 10.3 %collective-permute-start = (bf16[32,3072]{1,0:T(8,128)(2,1)}, bf16[32,3072]{1,0:T(8,128)(2,1)S(1)}, u32[]{:S(2)}, u32[]{:S(2)}) collective-permute-start(bf16[32,3072]{1,0:T(8,128)(2,1)} %get-tuple-element.43), channel_id=1, source_target_pairs={{0,16},{4,20},{8,24},{12,28},{16,32},{20,36},{24,40},{28,44},{32,4... | collective-permute-start | bytes 589832 | tf_op jit(solution)/shard_map/ppermute | solution.py:46
  5.6 11.2 %collective-permute-start.1 = (bf16[32,3072]{1,0:T(8,128)(2,1)}, bf16[32,3072]{1,0:T(8,128)(2,1)S(1)}, u32[]{:S(2)}, u32[]{:S(2)}) collective-permute-start(bf16[32,3072]{1,0:T(8,128)(2,1)} %get-tuple-element.44), channel_id=1, source_target_pairs={{0,32},{4,36},{8,40},{12,44},{16,48},{20,52},{24,56},{28,60},{32,0... | collective-permute-start | bytes 589832 | tf_op jit(solution)/shard_map/ppermute | solution.py:46
  8.1 8.7 %collective-permute-start.2 = (bf16[32,3072]{1,0:T(8,128)(2,1)}, bf16[32,3072]{1,0:T(8,128)(2,1)S(1)}, u32[]{:S(2)}, u32[]{:S(2)}) collective-permute-start(bf16[32,3072]{1,0:T(8,128)(2,1)} %get-tuple-element.45), channel_id=1, source_target_pairs={{0,48},{4,52},{8,56},{12,60},{16,0},{20,4},{24,8},{28,12},{32,16},... | collective-permute-start | bytes 589832 | tf_op jit(solution)/shard_map/ppermute | solution.py:46
  13.9 2.9 %copy-start.19 = (bf16[32,3072]{1,0:T(8,128)(2,1)}, bf16[32,3072]{1,0:T(8,128)(2,1)S(1)}, u32[]{:S(2)}) copy-start(bf16[32,3072]{1,0:T(8,128)(2,1)S(1)} %collective-permute-done.b1) | copy-start | bytes 589828
  19.7 19.0 %collective-permute-start.6 = (bf16[64,3072]{1,0:T(8,128)(2,1)}, bf16[64,3072]{1,0:T(8,128)(2,1)S(1)}, u32[]{:S(2)}, u32[]{:S(2)}) collective-permute-start(bf16[64,3072]{1,0:T(8,128)(2,1)} %get-tuple-element.46.refs_1_.refs_2_), channel_id=1, source_target_pairs={{1,2},{5,6},{9,10},{13,14},{17,18},{21,22},{25,26},{29,30},{33,34}... | collective-permute-start | bytes 1179656 | tf_op jit(solution)/shard_map/ppermute | solution.py:46
  20.4 18.4 %collective-permute-start.5 = (bf16[64,3072]{1,0:T(8,128)(2,1)}, bf16[64,3072]{1,0:T(8,128)(2,1)S(1)}, u32[]{:S(2)}, u32[]{:S(2)}) collective-permute-start(bf16[64,3072]{1,0:T(8,128)(2,1)} %get-tuple-element.46.refs_1_.refs_2_), channel_id=1, source_target_pairs={{0,1},{4,5},{8,9},{12,13},{16,17},{20,21},{24,25},{28,29},{32,33},... | collective-permute-start | bytes 1179656 | tf_op jit(solution)/shard_map/ppermute | solution.py:46
  25.0 13.8 %collective-permute-start.4 = (bf16[64,3072]{1,0:T(8,128)(2,1)}, bf16[64,3072]{1,0:T(8,128)(2,1)S(1)}, u32[]{:S(2)}, u32[]{:S(2)}) collective-permute-start(bf16[64,3072]{1,0:T(8,128)(2,1)} %get-tuple-element.46.refs_1_.refs_2_), channel_id=1, source_target_pairs={{0,12},{4,0},{8,4},{12,8},{16,28},{20,16},{24,20},{28,24},{32,44},... | collective-permute-start | bytes 1179656 | tf_op jit(solution)/shard_map/ppermute | solution.py:46
  26.3 12.5 %collective-permute-start.3 = (bf16[64,3072]{1,0:T(8,128)(2,1)}, bf16[64,3072]{1,0:T(8,128)(2,1)S(1)}, u32[]{:S(2)}, u32[]{:S(2)}) collective-permute-start(bf16[64,3072]{1,0:T(8,128)(2,1)} %get-tuple-element.46.refs_1_.refs_2_), channel_id=1, source_target_pairs={{0,4},{4,8},{8,12},{12,0},{16,20},{20,24},{24,28},{28,16},{32,36},... | collective-permute-start | bytes 1179656 | tf_op jit(solution)/shard_map/ppermute | solution.py:46
  27.7 11.0 %collective-permute-start.7 = (bf16[32,3072]{1,0:T(8,128)(2,1)}, bf16[32,3072]{1,0:T(8,128)(2,1)S(1)}, u32[]{:S(2)}, u32[]{:S(2)}) collective-permute-start(bf16[32,3072]{1,0:T(8,128)(2,1)} %get-tuple-element.47), channel_id=1, source_target_pairs={{0,67},{4,71},{8,75},{12,79},{16,83},{20,87},{24,91},{28,95},{32,9... | collective-permute-start | bytes 589832 | tf_op jit(solution)/shard_map/ppermute | solution.py:46
  38.8 0.8 copy-start.10
  38.8 0.9 copy-start.9
  38.8 1.0 copy-start.6
  39.8 0.8 copy-start.4
  40.6 12.4 %collective-permute-start.11 = (bf16[64,3072]{1,0:T(8,128)(2,1)}, bf16[64,3072]{1,0:T(8,128)(2,1)S(1)}, u32[]{:S(2)}, u32[]{:S(2)}) collective-permute-start(bf16[64,3072]{1,0:T(8,128)(2,1)} %get-tuple-element.51.refs_2_), channel_id=1, source_target_pairs={{0,1},{4,5},{8,9},{12,13},{16,17},{20,21},{24,25},{28,29},{32,33},... | collective-permute-start | bytes 1179656 | tf_op jit(solution)/shard_map/ppermute | solution.py:46
  43.5 9.5 %collective-permute-start.12 = (bf16[64,3072]{1,0:T(8,128)(2,1)}, bf16[64,3072]{1,0:T(8,128)(2,1)S(1)}, u32[]{:S(2)}, u32[]{:S(2)}) collective-permute-start(bf16[64,3072]{1,0:T(8,128)(2,1)} %get-tuple-element.48.refs_4_.refs_5_), channel_id=1, source_target_pairs={{1,2},{5,6},{9,10},{13,14},{17,18},{21,22},{25,26},{29,30},{33,34}... | collective-permute-start | bytes 1179656 | tf_op jit(solution)/shard_map/ppermute | solution.py:46
  44.2 8.9 %collective-permute-start.9 = (bf16[64,3072]{1,0:T(8,128)(2,1)}, bf16[64,3072]{1,0:T(8,128)(2,1)S(1)}, u32[]{:S(2)}, u32[]{:S(2)}) collective-permute-start(bf16[64,3072]{1,0:T(8,128)(2,1)} %get-tuple-element.48.refs_4_.refs_5_), channel_id=1, source_target_pairs={{0,12},{4,0},{8,4},{12,8},{16,28},{20,16},{24,20},{28,24},{32,44},... | collective-permute-start | bytes 1179656 | tf_op jit(solution)/shard_map/ppermute | solution.py:46
  45.6 9.4 %collective-permute-start.8 = (bf16[64,3072]{1,0:T(8,128)(2,1)}, bf16[64,3072]{1,0:T(8,128)(2,1)S(1)}, u32[]{:S(2)}, u32[]{:S(2)}) collective-permute-start(bf16[64,3072]{1,0:T(8,128)(2,1)} %get-tuple-element.48.refs_4_.refs_5_), channel_id=1, source_target_pairs={{0,4},{4,8},{8,12},{12,0},{16,20},{20,24},{24,28},{28,16},{32,36},... | collective-permute-start | bytes 1179656 | tf_op jit(solution)/shard_map/ppermute | solution.py:46
  47.1 5.9 %collective-permute-start.10 = (bf16[32,3072]{1,0:T(8,128)(2,1)}, bf16[32,3072]{1,0:T(8,128)(2,1)S(1)}, u32[]{:S(2)}, u32[]{:S(2)}) collective-permute-start(bf16[32,3072]{1,0:T(8,128)(2,1)} %get-tuple-element.50), channel_id=1, source_target_pairs={{0,67},{4,71},{8,75},{12,79},{16,83},{20,87},{24,91},{28,95},{32,9... | collective-permute-start | bytes 589832 | tf_op jit(solution)/shard_map/ppermute | solution.py:46
  53.1 1.9 %copy-start.22 = (bf16[32,3072]{1,0:T(8,128)(2,1)}, bf16[32,3072]{1,0:T(8,128)(2,1)S(1)}, u32[]{:S(2)}) copy-start(bf16[32,3072]{1,0:T(8,128)(2,1)S(1)} %collective-permute-done.10.refs_1_) | copy-start | bytes 589828
  53.1 1.9 %copy-start.14 = (bf16[64,3072]{1,0:T(8,128)(2,1)}, bf16[64,3072]{1,0:T(8,128)(2,1)S(1)}, u32[]{:S(2)}) copy-start(bf16[64,3072]{1,0:T(8,128)(2,1)S(1)} %collective-permute-done.11.refs_3_) | copy-start | bytes 1179652
  53.1 1.9 %copy-start.15 = (bf16[64,3072]{1,0:T(8,128)(2,1)}, bf16[64,3072]{1,0:T(8,128)(2,1)S(1)}, u32[]{:S(2)}) copy-start(bf16[64,3072]{1,0:T(8,128)(2,1)S(1)} %collective-permute-done.12.refs_4_) | copy-start | bytes 1179652
  53.1 1.9 %copy-start.7 = (bf16[64,3072]{1,0:T(8,128)(2,1)}, bf16[64,3072]{1,0:T(8,128)(2,1)S(1)}, u32[]{:S(2)}) copy-start(bf16[64,3072]{1,0:T(8,128)(2,1)S(1)} %collective-permute-done.9.refs_6_.refs_8_.refs_7_) | copy-start | bytes 1179652
  55.0 0.8 copy-start.8
  59.9 18.1 %collective-permute-start.17 = (bf16[128,3072]{1,0:T(8,128)(2,1)}, bf16[128,3072]{1,0:T(8,128)(2,1)S(1)}, u32[]{:S(2)}, u32[]{:S(2)}) collective-permute-start(bf16[128,3072]{1,0:T(8,128)(2,1)} %get-tuple-element.60.refs_1_), channel_id=1, source_target_pairs={{0,1},{4,5},{8,9},{12,13},{16,17},{20,21},{24,25},{28,29},{32,33},... | collective-permute-start | bytes 2359304 | tf_op jit(solution)/shard_map/ppermute | solution.py:46
  63.6 14.4 %collective-permute-start.14 = (bf16[128,3072]{1,0:T(8,128)(2,1)}, bf16[128,3072]{1,0:T(8,128)(2,1)S(1)}, u32[]{:S(2)}, u32[]{:S(2)}) collective-permute-start(bf16[128,3072]{1,0:T(8,128)(2,1)} %get-tuple-element.54.refs_3_.refs_9_), channel_id=1, source_target_pairs={{0,4},{4,8},{8,12},{12,0},{16,20},{20,24},{24,28},{28,16},{32,36},... | collective-permute-start | bytes 2359304 | tf_op jit(solution)/shard_map/ppermute | solution.py:46
  64.1 27.9 %collective-permute-start.13 = (bf16[128,3072]{1,0:T(8,128)(2,1)}, bf16[128,3072]{1,0:T(8,128)(2,1)}, u32[]{:S(2)}, u32[]{:S(2)}) collective-permute-start(bf16[128,3072]{1,0:T(8,128)(2,1)} %get-tuple-element.53), channel_id=1, source_target_pairs={{0,4},{4,8},{8,12},{12,0},{16,20},{20,24},{24,28},{28,16},{32,36},... | collective-permute-start | bytes 2359304 | tf_op jit(solution)/shard_map/ppermute | solution.py:46
  64.5 27.5 %collective-permute-start.15 = (bf16[128,3072]{1,0:T(8,128)(2,1)}, bf16[128,3072]{1,0:T(8,128)(2,1)}, u32[]{:S(2)}, u32[]{:S(2)}) collective-permute-start(bf16[128,3072]{1,0:T(8,128)(2,1)} %get-tuple-element.54.refs_3_.refs_9_), channel_id=1, source_target_pairs={{0,12},{4,0},{8,4},{12,8},{16,28},{20,16},{24,20},{28,24},{32,44},... | collective-permute-start | bytes 2359304 | tf_op jit(solution)/shard_map/ppermute | solution.py:46
  65.5 17.6 %collective-permute-start.21 = (bf16[64,3072]{1,0:T(8,128)(2,1)}, bf16[64,3072]{1,0:T(8,128)(2,1)S(1)}, u32[]{:S(2)}, u32[]{:S(2)}) collective-permute-start(bf16[64,3072]{1,0:T(8,128)(2,1)} %get-tuple-element.67), channel_id=1, source_target_pairs={{1,2},{5,6},{9,10},{13,14},{17,18},{21,22},{25,26},{29,30},{33,34}... | collective-permute-start | bytes 1179656 | tf_op jit(solution)/shard_map/ppermute | solution.py:46
  78.0 0.9 copy-start.13
  78.0 1.2 copy-start.5
  82.2 12.4 %collective-permute-start.23 = (bf16[64,3072]{1,0:T(8,128)(2,1)}, bf16[64,3072]{1,0:T(8,128)(2,1)S(1)}, u32[]{:S(2)}, u32[]{:S(2)}) collective-permute-start(bf16[64,3072]{1,0:T(8,128)(2,1)} %get-tuple-element.68), channel_id=1, source_target_pairs={{1,2},{5,6},{9,10},{13,14},{17,18},{21,22},{25,26},{29,30},{33,34}... | collective-permute-start | bytes 1179656 | tf_op jit(solution)/shard_map/ppermute | solution.py:46
  82.9 28.7 %collective-permute-start.18 = (bf16[128,3072]{1,0:T(8,128)(2,1)}, bf16[128,3072]{1,0:T(8,128)(2,1)S(1)}, u32[]{:S(2)}, u32[]{:S(2)}) collective-permute-start(bf16[128,3072]{1,0:T(8,128)(2,1)} %get-tuple-element.61.refs_3_), channel_id=1, source_target_pairs={{0,4},{4,8},{8,12},{12,0},{16,20},{20,24},{24,28},{28,16},{32,36},... | collective-permute-start | bytes 2359304 | tf_op jit(solution)/shard_map/ppermute | solution.py:46
  83.2 19.8 %copy-start.16 = (bf16[64,3072]{1,0:T(8,128)(2,1)}, bf16[64,3072]{1,0:T(8,128)(2,1)S(1)}, u32[]{:S(2)}) copy-start(bf16[64,3072]{1,0:T(8,128)(2,1)S(1)} %collective-permute-done.21.refs_0_) | copy-start | bytes 1179652
  83.2 28.5 %collective-permute-start.22 = (bf16[64,3072]{1,0:T(8,128)(2,1)S(1)}, bf16[64,3072]{1,0:T(8,128)(2,1)S(1)}, u32[]{:S(2)}, u32[]{:S(2)}) collective-permute-start(bf16[64,3072]{1,0:T(8,128)(2,1)S(1)} %collective-permute-done.21.refs_0_), channel_id=1, source_target_pairs={{0,1},{4,5},{8,9},{12,13},{16,17},{20,21},{24,25},{28,29},{32,33},... | collective-permute-start | bytes 1179656 | tf_op jit(solution)/shard_map/ppermute | solution.py:46
  92.0 26.3 %collective-permute-start.19 = (bf16[128,3072]{1,0:T(8,128)(2,1)}, bf16[128,3072]{1,0:T(8,128)(2,1)}, u32[]{:S(2)}, u32[]{:S(2)}) collective-permute-start(bf16[128,3072]{1,0:T(8,128)(2,1)} %get-tuple-element.61.refs_3_), channel_id=1, source_target_pairs={{0,12},{4,0},{8,4},{12,8},{16,28},{20,16},{24,20},{28,24},{32,44},... | collective-permute-start | bytes 2359304 | tf_op jit(solution)/shard_map/ppermute | solution.py:46
  92.0 26.2 %collective-permute-start.16 = (bf16[128,3072]{1,0:T(8,128)(2,1)}, bf16[128,3072]{1,0:T(8,128)(2,1)}, u32[]{:S(2)}, u32[]{:S(2)}) collective-permute-start(bf16[128,3072]{1,0:T(8,128)(2,1)} %copy-done.5), channel_id=1, source_target_pairs={{0,4},{4,8},{8,12},{12,0},{16,20},{20,24},{24,28},{28,16},{32,36},... | collective-permute-start | bytes 2359304 | tf_op jit(solution)/shard_map/ppermute | solution.py:46
  94.6 8.3 %copy-start.17 = (bf16[64,3072]{1,0:T(8,128)(2,1)}, bf16[64,3072]{1,0:T(8,128)(2,1)S(1)}, u32[]{:S(2)}) copy-start(bf16[64,3072]{1,0:T(8,128)(2,1)S(1)} %collective-permute-done.23.refs_2_) | copy-start | bytes 1179652
  94.6 17.0 %collective-permute-start.24 = (bf16[64,3072]{1,0:T(8,128)(2,1)S(1)}, bf16[64,3072]{1,0:T(8,128)(2,1)}, u32[]{:S(2)}, u32[]{:S(2)}) collective-permute-start(bf16[64,3072]{1,0:T(8,128)(2,1)S(1)} %collective-permute-done.23.refs_2_), channel_id=1, source_target_pairs={{0,1},{4,5},{8,9},{12,13},{16,17},{20,21},{24,25},{28,29},{32,33},... | collective-permute-start | bytes 1179656 | tf_op jit(solution)/shard_map/ppermute | solution.py:46
  111.7 1.0 copy-start.3
  115.3 20.3 %collective-permute-start.25 = (bf16[128,3072]{1,0:T(8,128)(2,1)}, bf16[128,3072]{1,0:T(8,128)(2,1)S(1)}, u32[]{:S(2)}, u32[]{:S(2)}) collective-permute-start(bf16[128,3072]{1,0:T(8,128)(2,1)} %pack.5.refs_3_), channel_id=1, source_target_pairs={{0,4},{4,8},{8,12},{12,0},{16,20},{20,24},{24,28},{28,16},{32,36},... | collective-permute-start | bytes 2359304 | tf_op jit(solution)/shard_map/ppermute | solution.py:46
  115.5 22.1 %collective-permute-start.26 = (bf16[128,3072]{1,0:T(8,128)(2,1)}, bf16[128,3072]{1,0:T(8,128)(2,1)S(1)}, u32[]{:S(2)}, u32[]{:S(2)}) collective-permute-start(bf16[128,3072]{1,0:T(8,128)(2,1)} %pack.5.refs_3_), channel_id=1, source_target_pairs={{0,12},{4,0},{8,4},{12,8},{16,28},{20,16},{24,20},{28,24},{32,44},... | collective-permute-start | bytes 2359304 | tf_op jit(solution)/shard_map/ppermute | solution.py:46
  116.9 26.8 %collective-permute-start.20 = (bf16[128,3072]{1,0:T(8,128)(2,1)}, bf16[128,3072]{1,0:T(8,128)(2,1)}, u32[]{:S(2)}, u32[]{:S(2)}) collective-permute-start(bf16[128,3072]{1,0:T(8,128)(2,1)} %copy-done.3), channel_id=1, source_target_pairs={{0,4},{4,8},{8,12},{12,0},{16,20},{20,24},{24,28},{28,16},{32,36},... | collective-permute-start | bytes 2359304 | tf_op jit(solution)/shard_map/ppermute | solution.py:46
  135.6 0.9 copy-start
  137.2 14.8 %collective-permute-start.27 = (bf16[128,3072]{1,0:T(8,128)(2,1)}, bf16[128,3072]{1,0:T(8,128)(2,1)S(1)}, u32[]{:S(2)}, u32[]{:S(2)}) collective-permute-start(bf16[128,3072]{1,0:T(8,128)(2,1)} %after.3.refs_4_), channel_id=1, source_target_pairs={{0,4},{4,8},{8,12},{12,0},{16,20},{20,24},{24,28},{28,16},{32,36},... | collective-permute-start | bytes 2359304 | tf_op jit(solution)/shard_map/ppermute | solution.py:46
  137.6 6.1 %copy-start.2 = (bf16[128,3072]{1,0:T(8,128)(2,1)}, bf16[128,3072]{1,0:T(8,128)(2,1)S(1)}, u32[]{:S(2)}) copy-start(bf16[128,3072]{1,0:T(8,128)(2,1)S(1)} %collective-permute-done.26.refs_5_) | copy-start | bytes 2359300
  152.0 0.9 copy-start.1
  159.3 10.0 %collective-permute-start.28 = (bf16[512,1536]{1,0:T(8,128)(2,1)}, bf16[512,1536]{1,0:T(8,128)(2,1)S(1)}, u32[]{:S(2)}, u32[]{:S(2)}) collective-permute-start(bf16[512,1536]{1,0:T(8,128)(2,1)} %get-tuple-element.79), channel_id=1, source_target_pairs={{0,128},{4,132},{8,136},{12,140},{16,144},{20,148},{24,152},{28,15... | collective-permute-start | bytes 4718600 | tf_op jit(solution)/shard_map/ppermute | solution.py:46
  169.2 1.2 copy-start.11
  (4 other events, 2.9 us)

commit v4 on v3

--- a/solution.py
+++ b/solution.py
@@ -12,8 +12,9 @@
 SLOT = 16
 HALF = NX * SLOT
 ANY = pl.ANY
-VMEM_LIMIT = 62 * 1024 * 1024
+VMEM_LIMIT = 20 * 1024 * 1024
 PARAMS = pltpu.CompilerParams(vmem_limit_bytes=VMEM_LIMIT)
+WHOLE = pltpu.CompilerParams(vmem_limit_bytes=62 * 1024 * 1024)
 
 
 def chip_perm(fn):
@@ -118,6 +119,7 @@
 COLS = 512
 SMEM_SPEC = pl.BlockSpec(memory_space=pltpu.SMEM)
 ANY_SPEC = pl.BlockSpec(memory_space=ANY)
+HBM_SPEC = pl.BlockSpec(memory_space=pltpu.HBM)
 MARK = jax.ShapeDtypeStruct((1,), jnp.int32)
 
 
@@ -199,7 +201,7 @@
         c.wait()
 
 
-def hidden_grads(parts, offs, gate, up, wt, outs, *marks):
+def hidden_grads(parts, offs, gate, up, wt, outs, *marks, params=PARAMS):
     rows = [p[0] for p in parts]
     ids = tuple(i for p in parts for i in p[1])
     counts = tuple(r.shape[0] for r in rows)
@@ -214,8 +216,8 @@
     *outs, mark = pl.pallas_call(
         functools.partial(hidden_grad_kernel, counts, ids, waits, bool(outs)),
         out_shape=(jax.ShapeDtypeStruct(gate.shape, jnp.bfloat16),) * 2 + (MARK,),
-        in_specs=[SMEM_SPEC] * (waits + 1) + [ANY_SPEC] * (len(args) - waits - 1),
-        out_specs=(ANY_SPEC, ANY_SPEC, SMEM_SPEC),
+        in_specs=[SMEM_SPEC] * (waits + 1) + [ANY_SPEC] * (n + 3) + [HBM_SPEC] * (2 if outs else 0),
+        out_specs=(HBM_SPEC, HBM_SPEC, SMEM_SPEC),
         scratch_shapes=[
             pltpu.VMEM((total, width), jnp.bfloat16),
             pltpu.VMEM((width, units), jnp.bfloat16),
@@ -226,7 +228,7 @@
             pltpu.SemaphoreType.DMA((1,)),
         ],
         input_output_aliases=aliases,
-        compiler_params=PARAMS,
+        compiler_params=params,
         cost_estimate=pl.CostEstimate(
             flops=2 * total * units * width,
             bytes_accessed=2 * (total * width + width * units + 4 * total * units),
@@ -288,7 +290,7 @@
         c.wait()
 
 
-def weight_sums(parts, hid, lane, kind, *marks, acc=None, got=None, first=None, factor=None):
+def weight_sums(parts, hid, lane, kind, *marks, acc=None, got=None, first=None, factor=None, params=PARAMS):
     rows = [p[0] for p in parts]
     counts = tuple(r.shape[0] for r in rows)
     total, n, waits = sum(counts), len(rows), len(marks)
@@ -312,10 +314,13 @@
             weight_sum_kernel, counts, lane, span, factor, waits, acc is not None, got is not None
         ),
         out_shape=(jax.ShapeDtypeStruct((units, span * COLS), kind), MARK),
-        in_specs=[SMEM_SPEC] * (waits + 1) + [ANY_SPEC] * (len(args) - waits - 1),
-        out_specs=(ANY_SPEC, SMEM_SPEC),
+        in_specs=[SMEM_SPEC] * (waits + 1)
+        + [ANY_SPEC] * (n + 1)
+        + [HBM_SPEC] * (acc is not None)
+        + [ANY_SPEC] * (got is not None),
+        out_specs=(HBM_SPEC, SMEM_SPEC),
         scratch_shapes=scratch,
-        compiler_params=PARAMS,
+        compiler_params=params,
         cost_estimate=pl.CostEstimate(
             flops=2 * total * units * span * COLS,
             bytes_accessed=2 * total * (units + span * COLS) + 4 * units * span * COLS,
@@ -481,14 +486,14 @@
     acc, m5 = weight_sums(b4 + c3, hid, 14 * HALF, jnp.float32, m4, acc=acc)
     d[1], = after([d[1]], m5)
     d3, d4 = fill(d3, d), fill(d4, [send(d[1], Y_ON)])
-    outs, m6 = hidden_grads(c4 + d3, offs, gate, up, wt, outs, m5)
+    outs, m6 = hidden_grads(c4 + d3, offs, gate, up, wt, outs, m5, params=WHOLE)
     rest, lane = c4 + d3 + d4, 22 * HALF
-    give, m7 = weight_sums(rest, hid, lane, jnp.bfloat16, m6, acc=acc, first=theirs)
+    give, m7 = weight_sums(rest, hid, lane, jnp.bfloat16, m6, acc=acc, first=theirs, params=WHOLE)
     got = send(give, DP_SWAP)
-    outs, m8 = hidden_grads(d4, offs, gate, up, wt, outs, m7)
+    outs, m8 = hidden_grads(d4, offs, gate, up, wt, outs, m7, params=WHOLE)
     factor = 1.0 / (2 * 64 * 8 * 16) ** 0.5
     weight_grad, _ = weight_sums(
-        rest, hid, lane, jnp.bfloat16, m8, acc=acc, got=got, first=mine, factor=factor
+        rest, hid, lane, jnp.bfloat16, m8, acc=acc, got=got, first=mine, factor=factor, params=WHOLE
     )
     return (outs[0][None, None], outs[1][None, None], weight_grad[None])
 

time: 179 us -> 174 us (0.972)
  Pallas kernels: 88 us -> 75 us
  waiting for transfers between devices: 26.9 us -> 35.9 us
  starting transfers between devices: 47.6 us -> 45.2 us
    ppermute x29, waiting for transfers between devices: 26.9 us -> 35.9 us  [send(): return lax.ppermute(a, AX, pairs)]
    pallas_call x3, Pallas kernels: 9.78 us -> 6.01 us  [pack(): pl.pallas_call(functools.partial(pack_kernel, plan, len(arrays)), out_sha...]
    pallas_call x5, Pallas kernels: 36.7 us -> 33.7 us  [hidden_grads(): pl.pallas_call(functools.partial(hidden_grad_kernel, counts, ids, waits,...]
    pallas_call x1, Pallas kernels: 4.65 us -> 1.97 us  [hidden_rows(): pl.pallas_call(hidden_kernel, out_shape=(jax.ShapeDtypeStruct((units, slo...]
    pallas_call x4, Pallas kernels: 31.8 us -> 29.1 us  [weight_sums(): pl.pallas_call(functools.partial(weight_sum_kernel, counts, lane, span, f...]
    ppermute x29, starting transfers between devices: 47.6 us -> 45.2 us  [send(): return lax.ppermute(a, AX, pairs)]
    unnamed x47 -> x39, local copies, waits for them, and re-layouts: 13.2 us -> 14.9 us
  transfers between devices with their start and end apart: 29 -> 29, of which waited for: 8 -> 9; matrix products, arithmetic and copies ran while one was open for 3% -> 2% of each run, Pallas kernels for 37% -> 32%
where the time goes in v4:
time: 174 us; the launch traced here: 172 us
  Pallas kernels  75 us (43%)
  starting transfers between devices  45.2 us (26%)
  waiting for transfers between devices  35.9 us (21%)
  local copies, waits for them, and re-layouts  15 us (9%)
    ppermute x29, starting transfers between devices, send(): return lax.ppermute(a, AX, pairs)  45.2 us
    ppermute x29, waiting for transfers between devices, send(): return lax.ppermute(a, AX, pairs)  35.9 us
    pallas_call x5, Pallas kernels, hidden_grads(): pl.pallas_call(functools.partial(hidden_grad_kernel, counts, ids, waits,...  33.7 us
    pallas_call x4, Pallas kernels, weight_sums(): pl.pallas_call(functools.partial(weight_sum_kernel, counts, lane, span, f...  29.1 us
    unnamed x39, local copies, waits for them, and re-layouts  14.9 us
    pallas_call x3, Pallas kernels, pack(): pl.pallas_call(functools.partial(pack_kernel, plan, len(arrays)), out_sha...  6.01 us
  transfers between devices with their start and end apart: 29, of which 9 were waited for; matrix products, arithmetic and copies ran while one was open for 2% of the time, Pallas kernels for 32%

profile of v4, /device:TPU:1, one launch (start us, length us, event | category | flops | bytes accessed | tf_op | source)
XLA Modules:
  0.0 172.3 jit_solution(5704872376948226716)
XLA Ops:
  0.7 1.0 copy-done.13
  3.0 1.8 %dispatch.1 = (bf16[32,3072]{1,0:T(8,128)(2,1)S(1)}, bf16[32,3072]{1,0:T(8,128)(2,1)}, bf16[32,3072]{1,0:T(8,128)(2,1)}, bf16[32,3072]{1,0:T(8,128)(2,1)}) custom-call(s32[2]{0:T(128)S(1)} %pad_add_fusion.place, bf16[64,3072]{1,0:T(8,128)(2,1)S(1)} %bitcast.65, f32[1,64]{1,0:T(1,128)S(1)} %copy-done.15, s32[1,64]{1,0:T(1,128)S(1)} %bitcast.66), custom_call_target="tpu_custom_call" | custom-call | tf_op jit(solution)/shard_map/dispatch/pallas_call | solution.py:77
  4.8 2.0 %collective-permute-start = (bf16[32,3072]{1,0:T(8,128)(2,1)}, bf16[32,3072]{1,0:T(8,128)(2,1)S(1)}, u32[]{:S(2)}, u32[]{:S(2)}) collective-permute-start(bf16[32,3072]{1,0:T(8,128)(2,1)} %get-tuple-element.43), channel_id=1, source_target_pairs={{0,16},{4,20},{8,24},{12,28},{16,32},{20,36},{24,40},{28,44},{32,4... | collective-permute-start | bytes 589832 | tf_op jit(solution)/shard_map/ppermute | solution.py:47
  6.8 2.5 %collective-permute-start.1 = (bf16[32,3072]{1,0:T(8,128)(2,1)}, bf16[32,3072]{1,0:T(8,128)(2,1)}, u32[]{:S(2)}, u32[]{:S(2)}) collective-permute-start(bf16[32,3072]{1,0:T(8,128)(2,1)} %get-tuple-element.44), channel_id=1, source_target_pairs={{0,32},{4,36},{8,40},{12,44},{16,48},{20,52},{24,56},{28,60},{32,0... | collective-permute-start | bytes 589832 | tf_op jit(solution)/shard_map/ppermute | solution.py:47
  9.3 1.1 collective-permute-start.2
  10.4 3.2 %copy.20 = bf16[1,512,3072]{1,2,0:T(8,128)(2,1)S(1)} copy(bf16[1,512,3072]{2,1,0:T(8,128)(2,1)} %param.11) | data formatting | bytes 6291456 | tf_op args[5]
  13.6 4.5 %collective-permute-done.1.b2 = bf16[32,3072]{1,0:T(8,128)(2,1)} collective-permute-done((bf16[32,3072]{1,0:T(8,128)(2,1)}, bf16[32,3072]{1,0:T(8,128)(2,1)}, u32[]{:S(2)}, u32[]{:S(2)}) %collective-permute-start.1) | collective-permute-done | bytes 196640 | tf_op jit(solution)/shard_map/ppermute | solution.py:47
  18.1 1.8 %assemble.1 = (bf16[64,3072]{1,0:T(8,128)(2,1)S(1)}, bf16[32,3072]{1,0:T(8,128)(2,1)S(1)}, bf16[32,3072]{1,0:T(8,128)(2,1)}) custom-call(s32[2]{0:T(128)S(1)} %pad_add_fusion.place, bf16[32,3072]{1,0:T(8,128)(2,1)S(1)} %get-tuple-element.42.b0, bf16[32,3072]{1,0:T(8,128)(2,1)S(1)} %collective-permute-done.b1, bf16[32,3072]{1,0:T(8,128)(2,1)} %collective-permute-done.1.b2, ...), custom_call_target="tpu_custom_call" | custom-call | tf_op jit(solution)/shard_map/assemble/pallas_call | solution.py:101
  19.9 1.4 collective-permute-start.6
  21.3 3.9 %collective-permute-start.5 = (bf16[64,3072]{1,0:T(8,128)(2,1)S(1)}, bf16[64,3072]{1,0:T(8,128)(2,1)}, u32[]{:S(2)}, u32[]{:S(2)}) collective-permute-start(bf16[64,3072]{1,0:T(8,128)(2,1)S(1)} %get-tuple-element.46.refs_1_.refs_2_), channel_id=1, source_target_pairs={{0,1},{4,5},{8,9},{12,13},{16,17},{20,21},{24,25},{28,29},{32,33},... | collective-permute-start | bytes 1179656 | tf_op jit(solution)/shard_map/ppermute | solution.py:47
  25.2 1.3 collective-permute-start.4
  26.5 1.4 collective-permute-start.3
  27.9 3.8 %collective-permute-start.7 = (bf16[32,3072]{1,0:T(8,128)(2,1)S(1)}, bf16[32,3072]{1,0:T(8,128)(2,1)S(1)}, u32[]{:S(2)}, u32[]{:S(2)}) collective-permute-start(bf16[32,3072]{1,0:T(8,128)(2,1)S(1)} %get-tuple-element.47), channel_id=1, source_target_pairs={{0,67},{4,71},{8,75},{12,79},{16,83},{20,87},{24,91},{28,95},{32,9... | collective-permute-start | bytes 589832 | tf_op jit(solution)/shard_map/ppermute | solution.py:47
  31.7 7.0 %collective-permute-done.7.refs_2_.refs_0_ = bf16[32,3072]{1,0:T(8,128)(2,1)S(1)} collective-permute-done((bf16[32,3072]{1,0:T(8,128)(2,1)S(1)}, bf16[32,3072]{1,0:T(8,128)(2,1)S(1)}, u32[]{:S(2)}, u32[]{:S(2)}) %collective-permute-start.7) | collective-permute-done | bytes 196640 | tf_op jit(solution)/shard_map/ppermute | solution.py:47
  40.1 3.0 %collective-permute-start.11 = (bf16[64,3072]{1,0:T(8,128)(2,1)}, bf16[64,3072]{1,0:T(8,128)(2,1)}, u32[]{:S(2)}, u32[]{:S(2)}) collective-permute-start(bf16[64,3072]{1,0:T(8,128)(2,1)} %get-tuple-element.51.refs_2_), channel_id=1, source_target_pairs={{0,1},{4,5},{8,9},{12,13},{16,17},{20,21},{24,25},{28,29},{32,33},... | collective-permute-start | bytes 1179656 | tf_op jit(solution)/shard_map/ppermute | solution.py:47
  43.0 1.4 collective-permute-start.12
  44.5 1.3 collective-permute-start.9
  45.8 1.4 collective-permute-start.8
  47.9 1.6 copy-done.1
  49.4 1.6 copy-done.3
  51.0 2.0 %hidden_rows.1 = (bf16[512,2048]{1,0:T(8,128)(2,1)S(1)}, s32[1]{0:T(128)}) custom-call(s32[32]{0:T(128)S(1)} %stack.140.refs_0_.offs.refs_1_, bf16[2048,512]{1,0:T(8,128)(2,1)S(1)} %bitcast.55, bf16[2048,512]{1,0:T(8,128)(2,1)S(1)} %bitcast.61), custom_call_target="tpu_custom_call" | custom-call | bytes 6291456 | tf_op jit(solution)/shard_map/hidden_rows/pallas_call | solution.py:141
  53.3 1.9 %collective-permute-done.8.refs_5_.refs_6_ = bf16[64,3072]{1,0:T(8,128)(2,1)} collective-permute-done((bf16[64,3072]{1,0:T(8,128)(2,1)}, bf16[64,3072]{1,0:T(8,128)(2,1)}, u32[]{:S(2)}, u32[]{:S(2)}) %collective-permute-start.8) | collective-permute-done | bytes 393248 | tf_op jit(solution)/shard_map/ppermute | solution.py:47
  55.3 2.8 %pack.3 = (bf16[128,3072]{1,0:T(8,128)(2,1)S(1)}, bf16[128,3072]{1,0:T(8,128)(2,1)S(1)}, bf16[64,3072]{1,0:T(8,128)(2,1)S(1)}, bf16[128,3072]{1,0:T(8,128)(2,1)S(1)}) custom-call(s32[1]{0:T(128)} %bitcast.40.inner, bf16[32,3072]{1,0:T(8,128)(2,1)S(1)} %copy-done.10, bf16[32,3072]{1,0:T(8,128)(2,1)} %collective-permute-done.10.refs_1_, ...), custom_call_target="tpu_custom_call" | custom-call | bytes 5505024 | tf_op jit(solution)/shard_map/pack/pallas_call | solution.py:379
  58.1 2.9 %collective-permute-start.17 = (bf16[128,3072]{1,0:T(8,128)(2,1)S(1)}, bf16[128,3072]{1,0:T(8,128)(2,1)S(1)}, u32[]{:S(2)}, u32[]{:S(2)}) collective-permute-start(bf16[128,3072]{1,0:T(8,128)(2,1)S(1)} %get-tuple-element.60.refs_1_), channel_id=1, source_target_pairs={{0,1},{4,5},{8,9},{12,13},{16,17},{20,21},{24,25},{28,29},{32,33},... | collective-permute-start | bytes 2359304 | tf_op jit(solution)/shard_map/ppermute | solution.py:47
  63.4 6.5 %hidden_grads.5 = (bf16[2048,512]{1,0:T(8,128)(2,1)}, bf16[2048,512]{1,0:T(8,128)(2,1)}, s32[1]{0:T(128)}) custom-call(s32[32]{0:T(128)S(1)} %stack.140.refs_0_.offs.refs_1_, bf16[64,3072]{1,0:T(8,128)(2,1)S(1)} %copy-done.12, bf16[64,3072]{1,0:T(8,128)(2,1)S(1)} %collective-permute-done.3.refs_3_.refs_2_.refs_5_, bf16[64,3072]{1,0:T(8,128)(2,1)S(1)} %copy-done.8, ...), custom_call_target="tpu_custom_call" | custom-call | flops 1207959552 | bytes 7077888 | tf_op jit(solution)/shard_map/hidden_grads/pallas_call | solution.py:216
  69.9 5.1 %collective-permute-done.17.refs_0_ = bf16[128,3072]{1,0:T(8,128)(2,1)S(1)} collective-permute-done((bf16[128,3072]{1,0:T(8,128)(2,1)S(1)}, bf16[128,3072]{1,0:T(8,128)(2,1)S(1)}, u32[]{:S(2)}, u32[]{:S(2)}) %collective-permute-start.17) | collective-permute-done | bytes 786464 | tf_op jit(solution)/shard_map/ppermute | solution.py:47
  75.0 1.2 pack.4
  77.2 4.3 %collective-permute-start.22 = (bf16[64,3072]{1,0:T(8,128)(2,1)S(1)}, bf16[64,3072]{1,0:T(8,128)(2,1)S(1)}, u32[]{:S(2)}, u32[]{:S(2)}) collective-permute-start(bf16[64,3072]{1,0:T(8,128)(2,1)S(1)} %collective-permute-done.21.refs_0_), channel_id=1, source_target_pairs={{0,1},{4,5},{8,9},{12,13},{16,17},{20,21},{24,25},{28,29},{32,33},... | collective-permute-start | bytes 1179656 | tf_op jit(solution)/shard_map/ppermute | solution.py:47
  81.5 7.4 %collective-permute-done.13.refs_2_.refs_8_ = bf16[128,3072]{1,0:T(8,128)(2,1)S(1)} collective-permute-done((bf16[128,3072]{1,0:T(8,128)(2,1)S(1)}, bf16[128,3072]{1,0:T(8,128)(2,1)S(1)}, u32[]{:S(2)}, u32[]{:S(2)}) %collective-permute-start.13) | collective-permute-done | bytes 786464 | tf_op jit(solution)/shard_map/ppermute | solution.py:47
  89.0 2.7 %collective-permute-start.16 = (bf16[128,3072]{1,0:T(8,128)(2,1)S(1)}, bf16[128,3072]{1,0:T(8,128)(2,1)S(1)}, u32[]{:S(2)}, u32[]{:S(2)}) collective-permute-start(bf16[128,3072]{1,0:T(8,128)(2,1)S(1)} %collective-permute-done.14.refs_4_.refs_10_.refs_3_), channel_id=1, source_target_pairs={{0,4},{4,8},{8,12},{12,0},{16,20},{20,24},{24,28},{28,16},{32,36},... | collective-permute-start | bytes 2359304 | tf_op jit(solution)/shard_map/ppermute | solution.py:47
  91.7 6.8 %hidden_grads.6 = (bf16[2048,512]{1,0:T(8,128)(2,1)}, bf16[2048,512]{1,0:T(8,128)(2,1)}, s32[1]{0:T(128)}) custom-call(s32[1]{0:T(128)} %get-tuple-element.49.refs_0_.refs_2_, s32[32]{0:T(128)S(1)} %stack.140.refs_0_.offs.refs_1_, bf16[128,3072]{1,0:T(8,128)(2,1)S(1)} %collective-permute-done.13.refs_2_.refs_8_, ...), custom_call_target="tpu_custom_call", output_to_operand_aliasing={{0}: (9, {}), {1}: (10, {})} | custom-call | flops 1610612736 | bytes 8388608 | tf_op jit(solution)/shard_map/hidden_grads/pallas_call | solution.py:216
  98.6 8.5 %weight_sums.4 = (f32[512,3072]{1,0:T(8,128)S(1)}, s32[1]{0:T(128)}) custom-call(s32[1]{0:T(128)} %get-tuple-element.57.refs_0_, s32[1]{0:T(128)} %constant.29.clone.1.refs_1_, bf16[64,3072]{1,0:T(8,128)(2,1)S(1)} %copy-done.12, bf16[64,3072]{1,0:T(8,128)(2,1)S(1)} %collective-permute-done.3.refs_3_.refs_2_.refs_5_, bf16[64,3072]{1,0:T(8,128)(2,1)S(1)} %copy-done.8, ...), custom_call_target="tpu_custom_call" | custom-call | flops 2818572288 | bytes 12713984 | tf_op jit(solution)/shard_map/weight_sums/pallas_call | solution.py:312
  107.1 2.0 %pack.5.refs_3_ = bf16[128,3072]{1,0:T(8,128)(2,1)} custom-call(s32[1]{0:T(128)} %bitcast.40.inner, bf16[64,3072]{1,0:T(8,128)(2,1)S(1)} %collective-permute-done.21.refs_0_, bf16[64,3072]{1,0:T(8,128)(2,1)S(1)} %collective-permute-done.22.refs_1_, bf16[64,3072]{1,0:T(8,128)(2,1)S(1)} %collective-permute-done.23.refs_2_, ...), custom_call_target="tpu_custom_call" | custom-call | bytes 1572864 | tf_op jit(solution)/shard_map/pack/pallas_call | solution.py:379
  109.2 1.4 collective-permute-start.26
  110.6 1.3 collective-permute-start.20
  111.9 2.3 %collective-permute-done.16.refs_2_ = bf16[128,3072]{1,0:T(8,128)(2,1)S(1)} collective-permute-done((bf16[128,3072]{1,0:T(8,128)(2,1)S(1)}, bf16[128,3072]{1,0:T(8,128)(2,1)S(1)}, u32[]{:S(2)}, u32[]{:S(2)}) %collective-permute-start.16) | collective-permute-done | bytes 786464 | tf_op jit(solution)/shard_map/ppermute | solution.py:47
  114.3 6.8 %hidden_grads.7 = (bf16[2048,512]{1,0:T(8,128)(2,1)}, bf16[2048,512]{1,0:T(8,128)(2,1)}, s32[1]{0:T(128)}) custom-call(s32[1]{0:T(128)} %get-tuple-element.59.refs_0_.refs_4_, s32[32]{0:T(128)S(1)} %stack.140.refs_0_.offs.refs_1_, bf16[128,3072]{1,0:T(8,128)(2,1)S(1)} %collective-permute-done.16.refs_2_, ...), custom_call_target="tpu_custom_call", output_to_operand_aliasing={{0}: (9, {}), {1}: (10, {})} | custom-call | flops 1610612736 | bytes 8388608 | tf_op jit(solution)/shard_map/hidden_grads/pallas_call | solution.py:216
  121.0 6.9 %weight_sums.5 = (f32[512,3072]{1,0:T(8,128)S(1)}, s32[1]{0:T(128)}) custom-call(s32[1]{0:T(128)} %get-tuple-element.64.refs_0_, s32[1]{0:T(128)} %constant.29.clone.1.refs_1_, bf16[128,3072]{1,0:T(8,128)(2,1)S(1)} %collective-permute-done.16.refs_2_, bf16[128,3072]{1,0:T(8,128)(2,1)S(1)} %get-tuple-element.61.refs_3_, ...), custom_call_target="tpu_custom_call" | custom-call | flops 1610612736 | bytes 9961472 | tf_op jit(solution)/shard_map/weight_sums/pallas_call | solution.py:312
  127.9 2.7 %copy-done.5 = f32[512,3072]{1,0:T(8,128)} copy-done((f32[512,3072]{1,0:T(8,128)}, f32[512,3072]{1,0:T(8,128)S(1)}, u32[]{:S(2)}) %copy-start.5) | copy-done | bytes 6291480
  131.2 1.2 collective-permute-start.27
  132.4 7.2 %collective-permute-done.20.refs_2_ = bf16[128,3072]{1,0:T(8,128)(2,1)} collective-permute-done((bf16[128,3072]{1,0:T(8,128)(2,1)}, bf16[128,3072]{1,0:T(8,128)(2,1)}, u32[]{:S(2)}, u32[]{:S(2)}) %collective-permute-start.20) | collective-permute-done | bytes 786464 | tf_op jit(solution)/shard_map/ppermute | solution.py:47
  139.6 8.2 %hidden_grads.8 = (bf16[2048,512]{1,0:T(8,128)(2,1)}, bf16[2048,512]{1,0:T(8,128)(2,1)}, s32[1]{0:T(128)}) custom-call(s32[1]{0:T(128)} %get-tuple-element.66.refs_1_.refs_0_, s32[32]{0:T(128)} %copy-done.14, bf16[128,3072]{1,0:T(8,128)(2,1)} %collective-permute-done.20.refs_2_, ...), custom_call_target="tpu_custom_call", output_to_operand_aliasing={{0}: (9, {}), {1}: (10, {})} | custom-call | flops 1610612736 | bytes 8388608 | tf_op jit(solution)/shard_map/hidden_grads/pallas_call | solution.py:216
  148.0 0.9 copy-done.17
  148.9 6.4 %weight_sums.6 = (bf16[512,1536]{1,0:T(8,128)(2,1)}, s32[1]{0:T(128)}) custom-call(s32[1]{0:T(128)} %get-tuple-element.71.refs_0_, s32[1]{0:T(128)} %bitcast.41.refs_1_, bf16[128,3072]{1,0:T(8,128)(2,1)} %collective-permute-done.20.refs_2_, bf16[128,3072]{1,0:T(8,128)(2,1)} %pack.5.refs_3_, bf16[128,3072]{1,0:T(8,128)(2,1)} %after.3.refs_4_, ...), custom_call_target="tpu_custom_call" | custom-call | flops 1006632960 | bytes 5767168 | tf_op jit(solution)/shard_map/weight_sums/pallas_call | solution.py:312
  155.2 2.8 %collective-permute-start.28 = (bf16[512,1536]{1,0:T(8,128)(2,1)}, bf16[512,1536]{1,0:T(8,128)(2,1)S(1)}, u32[]{:S(2)}, u32[]{:S(2)}) collective-permute-start(bf16[512,1536]{1,0:T(8,128)(2,1)} %get-tuple-element.79), channel_id=1, source_target_pairs={{0,128},{4,132},{8,136},{12,140},{16,144},{20,148},{24,152},{28,15... | collective-permute-start | bytes 4718600 | tf_op jit(solution)/shard_map/ppermute | solution.py:47
  158.0 5.4 %hidden_grads.9 = (bf16[2048,512]{1,0:T(8,128)(2,1)}, bf16[2048,512]{1,0:T(8,128)(2,1)}, s32[1]{0:T(128)}) custom-call(s32[1]{0:T(128)} %get-tuple-element.73.refs_0_, s32[32]{0:T(128)} %copy-done.14, bf16[128,3072]{1,0:T(8,128)(2,1)} %copy-done.17, bf16[2048,512]{1,0:T(8,128)(2,1)} %bitcast.54, ...), custom_call_target="tpu_custom_call", output_to_operand_aliasing={{0}: (6, {}), {1}: (7, {})} | custom-call | flops 402653184 | bytes 4456448 | tf_op jit(solution)/shard_map/hidden_grads/pallas_call | solution.py:216
  163.5 1.2 copy-done.18
  164.7 7.4 %weight_sums.7 = (bf16[512,1536]{1,0:T(8,128)(2,1)}, s32[1]{0:T(128)}) custom-call(s32[1]{0:T(128)} %get-tuple-element.78.refs_0_, s32[1]{0:T(128)} %bitcast.44.refs_1_, bf16[128,3072]{1,0:T(8,128)(2,1)} %collective-permute-done.20.refs_2_, bf16[128,3072]{1,0:T(8,128)(2,1)} %pack.5.refs_3_, bf16[128,3072]{1,0:T(8,128)(2,1)} %after.3.refs_4_, ...), custom_call_target="tpu_custom_call" | custom-call | flops 1006632960 | bytes 5767168 | tf_op jit(solution)/shard_map/weight_sums/pallas_call | solution.py:312
  (68 shorter events, 8.1 us)
Async XLA Ops:
  0.7 1.0 copy-start.13
  1.7 0.7 copy-start.15
  2.4 0.7 copy-start.16
  4.8 8.8 %collective-permute-start = (bf16[32,3072]{1,0:T(8,128)(2,1)}, bf16[32,3072]{1,0:T(8,128)(2,1)S(1)}, u32[]{:S(2)}, u32[]{:S(2)}) collective-permute-start(bf16[32,3072]{1,0:T(8,128)(2,1)} %get-tuple-element.43), channel_id=1, source_target_pairs={{0,16},{4,20},{8,24},{12,28},{16,32},{20,36},{24,40},{28,44},{32,4... | collective-permute-start | bytes 589832 | tf_op jit(solution)/shard_map/ppermute | solution.py:47
  6.8 11.3 %collective-permute-start.1 = (bf16[32,3072]{1,0:T(8,128)(2,1)}, bf16[32,3072]{1,0:T(8,128)(2,1)}, u32[]{:S(2)}, u32[]{:S(2)}) collective-permute-start(bf16[32,3072]{1,0:T(8,128)(2,1)} %get-tuple-element.44), channel_id=1, source_target_pairs={{0,32},{4,36},{8,40},{12,44},{16,48},{20,52},{24,56},{28,60},{32,0... | collective-permute-start | bytes 589832 | tf_op jit(solution)/shard_map/ppermute | solution.py:47
  9.3 8.8 %collective-permute-start.2 = (bf16[32,3072]{1,0:T(8,128)(2,1)}, bf16[32,3072]{1,0:T(8,128)(2,1)}, u32[]{:S(2)}, u32[]{:S(2)}) collective-permute-start(bf16[32,3072]{1,0:T(8,128)(2,1)} %get-tuple-element.45), channel_id=1, source_target_pairs={{0,48},{4,52},{8,56},{12,60},{16,0},{20,4},{24,8},{28,12},{32,16},... | collective-permute-start | bytes 589832 | tf_op jit(solution)/shard_map/ppermute | solution.py:47
  13.6 100.6 %copy-start = (bf16[1,512,3072]{1,2,0:T(8,128)(2,1)}, bf16[1,512,3072]{1,2,0:T(8,128)(2,1)S(1)}, u32[]{:S(2)}) copy-start(bf16[1,512,3072]{1,2,0:T(8,128)(2,1)S(1)} %copy.20) | copy-start | bytes 9437188
  19.9 20.2 %copy-start.11 = (bf16[64,3072]{1,0:T(8,128)(2,1)}, bf16[64,3072]{1,0:T(8,128)(2,1)S(1)}, u32[]{:S(2)}) copy-start(bf16[64,3072]{1,0:T(8,128)(2,1)S(1)} %get-tuple-element.46.refs_1_.refs_2_) | copy-start | bytes 1179652
  19.9 18.7 %collective-permute-start.6 = (bf16[64,3072]{1,0:T(8,128)(2,1)S(1)}, bf16[64,3072]{1,0:T(8,128)(2,1)}, u32[]{:S(2)}, u32[]{:S(2)}) collective-permute-start(bf16[64,3072]{1,0:T(8,128)(2,1)S(1)} %get-tuple-element.46.refs_1_.refs_2_), channel_id=1, source_target_pairs={{1,2},{5,6},{9,10},{13,14},{17,18},{21,22},{25,26},{29,30},{33,34}... | collective-permute-start | bytes 1179656 | tf_op jit(solution)/shard_map/ppermute | solution.py:47
  21.3 17.3 %collective-permute-start.5 = (bf16[64,3072]{1,0:T(8,128)(2,1)S(1)}, bf16[64,3072]{1,0:T(8,128)(2,1)}, u32[]{:S(2)}, u32[]{:S(2)}) collective-permute-start(bf16[64,3072]{1,0:T(8,128)(2,1)S(1)} %get-tuple-element.46.refs_1_.refs_2_), channel_id=1, source_target_pairs={{0,1},{4,5},{8,9},{12,13},{16,17},{20,21},{24,25},{28,29},{32,33},... | collective-permute-start | bytes 1179656 | tf_op jit(solution)/shard_map/ppermute | solution.py:47
  25.2 13.5 %collective-permute-start.4 = (bf16[64,3072]{1,0:T(8,128)(2,1)S(1)}, bf16[64,3072]{1,0:T(8,128)(2,1)S(1)}, u32[]{:S(2)}, u32[]{:S(2)}) collective-permute-start(bf16[64,3072]{1,0:T(8,128)(2,1)S(1)} %get-tuple-element.46.refs_1_.refs_2_), channel_id=1, source_target_pairs={{0,12},{4,0},{8,4},{12,8},{16,28},{20,16},{24,20},{28,24},{32,44},... | collective-permute-start | bytes 1179656 | tf_op jit(solution)/shard_map/ppermute | solution.py:47
  26.5 12.2 %collective-permute-start.3 = (bf16[64,3072]{1,0:T(8,128)(2,1)S(1)}, bf16[64,3072]{1,0:T(8,128)(2,1)S(1)}, u32[]{:S(2)}, u32[]{:S(2)}) collective-permute-start(bf16[64,3072]{1,0:T(8,128)(2,1)S(1)} %get-tuple-element.46.refs_1_.refs_2_), channel_id=1, source_target_pairs={{0,4},{4,8},{8,12},{12,0},{16,20},{20,24},{24,28},{28,16},{32,36},... | collective-permute-start | bytes 1179656 | tf_op jit(solution)/shard_map/ppermute | solution.py:47
  27.9 10.7 %collective-permute-start.7 = (bf16[32,3072]{1,0:T(8,128)(2,1)S(1)}, bf16[32,3072]{1,0:T(8,128)(2,1)S(1)}, u32[]{:S(2)}, u32[]{:S(2)}) collective-permute-start(bf16[32,3072]{1,0:T(8,128)(2,1)S(1)} %get-tuple-element.47), channel_id=1, source_target_pairs={{0,67},{4,71},{8,75},{12,79},{16,83},{20,87},{24,91},{28,95},{32,9... | collective-permute-start | bytes 589832 | tf_op jit(solution)/shard_map/ppermute | solution.py:47
  38.6 0.7 copy-start.9
  39.3 0.7 copy-start.7
  40.1 13.2 %collective-permute-start.11 = (bf16[64,3072]{1,0:T(8,128)(2,1)}, bf16[64,3072]{1,0:T(8,128)(2,1)}, u32[]{:S(2)}, u32[]{:S(2)}) collective-permute-start(bf16[64,3072]{1,0:T(8,128)(2,1)} %get-tuple-element.51.refs_2_), channel_id=1, source_target_pairs={{0,1},{4,5},{8,9},{12,13},{16,17},{20,21},{24,25},{28,29},{32,33},... | collective-permute-start | bytes 1179656 | tf_op jit(solution)/shard_map/ppermute | solution.py:47
  43.0 10.2 %collective-permute-start.12 = (bf16[64,3072]{1,0:T(8,128)(2,1)}, bf16[64,3072]{1,0:T(8,128)(2,1)}, u32[]{:S(2)}, u32[]{:S(2)}) collective-permute-start(bf16[64,3072]{1,0:T(8,128)(2,1)} %get-tuple-element.48.refs_4_.refs_5_), channel_id=1, source_target_pairs={{1,2},{5,6},{9,10},{13,14},{17,18},{21,22},{25,26},{29,30},{33,34}... | collective-permute-start | bytes 1179656 | tf_op jit(solution)/shard_map/ppermute | solution.py:47
  44.5 8.8 %collective-permute-start.9 = (bf16[64,3072]{1,0:T(8,128)(2,1)}, bf16[64,3072]{1,0:T(8,128)(2,1)}, u32[]{:S(2)}, u32[]{:S(2)}) collective-permute-start(bf16[64,3072]{1,0:T(8,128)(2,1)} %get-tuple-element.48.refs_4_.refs_5_), channel_id=1, source_target_pairs={{0,12},{4,0},{8,4},{12,8},{16,28},{20,16},{24,20},{28,24},{32,44},... | collective-permute-start | bytes 1179656 | tf_op jit(solution)/shard_map/ppermute | solution.py:47
  45.8 9.5 %collective-permute-start.8 = (bf16[64,3072]{1,0:T(8,128)(2,1)}, bf16[64,3072]{1,0:T(8,128)(2,1)}, u32[]{:S(2)}, u32[]{:S(2)}) collective-permute-start(bf16[64,3072]{1,0:T(8,128)(2,1)} %get-tuple-element.48.refs_4_.refs_5_), channel_id=1, source_target_pairs={{0,4},{4,8},{8,12},{12,0},{16,20},{20,24},{24,28},{28,16},{32,36},... | collective-permute-start | bytes 1179656 | tf_op jit(solution)/shard_map/ppermute | solution.py:47
  47.2 6.1 %collective-permute-start.10 = (bf16[32,3072]{1,0:T(8,128)(2,1)}, bf16[32,3072]{1,0:T(8,128)(2,1)}, u32[]{:S(2)}, u32[]{:S(2)}) collective-permute-start(bf16[32,3072]{1,0:T(8,128)(2,1)} %get-tuple-element.50), channel_id=1, source_target_pairs={{0,67},{4,71},{8,75},{12,79},{16,83},{20,87},{24,91},{28,95},{32,9... | collective-permute-start | bytes 589832 | tf_op jit(solution)/shard_map/ppermute | solution.py:47
  47.8 66.4 %copy-start.14 = (s32[32]{0:T(128)}, s32[32]{0:T(128)S(1)}, u32[]{:S(2)}) copy-start(s32[32]{0:T(128)S(1)} %stack.140.refs_0_.offs.refs_1_) | copy-start | bytes 388
  47.8 1.6 copy-start.1
  49.4 1.6 copy-start.3
  51.0 4.2 %copy-start.10 = (bf16[32,3072]{1,0:T(8,128)(2,1)S(1)}, bf16[32,3072]{1,0:T(8,128)(2,1)}, u32[]{:S(2)}) copy-start(bf16[32,3072]{1,0:T(8,128)(2,1)} %copy-done.9) | copy-start | bytes 589828
  51.0 12.3 %copy-start.4 = (bf16[1,1,2048,512]{3,2,1,0:T(8,128)(2,1)S(1)}, bf16[1,1,2048,512]{3,2,1,0:T(8,128)(2,1)}, u32[]{:S(2)}) copy-start(bf16[1,1,2048,512]{3,2,1,0:T(8,128)(2,1)} %param.10) | copy-start | bytes 6291460
  51.0 12.3 %copy-start.12 = (bf16[64,3072]{1,0:T(8,128)(2,1)S(1)}, bf16[64,3072]{1,0:T(8,128)(2,1)}, u32[]{:S(2)}) copy-start(bf16[64,3072]{1,0:T(8,128)(2,1)} %copy-done.11) | copy-start | bytes 1179652
  53.0 68.0 %copy-start.6 = (bf16[512,2048]{1,0:T(8,128)(2,1)}, bf16[512,2048]{1,0:T(8,128)(2,1)S(1)}, u32[]{:S(2)}) copy-start(bf16[512,2048]{1,0:T(8,128)(2,1)S(1)} %get-tuple-element.58.refs_12_.refs_6_.refs_7_) | copy-start | bytes 6291460
  53.0 10.3 %copy-start.2 = (bf16[1,1,2048,512]{3,2,1,0:T(8,128)(2,1)S(1)}, bf16[1,1,2048,512]{3,2,1,0:T(8,128)(2,1)}, u32[]{:S(2)}) copy-start(bf16[1,1,2048,512]{3,2,1,0:T(8,128)(2,1)} %param.9) | copy-start | bytes 6291460
  53.0 10.3 %copy-start.8 = (bf16[64,3072]{1,0:T(8,128)(2,1)S(1)}, bf16[64,3072]{1,0:T(8,128)(2,1)}, u32[]{:S(2)}) copy-start(bf16[64,3072]{1,0:T(8,128)(2,1)} %copy-done.7) | copy-start | bytes 1179652
  58.1 16.9 %collective-permute-start.17 = (bf16[128,3072]{1,0:T(8,128)(2,1)S(1)}, bf16[128,3072]{1,0:T(8,128)(2,1)S(1)}, u32[]{:S(2)}, u32[]{:S(2)}) collective-permute-start(bf16[128,3072]{1,0:T(8,128)(2,1)S(1)} %get-tuple-element.60.refs_1_), channel_id=1, source_target_pairs={{0,1},{4,5},{8,9},{12,13},{16,17},{20,21},{24,25},{28,29},{32,33},... | collective-permute-start | bytes 2359304 | tf_op jit(solution)/shard_map/ppermute | solution.py:47
  61.0 14.0 %collective-permute-start.14 = (bf16[128,3072]{1,0:T(8,128)(2,1)S(1)}, bf16[128,3072]{1,0:T(8,128)(2,1)S(1)}, u32[]{:S(2)}, u32[]{:S(2)}) collective-permute-start(bf16[128,3072]{1,0:T(8,128)(2,1)S(1)} %get-tuple-element.54.refs_3_.refs_9_), channel_id=1, source_target_pairs={{0,4},{4,8},{8,12},{12,0},{16,20},{20,24},{24,28},{28,16},{32,36},... | collective-permute-start | bytes 2359304 | tf_op jit(solution)/shard_map/ppermute | solution.py:47
  61.2 27.8 %collective-permute-start.13 = (bf16[128,3072]{1,0:T(8,128)(2,1)S(1)}, bf16[128,3072]{1,0:T(8,128)(2,1)S(1)}, u32[]{:S(2)}, u32[]{:S(2)}) collective-permute-start(bf16[128,3072]{1,0:T(8,128)(2,1)S(1)} %get-tuple-element.53), channel_id=1, source_target_pairs={{0,4},{4,8},{8,12},{12,0},{16,20},{20,24},{24,28},{28,16},{32,36},... | collective-permute-start | bytes 2359304 | tf_op jit(solution)/shard_map/ppermute | solution.py:47
  62.1 26.9 %collective-permute-start.15 = (bf16[128,3072]{1,0:T(8,128)(2,1)S(1)}, bf16[128,3072]{1,0:T(8,128)(2,1)S(1)}, u32[]{:S(2)}, u32[]{:S(2)}) collective-permute-start(bf16[128,3072]{1,0:T(8,128)(2,1)S(1)} %get-tuple-element.54.refs_3_.refs_9_), channel_id=1, source_target_pairs={{0,12},{4,0},{8,4},{12,8},{16,28},{20,16},{24,20},{28,24},{32,44},... | collective-permute-start | bytes 2359304 | tf_op jit(solution)/shard_map/ppermute | solution.py:47
  62.6 14.6 %collective-permute-start.21 = (bf16[64,3072]{1,0:T(8,128)(2,1)S(1)}, bf16[64,3072]{1,0:T(8,128)(2,1)S(1)}, u32[]{:S(2)}, u32[]{:S(2)}) collective-permute-start(bf16[64,3072]{1,0:T(8,128)(2,1)S(1)} %get-tuple-element.67), channel_id=1, source_target_pairs={{1,2},{5,6},{9,10},{13,14},{17,18},{21,22},{25,26},{29,30},{33,34}... | collective-permute-start | bytes 1179656 | tf_op jit(solution)/shard_map/ppermute | solution.py:47
  76.2 15.4 %collective-permute-start.23 = (bf16[64,3072]{1,0:T(8,128)(2,1)S(1)}, bf16[64,3072]{1,0:T(8,128)(2,1)S(1)}, u32[]{:S(2)}, u32[]{:S(2)}) collective-permute-start(bf16[64,3072]{1,0:T(8,128)(2,1)S(1)} %get-tuple-element.68), channel_id=1, source_target_pairs={{1,2},{5,6},{9,10},{13,14},{17,18},{21,22},{25,26},{29,30},{33,34}... | collective-permute-start | bytes 1179656 | tf_op jit(solution)/shard_map/ppermute | solution.py:47
  76.9 30.2 %collective-permute-start.18 = (bf16[128,3072]{1,0:T(8,128)(2,1)S(1)}, bf16[128,3072]{1,0:T(8,128)(2,1)}, u32[]{:S(2)}, u32[]{:S(2)}) collective-permute-start(bf16[128,3072]{1,0:T(8,128)(2,1)S(1)} %get-tuple-element.61.refs_3_), channel_id=1, source_target_pairs={{0,4},{4,8},{8,12},{12,0},{16,20},{20,24},{24,28},{28,16},{32,36},... | collective-permute-start | bytes 2359304 | tf_op jit(solution)/shard_map/ppermute | solution.py:47
  77.2 29.8 %collective-permute-start.22 = (bf16[64,3072]{1,0:T(8,128)(2,1)S(1)}, bf16[64,3072]{1,0:T(8,128)(2,1)S(1)}, u32[]{:S(2)}, u32[]{:S(2)}) collective-permute-start(bf16[64,3072]{1,0:T(8,128)(2,1)S(1)} %collective-permute-done.21.refs_0_), channel_id=1, source_target_pairs={{0,1},{4,5},{8,9},{12,13},{16,17},{20,21},{24,25},{28,29},{32,33},... | collective-permute-start | bytes 1179656 | tf_op jit(solution)/shard_map/ppermute | solution.py:47
  89.0 25.3 %collective-permute-start.19 = (bf16[128,3072]{1,0:T(8,128)(2,1)S(1)}, bf16[128,3072]{1,0:T(8,128)(2,1)S(1)}, u32[]{:S(2)}, u32[]{:S(2)}) collective-permute-start(bf16[128,3072]{1,0:T(8,128)(2,1)S(1)} %get-tuple-element.61.refs_3_), channel_id=1, source_target_pairs={{0,12},{4,0},{8,4},{12,8},{16,28},{20,16},{24,20},{28,24},{32,44},... | collective-permute-start | bytes 2359304 | tf_op jit(solution)/shard_map/ppermute | solution.py:47
  89.0 25.3 %collective-permute-start.16 = (bf16[128,3072]{1,0:T(8,128)(2,1)S(1)}, bf16[128,3072]{1,0:T(8,128)(2,1)S(1)}, u32[]{:S(2)}, u32[]{:S(2)}) collective-permute-start(bf16[128,3072]{1,0:T(8,128)(2,1)S(1)} %collective-permute-done.14.refs_4_.refs_10_.refs_3_), channel_id=1, source_target_pairs={{0,4},{4,8},{8,12},{12,0},{16,20},{20,24},{24,28},{28,16},{32,36},... | collective-permute-start | bytes 2359304 | tf_op jit(solution)/shard_map/ppermute | solution.py:47
  91.7 15.4 %collective-permute-start.24 = (bf16[64,3072]{1,0:T(8,128)(2,1)S(1)}, bf16[64,3072]{1,0:T(8,128)(2,1)S(1)}, u32[]{:S(2)}, u32[]{:S(2)}) collective-permute-start(bf16[64,3072]{1,0:T(8,128)(2,1)S(1)} %collective-permute-done.23.refs_2_), channel_id=1, source_target_pairs={{0,1},{4,5},{8,9},{12,13},{16,17},{20,21},{24,25},{28,29},{32,33},... | collective-permute-start | bytes 1179656 | tf_op jit(solution)/shard_map/ppermute | solution.py:47
  109.1 21.5 %collective-permute-start.25 = (bf16[128,3072]{1,0:T(8,128)(2,1)}, bf16[128,3072]{1,0:T(8,128)(2,1)}, u32[]{:S(2)}, u32[]{:S(2)}) collective-permute-start(bf16[128,3072]{1,0:T(8,128)(2,1)} %pack.5.refs_3_), channel_id=1, source_target_pairs={{0,4},{4,8},{8,12},{12,0},{16,20},{20,24},{24,28},{28,16},{32,36},... | collective-permute-start | bytes 2359304 | tf_op jit(solution)/shard_map/ppermute | solution.py:47
  109.2 23.2 %collective-permute-start.26 = (bf16[128,3072]{1,0:T(8,128)(2,1)}, bf16[128,3072]{1,0:T(8,128)(2,1)}, u32[]{:S(2)}, u32[]{:S(2)}) collective-permute-start(bf16[128,3072]{1,0:T(8,128)(2,1)} %pack.5.refs_3_), channel_id=1, source_target_pairs={{0,12},{4,0},{8,4},{12,8},{16,28},{20,16},{24,20},{28,24},{32,44},... | collective-permute-start | bytes 2359304 | tf_op jit(solution)/shard_map/ppermute | solution.py:47
  110.6 29.0 %collective-permute-start.20 = (bf16[128,3072]{1,0:T(8,128)(2,1)}, bf16[128,3072]{1,0:T(8,128)(2,1)}, u32[]{:S(2)}, u32[]{:S(2)}) collective-permute-start(bf16[128,3072]{1,0:T(8,128)(2,1)} %collective-permute-done.18.refs_4_.refs_5_), channel_id=1, source_target_pairs={{0,4},{4,8},{8,12},{12,0},{16,20},{20,24},{24,28},{28,16},{32,36},... | collective-permute-start | bytes 2359304 | tf_op jit(solution)/shard_map/ppermute | solution.py:47
  127.9 2.7 %copy-start.5 = (f32[512,3072]{1,0:T(8,128)}, f32[512,3072]{1,0:T(8,128)S(1)}, u32[]{:S(2)}) copy-start(f32[512,3072]{1,0:T(8,128)S(1)} %get-tuple-element.72.refs_8_) | copy-start | bytes 18874372
  131.2 16.7 %collective-permute-start.27 = (bf16[128,3072]{1,0:T(8,128)(2,1)}, bf16[128,3072]{1,0:T(8,128)(2,1)S(1)}, u32[]{:S(2)}, u32[]{:S(2)}) collective-permute-start(bf16[128,3072]{1,0:T(8,128)(2,1)} %after.3.refs_4_), channel_id=1, source_target_pairs={{0,4},{4,8},{8,12},{12,0},{16,20},{20,24},{24,28},{28,16},{32,36},... | collective-permute-start | bytes 2359304 | tf_op jit(solution)/shard_map/ppermute | solution.py:47
  148.0 0.9 copy-start.17
  155.2 8.2 %collective-permute-start.28 = (bf16[512,1536]{1,0:T(8,128)(2,1)}, bf16[512,1536]{1,0:T(8,128)(2,1)S(1)}, u32[]{:S(2)}, u32[]{:S(2)}) collective-permute-start(bf16[512,1536]{1,0:T(8,128)(2,1)} %get-tuple-element.79), channel_id=1, source_target_pairs={{0,128},{4,132},{8,136},{12,140},{16,144},{20,148},{24,152},{28,15... | collective-permute-start | bytes 4718600 | tf_op jit(solution)/shard_map/ppermute | solution.py:47
  163.4 1.2 copy-start.18
